TPU v7x, 32 devices: a whole 2x2x4 slice. The times are simulated.
32 devices in a mesh: fsdp: 8 (over y, x, core), rep: 4 (over z).
Axes of the slice: x: 2, y: 2, z: 4, core: 2. Of those that a mesh axis runs over, the one named last changes fastest.
Arguments:
- tokens: bfloat16 [32768, 768], P(('fsdp', 'rep')), may hold values from -6 to 6
- segment_ids: int32 [32768], P(('fsdp', 'rep')), may hold values from 0 to 127, never falling along the last dimension, each value on 1 to 1024 neighbouring positions
- w_in: bfloat16 [768, 3376], P(('fsdp', 'rep')), may hold values from -0.21875 to 0.21875
- w_out: bfloat16 [1536, 768], P(None, ('fsdp', 'rep')), may hold values from -0.15625 to 0.15625
- norm_gain: bfloat16 [768], P(('fsdp', 'rep')), may hold values from 0.25 to 1.75
- conv_w: float32 [4, 1792], replicated, may hold values from -3 to 3
- conv_b: float32 [1792], replicated, may hold values from -1.5 to 1.5
- dt_bias: float32 [48], replicated, may hold values from -7.5 to -2
- a_log: float32 [48], replicated, may hold values from -1.5 to 0
- d_skip: float32 [24], replicated, may hold values from 0.5 to 1.5
- out_gain: float32 [1536], replicated, may hold values from 0.25 to 1.75
- cotangent: bfloat16 [32768, 768], P(('fsdp', 'rep')), may hold values from -6 to 6
Outputs:
- output: bfloat16 [32768, 768], P(('fsdp', 'rep'))
- d_tokens: float32 [32768, 768], P(('fsdp', 'rep'))
- d_w_in: float32 [768, 3376], P(('fsdp', 'rep'))
- d_w_out: float32 [1536, 768], P(None, ('fsdp', 'rep'))
- d_norm_gain: float32 [768], P(('fsdp', 'rep'))
- d_conv_w: float32 [4, 1792], replicated
- d_conv_b: float32 [1792], replicated
- d_dt_bias: float32 [48], replicated
- d_a_log: float32 [48], replicated
- d_d_skip: float32 [24], replicated
- d_out_gain: float32 [1536], replicated
Inputs may be any that keep to these rules, and one draw needn't show every extreme that they name: `segment_ids`: segment ids never fall along the tokens; each segment has 1 to 1024 tokens and one has exactly 1024.
All inputs are finite; a program needn't handle non-finite values.
Results may differ from a plain program's by a relative error of at most 0.0083.
Values may be sent and summed in bfloat16 or wider, within the bound.
A program may use at most 256 MiB of HBM per device.

v0:
```python
import math

import jax
import jax.numpy as jnp
from jax import lax
from jax.sharding import PartitionSpec as P

eps = 1e-05


def conv_silu(conv_in, conv_w, conv_b, segment_ids):
    length = conv_in.shape[0]
    summed = conv_b[None, :] + conv_w[0][None, :] * conv_in
    for offset in range(1, conv_w.shape[0]):
        earlier = jnp.concatenate(
            [jnp.zeros((offset, conv_in.shape[1]), conv_in.dtype), conv_in[: length - offset]],
            axis=0,
        )
        before = jnp.concatenate(
            [jnp.full((offset,), -1, jnp.int32), segment_ids[: length - offset]], axis=0
        )
        same_doc = (before == segment_ids).astype(conv_in.dtype)
        summed = summed + conv_w[offset][None, :] * earlier * same_doc[:, None]
    return jax.nn.silu(summed)


def decays(dt_raw, dt_bias, a_log):
    head_count = dt_bias.shape[0] // 2
    step_sizes = jax.nn.softplus(dt_raw + dt_bias[None, :])
    log_rates = -step_sizes * jnp.exp(a_log)[None, :]
    cum_fwd = jnp.cumsum(log_rates[:, :head_count], axis=0)
    cum_bwd = jnp.cumsum(log_rates[:, head_count:], axis=0) - log_rates[:, head_count:]
    return (step_sizes[:, :head_count], step_sizes[:, head_count:], cum_fwd, cum_bwd)


def group_decays(lower_mask, upper_mask, cum_fwd_g, cum_bwd_g):
    fwd_gap = jnp.where(lower_mask[None], cum_fwd_g[:, :, None] - cum_fwd_g[:, None, :], 0.0)
    bwd_gap = jnp.where(upper_mask[None], cum_bwd_g[:, None, :] - cum_bwd_g[:, :, None], 0.0)
    return (
        jnp.where(lower_mask[None], jnp.exp(fwd_gap), 0.0),
        jnp.where(upper_mask[None], jnp.exp(bwd_gap), 0.0),
    )


def norm_rows(residual, gain_rows):
    inv_rms = lax.rsqrt(jnp.mean(residual * residual, axis=1, keepdims=True) + eps)
    return residual * inv_rms * gain_rows[None, :]


def gate_norm(ssm_out, gate_in, out_gain):
    gated_out = ssm_out * jax.nn.silu(gate_in)
    inv_out = lax.rsqrt(jnp.mean(gated_out * gated_out, axis=1, keepdims=True) + eps)
    return gated_out * inv_out * out_gain[None, :]


def contract(left, right, left_dim, right_dim):
    return lax.dot_general(
        left, right, (((left_dim,), (right_dim,)), ((), ())), preferred_element_type=jnp.float32
    )


def body(
    tokens,
    segment_ids,
    w_in,
    w_out,
    norm_gain,
    conv_w,
    conv_b,
    dt_bias,
    a_log,
    d_skip,
    out_gain,
    cotangent,
):
    length = tokens.shape[0]
    head_count = d_skip.shape[0]
    inner_width = out_gain.shape[0]
    channels = conv_w.shape[1]
    head_dim = inner_width // head_count
    state_dim = (channels - inner_width) // 4
    head_group = math.gcd(head_count, 4)
    group_count = head_count // head_group
    full_in, full_out, full_gain = (
        lax.all_gather(w_in, ("fsdp", "rep"), axis=0, tiled=True),
        lax.all_gather(w_out, ("fsdp", "rep"), axis=1, tiled=True),
        lax.all_gather(norm_gain, ("fsdp", "rep"), axis=0, tiled=True),
    )
    residual = tokens.astype(jnp.float32)
    gain_rows = full_gain.astype(jnp.float32)
    normed_f, norm_pull = jax.vjp(norm_rows, residual, gain_rows)
    normed = normed_f.astype(jnp.bfloat16)
    projected = jnp.dot(normed, full_in, preferred_element_type=jnp.float32)
    gate_in = projected[:, :inner_width]
    conv_in = projected[:, inner_width : inner_width + channels]
    dt_raw = projected[:, inner_width + channels :]

    def conv_local(conv_in_rows, taps, bias_row):
        return conv_silu(conv_in_rows, taps, bias_row, segment_ids)

    act, conv_pull = jax.vjp(conv_local, conv_in, conv_w, conv_b)
    values = act[:, :inner_width]
    b_fwd = act[:, inner_width : inner_width + state_dim].astype(jnp.bfloat16)
    c_fwd = act[:, inner_width + state_dim : inner_width + 2 * state_dim].astype(jnp.bfloat16)
    b_bwd = act[:, inner_width + 2 * state_dim : inner_width + 3 * state_dim].astype(jnp.bfloat16)
    c_bwd = act[:, inner_width + 3 * state_dim :].astype(jnp.bfloat16)
    (dt_fwd, dt_bwd, cum_fwd, cum_bwd), decay_pull = jax.vjp(decays, dt_raw, dt_bias, a_log)
    g_fwd = contract(c_fwd, b_fwd, 1, 1)
    g_bwd = contract(c_bwd, b_bwd, 1, 1)
    positions = jnp.arange(length, dtype=jnp.int32)
    same_seg = segment_ids[:, None] == segment_ids[None, :]
    lower_mask = same_seg & (positions[None, :] < positions[:, None])
    upper_mask = same_seg & (positions[None, :] > positions[:, None])
    per_head = values.astype(jnp.bfloat16).reshape(length, head_count, head_dim).transpose(1, 0, 2)

    def grouped(array):
        return array.reshape((group_count, head_group) + array.shape[1:])

    head_inputs = (
        grouped(dt_fwd.T),
        grouped(dt_bwd.T),
        grouped(cum_fwd.T),
        grouped(cum_bwd.T),
        grouped(per_head),
    )

    def group_mixer(dt_fwd_g, dt_bwd_g, decay_fwd, decay_bwd):
        return (
            g_fwd[None] * decay_fwd * dt_fwd_g[:, None, :]
            + g_bwd[None] * decay_bwd * dt_bwd_g[:, None, :]
        ).astype(jnp.bfloat16)

    def group_forward(pieces):
        dt_fwd_g, dt_bwd_g, cum_fwd_g, cum_bwd_g, group_vals = pieces
        decay_fwd, decay_bwd = group_decays(lower_mask, upper_mask, cum_fwd_g, cum_bwd_g)
        mixer_group = group_mixer(dt_fwd_g, dt_bwd_g, decay_fwd, decay_bwd)
        return jnp.einsum(
            "gts,gsd->gtd", mixer_group, group_vals, preferred_element_type=jnp.float32
        )

    mixed_heads = lax.map(group_forward, head_inputs).reshape(head_count, length, head_dim)
    mixed_out = mixed_heads.transpose(1, 0, 2).reshape(length, inner_width)
    skip_row = jnp.repeat(d_skip, head_dim)
    ssm_out = mixed_out + values * skip_row[None, :]
    normed_out_f, gate_pull = jax.vjp(gate_norm, ssm_out, gate_in, out_gain)
    normed_out = normed_out_f.astype(jnp.bfloat16)
    output = (residual + jnp.dot(normed_out, full_out, preferred_element_type=jnp.float32)).astype(
        jnp.bfloat16
    )
    back_in, back_out = (
        lax.all_gather(w_in, ("fsdp", "rep"), axis=0, tiled=True),
        lax.all_gather(w_out, ("fsdp", "rep"), axis=1, tiled=True),
    )
    grad_out_w = contract(normed_out, cotangent, 0, 0)
    d_normed_out = contract(cotangent, back_out, 1, 1)
    d_ssm, d_gate_in, d_out_gain = gate_pull(d_normed_out)
    d_mixed = d_ssm.astype(jnp.bfloat16)
    d_skip_grad = jnp.sum((d_ssm * values).reshape(length, head_count, head_dim), axis=(0, 2))
    d_heads = grouped(d_mixed.reshape(length, head_count, head_dim).transpose(1, 0, 2))

    def group_backward(carry, pieces):
        grad_fwd, grad_bwd = carry
        dt_fwd_g, dt_bwd_g, cum_fwd_g, cum_bwd_g, group_vals, group_grads = pieces
        decay_fwd, decay_bwd = group_decays(lower_mask, upper_mask, cum_fwd_g, cum_bwd_g)
        mixer_group = group_mixer(dt_fwd_g, dt_bwd_g, decay_fwd, decay_bwd)
        d_group_vals = jnp.einsum(
            "gts,gtd->gsd", mixer_group, group_grads, preferred_element_type=jnp.float32
        )
        d_mixer = jnp.einsum(
            "gtd,gsd->gts", group_grads, group_vals, preferred_element_type=jnp.float32
        )
        fwd_prod = d_mixer * g_fwd[None] * decay_fwd
        bwd_prod = d_mixer * g_bwd[None] * decay_bwd
        d_dt_fwd_g = jnp.sum(fwd_prod, axis=1)
        d_dt_bwd_g = jnp.sum(bwd_prod, axis=1)
        fwd_term = fwd_prod * dt_fwd_g[:, None, :]
        bwd_term = bwd_prod * dt_bwd_g[:, None, :]
        d_cum_fwd_g = jnp.sum(fwd_term, axis=2) - jnp.sum(fwd_term, axis=1)
        d_cum_bwd_g = jnp.sum(bwd_term, axis=1) - jnp.sum(bwd_term, axis=2)
        grad_fwd = grad_fwd + jnp.sum(d_mixer * decay_fwd * dt_fwd_g[:, None, :], axis=0)
        grad_bwd = grad_bwd + jnp.sum(d_mixer * decay_bwd * dt_bwd_g[:, None, :], axis=0)
        return (
            (grad_fwd, grad_bwd),
            (d_group_vals, d_dt_fwd_g, d_dt_bwd_g, d_cum_fwd_g, d_cum_bwd_g),
        )

    zero_square = jnp.zeros((length, length), jnp.float32)
    (grad_fwd, grad_bwd), (d_head_vals, d_dt_fwd, d_dt_bwd, d_cum_fwd, d_cum_bwd) = lax.scan(
        group_backward, (zero_square, zero_square), head_inputs + (d_heads,)
    )
    d_head_vals = d_head_vals.reshape(head_count, length, head_dim)
    d_dt_fwd = d_dt_fwd.reshape(head_count, length)
    d_dt_bwd = d_dt_bwd.reshape(head_count, length)
    d_cum_fwd = d_cum_fwd.reshape(head_count, length)
    d_cum_bwd = d_cum_bwd.reshape(head_count, length)
    d_values = d_ssm * skip_row[None, :] + d_head_vals.transpose(1, 0, 2).reshape(
        length, inner_width
    )
    grad_fwd_low = grad_fwd.astype(jnp.bfloat16)
    grad_bwd_low = grad_bwd.astype(jnp.bfloat16)
    d_c_fwd = jnp.dot(grad_fwd_low, b_fwd, preferred_element_type=jnp.float32)
    d_b_fwd = contract(grad_fwd_low, c_fwd, 0, 0)
    d_c_bwd = jnp.dot(grad_bwd_low, b_bwd, preferred_element_type=jnp.float32)
    d_b_bwd = contract(grad_bwd_low, c_bwd, 0, 0)
    d_act = jnp.concatenate([d_values, d_b_fwd, d_c_fwd, d_b_bwd, d_c_bwd], axis=1)
    d_conv_in, d_conv_w, d_conv_b = conv_pull(d_act)
    d_dt_raw, d_dt_bias, d_a_log = decay_pull((d_dt_fwd.T, d_dt_bwd.T, d_cum_fwd.T, d_cum_bwd.T))
    d_projected = jnp.concatenate([d_gate_in, d_conv_in, d_dt_raw], axis=1).astype(jnp.bfloat16)
    grad_in_w = contract(normed, d_projected, 0, 0)
    d_normed = contract(d_projected, back_in, 1, 1)
    d_residual, d_gain_rows = norm_pull(d_normed)
    d_tokens = cotangent.astype(jnp.float32) + d_residual
    d_w_in, d_w_out, d_norm_gain = (
        lax.psum_scatter(grad_in_w, ("fsdp", "rep"), scatter_dimension=0, tiled=True),
        lax.psum_scatter(grad_out_w, ("fsdp", "rep"), scatter_dimension=1, tiled=True),
        lax.psum_scatter(d_gain_rows, ("fsdp", "rep"), scatter_dimension=0, tiled=True),
    )
    summed_small = lax.psum(
        (d_conv_w, d_conv_b, d_dt_bias, d_a_log, d_skip_grad, d_out_gain), ("fsdp", "rep")
    )
    return (
        output,
        d_tokens,
        d_w_in,
        d_w_out,
        d_norm_gain,
        summed_small[0],
        summed_small[1],
        summed_small[2],
        summed_small[3],
        summed_small[4],
        summed_small[5],
    )


def solution(mesh):
    in_specs = (
        P(("fsdp", "rep"), None),
        P(("fsdp", "rep")),
        P(("fsdp", "rep"), None),
        P(None, ("fsdp", "rep")),
        P(("fsdp", "rep")),
        P(),
        P(),
        P(),
        P(),
        P(),
        P(),
        P(("fsdp", "rep"), None),
    )
    out_specs = (
        P(("fsdp", "rep"), None),
        P(("fsdp", "rep"), None),
        P(("fsdp", "rep"), None),
        P(None, ("fsdp", "rep")),
        P(("fsdp", "rep")),
        P(),
        P(),
        P(),
        P(),
        P(),
        P(),
    )
    return jax.shard_map(body, mesh=mesh, in_specs=in_specs, out_specs=out_specs, check_vma=False)
```

profile of v0, /device:TPU:0, one launch (start us, length us, event | category | flops | bytes accessed | tf_op | source)
XLA Modules:
  0.0 933.7 jit_solution(13090845764896243973)
XLA Ops:
  10.3 43.0 %all-reduce.17 = bf16[768]{0:T(1024)(128)(2,1)S(1)} all-reduce(bf16[768]{0:T(1024)(128)(2,1)S(1)} %dynamic-update-slice), channel_id=1, replica_groups=mesh['fsdp'=8,'rep'=4] {'fsdp','rep'}, use_global_device_ids=true, to_apply=%add.17 | all-reduce | flops 768 | bytes 3072
  59.1 20.3 %all-gather.3.cloned.1.call-done = bf16[768,3376]{1,0:T(8,128)(2,1)} async-done(((bf16[24,3376]{1,0:T(8,128)(2,1)}), bf16[768,3376]{1,0:T(8,128)(2,1)}) %all-gather.3.cloned.1.call-update) | async-done | bytes 5185552 | tf_op jit(solution)/shard_map/all_gather | solution.py:85
  100.8 17.5 %fusion.89 = (bf16[1024,1792]{0,1:T(8,128)(2,1)S(1)}, f32[1024,1792]{0,1:T(8,128)}, f32[1024,1792]{0,1:T(8,128)}) fusion(f32[1024]{0:T(1024)S(1)} %get-tuple-element.493, f32[1021,1792]{0,1:T(8,128)} %slice.131, f32[1792]{0:T(1024)S(1)} %get-tuple-element.388, f32[1024]{0:T(1024)S(1)} %get-tuple-element.494, f32[1022,1792]{0,1:T(8,128)} %slice.130, ...), kind=kLoop, calls=%fused_computation.181 | loop fusion | flops 29360128 | bytes 47715328 | tf_op jit(solution)/shard_map/convert.6
  147.4 104.4 %while.37 = (s32[]{:T(128)}, f32[6,4,1024,64]{2,3,1,0:T(8,128)}, f32[1024,1024]{1,0:T(8,128)}, f32[6,4,1024]{2,1,0:T(4,128)S(1)}, f32[6,4,1024]{2,1,0:T(4,128)S(...) while((s32[]{:T(128)}, f32[6,4,1024,64]{2,3,1,0:T(8,128)}, ...), condition=%wide.region_6.7_spmd.clone.clone, body=%wide.region_5.6_spmd.clone.clone.sunk | while | flops 592445440 | bytes 14390397 | solution.py:141
  150.0 14.8 %fusion.102 = f32[6,4,1024,64]{2,3,1,0:T(8,128)} fusion(f32[6,4,1024,64]{2,3,1,0:T(8,128)} %get-tuple-element.722, s32[]{:T(128)S(6)} %copy.75, f32[4,1024]{1,0:T(4,128)S(1)} %get-tuple-element.671, f32[4,1024]{1,0:T(4,128)S(1)} %get-tuple-element.672, f32[1024,1024]{1,0:T(8,128)} %get-tuple-element.737, f32[4,1024]{1,0:T(4,128)S(1)} %get-tuple-element.673, ...), kind=kOutput, calls=%fused_computation.13.clone.1 | convolution fusion | flops 587202560 | bytes 12157952 | tf_op jit(solution)/shard_map/while/body/eval_jaxpr/gts,gsd->gtd/dot_general | solution.py:137
  184.8 14.8 %fusion.102 = f32[6,4,1024,64]{2,3,1,0:T(8,128)} fusion(f32[6,4,1024,64]{2,3,1,0:T(8,128)} %get-tuple-element.722, s32[]{:T(128)S(6)} %copy.75, f32[4,1024]{1,0:T(4,128)S(1)} %get-tuple-element.671, f32[4,1024]{1,0:T(4,128)S(1)} %get-tuple-element.672, f32[1024,1024]{1,0:T(8,128)} %get-tuple-element.737, f32[4,1024]{1,0:T(4,128)S(1)} %get-tuple-element.673, ...), kind=kOutput, calls=%fused_computation.13.clone.1 | convolution fusion | flops 587202560 | bytes 12157952 | tf_op jit(solution)/shard_map/while/body/eval_jaxpr/gts,gsd->gtd/dot_general | solution.py:137
  202.2 14.8 %fusion.102 = f32[6,4,1024,64]{2,3,1,0:T(8,128)} fusion(f32[6,4,1024,64]{2,3,1,0:T(8,128)} %get-tuple-element.722, s32[]{:T(128)S(6)} %copy.75, f32[4,1024]{1,0:T(4,128)S(1)} %get-tuple-element.671, f32[4,1024]{1,0:T(4,128)S(1)} %get-tuple-element.672, f32[1024,1024]{1,0:T(8,128)} %get-tuple-element.737, f32[4,1024]{1,0:T(4,128)S(1)} %get-tuple-element.673, ...), kind=kOutput, calls=%fused_computation.13.clone.1 | convolution fusion | flops 587202560 | bytes 12157952 | tf_op jit(solution)/shard_map/while/body/eval_jaxpr/gts,gsd->gtd/dot_general | solution.py:137
  297.2 341.4 %while.38 = (s32[]{:T(128)}, f32[1024,1024]{1,0:T(8,128)}, f32[1024,1024]{1,0:T(8,128)}, f32[6,4,1024,64]{2,3,1,0:T(8,128)}, f32[6,4,1024]{2,1,0:T(4,128)S(1)}, ...) while((s32[]{:T(128)}, f32[1024,1024]{1,0:T(8,128)}, ...), condition=%wide.region_18.19_spmd.clone.clone.clone, body=%wide.region_9.18_spmd.clone.clone.clone.sunk | while | flops 1232060416 | bytes 110172448 | solution.py:188
  300.1 16.3 %fusion.104 = f32[6,4,1024,64]{2,3,1,0:T(8,128)} fusion(f32[6,4,1024,64]{2,3,1,0:T(8,128)} %get-tuple-element.765, s32[]{:T(128)S(6)} %copy.87, f32[1024,1024]{1,0:T(8,128)} %get-tuple-element.796, f32[1024,1024]{1,0:T(8,128)} %get-tuple-element.795, f32[4,1024]{1,0:T(4,128)S(1)} %dynamic-slice_bitcast_fusion.16, ...), kind=kOutput, calls=%fused_computation.43.clone.1 | convolution fusion | flops 587202560 | bytes 12157952 | tf_op jit(solution)/shard_map/while/body/eval_jaxpr/gts,gtd->gsd/dot_general | solution.py:166
  316.3 26.9 %multiply_reduce_fusion.16 = (f32[4,1024]{1,0:T(4,128)S(1)}, f32[4,1024]{1,0:T(4,128)S(1)}, f32[4,1024]{1,0:T(4,128)S(1)}, f32[1024,1024]{1,0:T(8,128)}, f32[102...) fusion(f32[4,1024]{1,0:T(4,128)S(1)} %dynamic-slice_bitcast_fusion.16, ...), kind=kOutput, calls=%fused_computation.29.clone.1 | convolution fusion | flops 635412480 | bytes 20120576 | tf_op jit(solution)/shard_map/while/body/eval_jaxpr/gtd,gsd->gts/dot_general | solution.py:169
  356.1 16.1 %fusion.104 = f32[6,4,1024,64]{2,3,1,0:T(8,128)} fusion(f32[6,4,1024,64]{2,3,1,0:T(8,128)} %get-tuple-element.765, s32[]{:T(128)S(6)} %copy.87, f32[1024,1024]{1,0:T(8,128)} %get-tuple-element.796, f32[1024,1024]{1,0:T(8,128)} %get-tuple-element.795, f32[4,1024]{1,0:T(4,128)S(1)} %dynamic-slice_bitcast_fusion.16, ...), kind=kOutput, calls=%fused_computation.43.clone.1 | convolution fusion | flops 587202560 | bytes 12157952 | tf_op jit(solution)/shard_map/while/body/eval_jaxpr/gts,gtd->gsd/dot_general | solution.py:166
  372.3 26.8 %multiply_reduce_fusion.16 = (f32[4,1024]{1,0:T(4,128)S(1)}, f32[4,1024]{1,0:T(4,128)S(1)}, f32[4,1024]{1,0:T(4,128)S(1)}, f32[1024,1024]{1,0:T(8,128)}, f32[102...) fusion(f32[4,1024]{1,0:T(4,128)S(1)} %dynamic-slice_bitcast_fusion.16, ...), kind=kOutput, calls=%fused_computation.29.clone.1 | convolution fusion | flops 635412480 | bytes 20120576 | tf_op jit(solution)/shard_map/while/body/eval_jaxpr/gtd,gsd->gts/dot_general | solution.py:169
  413.1 16.1 %fusion.104 = f32[6,4,1024,64]{2,3,1,0:T(8,128)} fusion(f32[6,4,1024,64]{2,3,1,0:T(8,128)} %get-tuple-element.765, s32[]{:T(128)S(6)} %copy.87, f32[1024,1024]{1,0:T(8,128)} %get-tuple-element.796, f32[1024,1024]{1,0:T(8,128)} %get-tuple-element.795, f32[4,1024]{1,0:T(4,128)S(1)} %dynamic-slice_bitcast_fusion.16, ...), kind=kOutput, calls=%fused_computation.43.clone.1 | convolution fusion | flops 587202560 | bytes 12157952 | tf_op jit(solution)/shard_map/while/body/eval_jaxpr/gts,gtd->gsd/dot_general | solution.py:166
  429.2 26.8 %multiply_reduce_fusion.16 = (f32[4,1024]{1,0:T(4,128)S(1)}, f32[4,1024]{1,0:T(4,128)S(1)}, f32[4,1024]{1,0:T(4,128)S(1)}, f32[1024,1024]{1,0:T(8,128)}, f32[102...) fusion(f32[4,1024]{1,0:T(4,128)S(1)} %dynamic-slice_bitcast_fusion.16, ...), kind=kOutput, calls=%fused_computation.29.clone.1 | convolution fusion | flops 635412480 | bytes 20120576 | tf_op jit(solution)/shard_map/while/body/eval_jaxpr/gtd,gsd->gts/dot_general | solution.py:169
  470.1 16.0 %fusion.104 = f32[6,4,1024,64]{2,3,1,0:T(8,128)} fusion(f32[6,4,1024,64]{2,3,1,0:T(8,128)} %get-tuple-element.765, s32[]{:T(128)S(6)} %copy.87, f32[1024,1024]{1,0:T(8,128)} %get-tuple-element.796, f32[1024,1024]{1,0:T(8,128)} %get-tuple-element.795, f32[4,1024]{1,0:T(4,128)S(1)} %dynamic-slice_bitcast_fusion.16, ...), kind=kOutput, calls=%fused_computation.43.clone.1 | convolution fusion | flops 587202560 | bytes 12157952 | tf_op jit(solution)/shard_map/while/body/eval_jaxpr/gts,gtd->gsd/dot_general | solution.py:166
  486.1 26.8 %multiply_reduce_fusion.16 = (f32[4,1024]{1,0:T(4,128)S(1)}, f32[4,1024]{1,0:T(4,128)S(1)}, f32[4,1024]{1,0:T(4,128)S(1)}, f32[1024,1024]{1,0:T(8,128)}, f32[102...) fusion(f32[4,1024]{1,0:T(4,128)S(1)} %dynamic-slice_bitcast_fusion.16, ...), kind=kOutput, calls=%fused_computation.29.clone.1 | convolution fusion | flops 635412480 | bytes 20120576 | tf_op jit(solution)/shard_map/while/body/eval_jaxpr/gtd,gsd->gts/dot_general | solution.py:169
  527.0 16.0 %fusion.104 = f32[6,4,1024,64]{2,3,1,0:T(8,128)} fusion(f32[6,4,1024,64]{2,3,1,0:T(8,128)} %get-tuple-element.765, s32[]{:T(128)S(6)} %copy.87, f32[1024,1024]{1,0:T(8,128)} %get-tuple-element.796, f32[1024,1024]{1,0:T(8,128)} %get-tuple-element.795, f32[4,1024]{1,0:T(4,128)S(1)} %dynamic-slice_bitcast_fusion.16, ...), kind=kOutput, calls=%fused_computation.43.clone.1 | convolution fusion | flops 587202560 | bytes 12157952 | tf_op jit(solution)/shard_map/while/body/eval_jaxpr/gts,gtd->gsd/dot_general | solution.py:166
  543.1 26.8 %multiply_reduce_fusion.16 = (f32[4,1024]{1,0:T(4,128)S(1)}, f32[4,1024]{1,0:T(4,128)S(1)}, f32[4,1024]{1,0:T(4,128)S(1)}, f32[1024,1024]{1,0:T(8,128)}, f32[102...) fusion(f32[4,1024]{1,0:T(4,128)S(1)} %dynamic-slice_bitcast_fusion.16, ...), kind=kOutput, calls=%fused_computation.29.clone.1 | convolution fusion | flops 635412480 | bytes 20120576 | tf_op jit(solution)/shard_map/while/body/eval_jaxpr/gtd,gsd->gts/dot_general | solution.py:169
  583.9 16.1 %fusion.104 = f32[6,4,1024,64]{2,3,1,0:T(8,128)} fusion(f32[6,4,1024,64]{2,3,1,0:T(8,128)} %get-tuple-element.765, s32[]{:T(128)S(6)} %copy.87, f32[1024,1024]{1,0:T(8,128)} %get-tuple-element.796, f32[1024,1024]{1,0:T(8,128)} %get-tuple-element.795, f32[4,1024]{1,0:T(4,128)S(1)} %dynamic-slice_bitcast_fusion.16, ...), kind=kOutput, calls=%fused_computation.43.clone.1 | convolution fusion | flops 587202560 | bytes 12157952 | tf_op jit(solution)/shard_map/while/body/eval_jaxpr/gts,gtd->gsd/dot_general | solution.py:166
  600.0 26.8 %multiply_reduce_fusion.16 = (f32[4,1024]{1,0:T(4,128)S(1)}, f32[4,1024]{1,0:T(4,128)S(1)}, f32[4,1024]{1,0:T(4,128)S(1)}, f32[1024,1024]{1,0:T(8,128)}, f32[102...) fusion(f32[4,1024]{1,0:T(4,128)S(1)} %dynamic-slice_bitcast_fusion.16, ...), kind=kOutput, calls=%fused_computation.29.clone.1 | convolution fusion | flops 635412480 | bytes 20120576 | tf_op jit(solution)/shard_map/while/body/eval_jaxpr/gtd,gsd->gts/dot_general | solution.py:169
  667.1 29.7 %reduce-window.36 = f32[24,8,128]{2,1,0:T(8,128)S(1)} reduce-window(f32[24,8,128]{2,1,0:T(8,128)S(1)} %reshape.264, f32[]{:T(128)} %constant.71.clone.1), window={size=1x1x128 pad=0_0x0_0x0_127}, to_apply=%region_21.22 | reduce-window | flops 3121152 | bytes 196612 | tf_op jit(solution)/shard_map/reduce-window.6
  697.2 29.7 %reduce-window.34 = f32[24,8,128]{2,1,0:T(8,128)S(1)} reduce-window(f32[24,8,128]{2,1,0:T(8,128)S(1)} %reshape.262, f32[]{:T(128)} %constant.71.clone.1), window={size=1x1x128 pad=0_0x0_0x0_127}, to_apply=%region_19.20 | reduce-window | flops 3121152 | bytes 196612 | tf_op jit(solution)/shard_map/reduce-window.4
  798.7 41.4 %all-reduce.20 = (f32[768]{0:T(1024)S(1)}, f32[4,1792]{1,0:T(4,128)}, f32[1792]{0:T(1024)}, f32[48]{0:T(128)}, f32[48]{0:T(128)}, /*index=5*/f32[24]{0:T(128)}, f32[1536]{0:T(1024)}) all-reduce(f32[768]{0:T(1024)S(1)} %get-tuple-element.384, ...), channel_id=4, replica_groups=mesh['fsdp'=8,'rep'=4] {'fsdp','rep'}, use_global_device_ids=true, to_apply=%region_27.28.clone | all-reduce | flops 11384 | bytes 91072
  852.1 74.7 %reduce-scatter.7.cloned.1.call-done = f32[24,3376]{1,0:T(8,128)} async-done(((f32[768,3376]{1,0:T(8,128)}), f32[24,3376]{1,0:T(8,128)}) %reduce-scatter.7.cloned.1.call-update) | async-done | bytes 324112
  (330 shorter events, 359.4 us)
Async XLA Ops:
  7.2 72.2 %all-gather.3.cloned.1.call-start = ((), (), s32[]{:S(2)}) async-start(), calls=%async_computation.2 | async-start | bytes 5474304 | tf_op jit(solution)/shard_map/all_gather | solution.py:85
  7.9 259.8 %all-gather.5.cloned.1.call-start = ((), (), s32[]{:S(2)}) async-start(), calls=%async_computation.3 | async-start | bytes 2433024 | tf_op jit(solution)/shard_map/all_gather | solution.py:86
  8.7 843.5 %reduce-scatter.5.cloned.1.call-start = ((), (), s32[]{:S(2)}) async-start(), calls=%async_computation.4 | async-start | bytes 4866048 | tf_op jit(solution)/shard_map/reduce_scatter | solution.py:215
  9.4 114.7 %copy-start.52 = (f32[48]{0:T(128)}, f32[48]{0:T(128)S(1)}, u32[]{:S(2)}) copy-start(f32[48]{0:T(128)S(1)} %exp.33) | copy-start | bytes 580
  58.1 42.6 %copy-start.23 = (f32[1792]{0:T(1024)}, f32[1792]{0:T(1024)S(1)}, u32[]{:S(2)}) copy-start(f32[1792]{0:T(1024)S(1)} %get-tuple-element.386) | copy-start | bytes 21508
  58.1 42.6 %copy-start.25 = (f32[1792]{0:T(1024)}, f32[1792]{0:T(1024)S(1)}, u32[]{:S(2)}) copy-start(f32[1792]{0:T(1024)S(1)} %get-tuple-element.388) | copy-start | bytes 21508
  58.1 42.6 %copy-start.27 = (f32[1792]{0:T(1024)}, f32[1792]{0:T(1024)S(1)}, u32[]{:S(2)}) copy-start(f32[1792]{0:T(1024)S(1)} %get-tuple-element.387) | copy-start | bytes 21508
  58.1 42.6 %copy-start.29 = (f32[1792]{0:T(1024)}, f32[1792]{0:T(1024)S(1)}, u32[]{:S(2)}) copy-start(f32[1792]{0:T(1024)S(1)} %get-tuple-element.389) | copy-start | bytes 21508
  59.0 41.7 %copy-start.31 = (f32[1024]{0:T(1024)}, f32[1024]{0:T(1024)S(1)}, u32[]{:S(2)}) copy-start(f32[1024]{0:T(1024)S(1)} %get-tuple-element.492) | copy-start | bytes 12292
  59.1 41.7 %copy-start.33 = (f32[1024]{0:T(1024)}, f32[1024]{0:T(1024)S(1)}, u32[]{:S(2)}) copy-start(f32[1024]{0:T(1024)S(1)} %get-tuple-element.494) | copy-start | bytes 12292
  59.1 41.7 %copy-start.37 = (f32[1024]{0:T(1024)}, f32[1024]{0:T(1024)S(1)}, u32[]{:S(2)}) copy-start(f32[1024]{0:T(1024)S(1)} %get-tuple-element.493) | copy-start | bytes 12292
  88.3 35.8 %copy-start.4 = (f32[1024,3376]{0,1:T(8,128)}, f32[1024,3376]{0,1:T(8,128)S(1)}, u32[]{:S(2)}) copy-start(f32[1024,3376]{0,1:T(8,128)S(1)} %fusion.58) | copy-start | bytes 41484292
  147.4 104.4 %copy-start.18 = (f32[1536]{0:T(1024)S(1)}, f32[1536]{0:T(1024)}, u32[]{:S(2)}) copy-start(f32[1536]{0:T(1024)} %mul.462) | copy-start | bytes 18436
  276.7 650.2 %reduce-scatter.7.cloned.1.call-start = ((), (), s32[]{:S(2)}) async-start(), calls=%async_computation.5 | async-start | bytes 10948608
  297.2 341.4 %copy-start.19 = (f32[1536]{0:T(1024)S(1)}, f32[1536]{0:T(1024)}, u32[]{:S(2)}) copy-start(f32[1536]{0:T(1024)} %mul.462) | copy-start | bytes 18436
  657.2 70.2 %copy-start.14 = (f32[1024,48]{0,1:T(8,128)S(1)}, f32[1024,48]{0,1:T(8,128)}, u32[]{:S(2)}) copy-start(f32[1024,48]{0,1:T(8,128)} %copy-done.13) | copy-start | bytes 589828
  657.2 70.2 %copy-start.51 = (f32[48]{0:T(128)S(1)}, f32[48]{0:T(128)}, u32[]{:S(2)}) copy-start(f32[48]{0:T(128)} %param.23) | copy-start | bytes 580
  657.2 70.2 %copy-start.53 = (f32[48]{0:T(128)S(1)}, f32[48]{0:T(128)}, u32[]{:S(2)}) copy-start(f32[48]{0:T(128)} %copy-done.52) | copy-start | bytes 580
  657.2 71.4 %copy-start.32 = (f32[1024]{0:T(1024)S(1)}, f32[1024]{0:T(1024)}, u32[]{:S(2)}) copy-start(f32[1024]{0:T(1024)} %copy-done.31) | copy-start | bytes 12292
  657.2 71.4 %copy-start.34 = (f32[1024]{0:T(1024)S(1)}, f32[1024]{0:T(1024)}, u32[]{:S(2)}) copy-start(f32[1024]{0:T(1024)} %copy-done.33) | copy-start | bytes 12292
  787.2 53.5 %copy-start.36 = (f32[1024]{0:T(1024)S(1)}, f32[1024]{0:T(1024)}, u32[]{:S(2)}) copy-start(f32[1024]{0:T(1024)} %copy-done.35) | copy-start | bytes 12292
  787.2 53.5 %copy-start.16 = (bf16[1024,768]{1,0:T(8,128)(2,1)S(1)}, bf16[1024,768]{1,0:T(8,128)(2,1)}, u32[]{:S(2)}) copy-start(bf16[1024,768]{1,0:T(8,128)(2,1)} %param.27) | copy-start | bytes 4718596
  798.7 46.5 %copy-start.45 = (f32[1024]{0:T(1024)S(1)}, f32[1024]{0:T(1024)}, u32[]{:S(2)}) copy-start(f32[1024]{0:T(1024)} %copy-done.44) | copy-start | bytes 12292
  798.7 46.5 %copy-start.48 = (f32[1536]{0:T(1024)S(1)}, f32[1536]{0:T(1024)}, u32[]{:S(2)}) copy-start(f32[1536]{0:T(1024)} %param.26) | copy-start | bytes 18436
  (55 other events, 621.6 us)
Sparse Core Ops, SparseCore 0:
  10.9 68.4 all-gather.2
  82.2 56.2 all-gather.4
  276.8 105.8 reduce-scatter.4
  786.3 140.5 reduce-scatter.6
where the time goes:
time: 943 us; the launch traced here: 934 us
  matrix products  417 us (44%)
  other arithmetic  274 us (29%)
  waiting for transfers between devices  96.5 us (10%)
  blocking collectives  84.4 us (9%)
  local copies, waits for them, and re-layouts  46 us (5%)
  between operations  14.9 us (2%)
    dot_general x6, matrix products, group_backward(): jnp.einsum('gtd,gsd->gts', group_grads, group_vals, preferred_element_typ...  161 us
    dot_general x6, matrix products, group_backward(): jnp.einsum('gts,gtd->gsd', mixer_group, group_grads, preferred_element_ty...  96.6 us
    another operation x17, other arithmetic  91 us
    dot_general x6, matrix products, group_forward(): jnp.einsum('gts,gsd->gtd', mixer_group, group_vals, preferred_element_typ...  88.8 us
    unnamed x2, blocking collectives  84.4 us
    unnamed x5, waiting for transfers between devices  76.1 us
    add x6, other arithmetic, group_backward(): grad_bwd + jnp.sum(d_mixer * decay_bwd * dt_bwd_g[:, None, :], axis=0)  55.8 us
    dot_general x8, matrix products, contract(): lax.dot_general(left, right, (((left_dim,), (right_dim,)), ((), ())), pre...  50 us
  transfers between devices with their start and end apart: 4, of which 2 were waited for; matrix products, arithmetic and copies ran while one was open for 76% of the time, Pallas kernels for 0%

commit v1 on v0

v1 whole, which is shorter than its diff:
```python
import functools

import jax
import jax.numpy as jnp
import numpy as np
from jax import lax
from jax.experimental import pallas as pl
from jax.experimental.pallas import tpu as pltpu
from jax.sharding import PartitionSpec as P

eps = 1e-05
Q = 128
HALO = 16
f32 = jnp.float32
bf16 = jnp.bfloat16
AXES = ("fsdp", "rep")


def nn(a, b):
    return lax.dot_general(a, b, (((1,), (0,)), ((), ())), preferred_element_type=f32)


def nt(a, b):
    return lax.dot_general(a, b, (((1,), (1,)), ((), ())), preferred_element_type=f32)


def tn(a, b):
    return lax.dot_general(a, b, (((0,), (0,)), ((), ())), preferred_element_type=f32)


def split2(x):
    hi = x.astype(bf16)
    lo = (x - hi.astype(f32)).astype(bf16)
    return jnp.concatenate([hi, lo], axis=1)


def split_rows(x):
    hi = x.astype(bf16)
    return jnp.concatenate([hi, (x - hi.astype(f32)).astype(bf16)], axis=0)


def nn_exact(ones_mask, x):
    hi = x.astype(bf16)
    r = x - hi.astype(f32)
    mid = r.astype(bf16)
    lo = (r - mid.astype(f32)).astype(bf16)
    return nn(ones_mask, hi) + (nn(ones_mask, mid) + nn(ones_mask, lo))


def iotas(shape):
    return (
        lax.broadcasted_iota(jnp.int32, shape, 0),
        lax.broadcasted_iota(jnp.int32, shape, 1),
    )


def front_kernel(
    sizes,
    tok_ref, halo_ref, gain_ref, w_ref, cw_ref, cb_ref, dtb_ref, rate_ref, aux_ref, x2_ref,
    normed_ref, gate_ref, conv_ref, act_ref, low_ref, dsil_ref, dt_ref, cum_ref, dtraw_ref, sb_ref,
    ext_ref, state_ref,
):
    inner, channels, heads, state = sizes
    step = pl.program_id(0)

    @pl.when(step == 0)
    def _():
        state_ref[...] = jnp.zeros_like(state_ref)

    gain = gain_ref[...]

    def norm(x):
        x = x.astype(f32)
        inv = lax.rsqrt(jnp.mean(x * x, axis=1, keepdims=True) + eps)
        return (x * inv * gain).astype(bf16)

    normed = norm(tok_ref[...])
    normed_ref[...] = normed
    both = jnp.concatenate([norm(halo_ref[...]), normed], axis=0)
    gate_ref[...] = nn(normed, w_ref[:, :inner])
    dt_raw = nn(normed, w_ref[:, inner + channels :])
    dtraw_ref[...] = dt_raw
    aux = aux_ref[...]
    m1, m2, m3 = aux[:, 0:1], aux[:, 1:2], aux[:, 2:3]
    block = 256
    for at in range(0, channels, block):
        sl = slice(at, at + block)
        ext_ref[:, sl] = nn(both, w_ref[:, inner + at : inner + at + block])
        x0 = ext_ref[HALO : HALO + Q, sl]
        conv_ref[:, sl] = x0
        pre = cb_ref[:, sl] + cw_ref[0:1, sl] * x0
        pre += cw_ref[1:2, sl] * (ext_ref[HALO - 1 : HALO - 1 + Q, sl] * m1)
        pre += cw_ref[2:3, sl] * (ext_ref[HALO - 2 : HALO - 2 + Q, sl] * m2)
        pre += cw_ref[3:4, sl] * (ext_ref[HALO - 3 : HALO - 3 + Q, sl] * m3)
        sig = 1.0 / (1.0 + jnp.exp(-pre))
        act = pre * sig
        act_ref[:, sl] = act
        low_ref[:, sl] = act.astype(bf16)
        dsil_ref[:, sl] = sig * (1.0 + pre * (1.0 - sig))
    v = dt_raw + dtb_ref[...]
    dt = jnp.maximum(v, 0.0) + jnp.log1p(jnp.exp(-jnp.abs(v)))
    dt_ref[...] = dt
    rate = -dt * rate_ref[...]
    row, col = iotas((Q, Q))
    cum = nn_exact((col <= row).astype(bf16), rate)
    cum_ref[...] = cum
    sb_ref[0] = state_ref[...].astype(bf16)
    weight = dt[:, heads:] * jnp.exp(cum[:, heads:] - rate[:, heads:]) * aux[:, 5:6]
    whole = jnp.exp(cum[Q - 1 :, heads:]) * aux[0:1, 7:8]
    scales = split2(jnp.concatenate([weight, jnp.broadcast_to(whole, (8, heads))], axis=0))
    b_bwd = low_ref[:, inner + 2 * state : inner + 3 * state]
    for at in range(0, inner, block):
        sl = slice(at, at + block)
        wide = nn(scales, x2_ref[:, sl])
        vs = (low_ref[:, sl].astype(f32) * wide[:Q]).astype(bf16)
        state_ref[:, sl] = state_ref[:, sl] * wide[Q : Q + 1] + tn(b_bwd, vs)


def front(tokens, gain_row, w_in, conv_w, conv_b, dt_bias, rate_row, aux, x2, sizes):
    inner, channels, heads, state = sizes
    t, d = tokens.shape
    n = t // Q
    proj = w_in.shape[1]
    rev = lambda i: (n - 1 - i, 0)
    fixed = lambda i: (0, 0)
    blk = lambda width: pl.BlockSpec((Q, width), rev)
    whole = lambda a: pl.BlockSpec(a.shape, fixed)
    per = Q // HALO
    out = lambda width, dtype: jax.ShapeDtypeStruct((t, width), dtype)
    return pl.pallas_call(
        functools.partial(front_kernel, sizes),
        grid=(n,),
        in_specs=[
            blk(d),
            pl.BlockSpec((HALO, d), lambda i: (jnp.maximum((n - 1 - i) * per - 1, 0), 0)),
            whole(gain_row), whole(w_in), whole(conv_w), whole(conv_b), whole(dt_bias), whole(rate_row),
            blk(aux.shape[1]), whole(x2),
        ],
        out_specs=[
            blk(d), blk(inner), blk(channels), blk(channels), blk(channels), blk(channels),
            blk(2 * heads), blk(2 * heads), blk(2 * heads),
            pl.BlockSpec((1, state, inner), lambda i: (n - 1 - i, 0, 0)),
        ],
        out_shape=[
            out(d, bf16), out(inner, f32), out(channels, f32), out(channels, f32), out(channels, bf16), out(channels, f32),
            out(2 * heads, f32), out(2 * heads, f32), out(2 * heads, f32),
            jax.ShapeDtypeStruct((n, state, inner), bf16),
        ],
        scratch_shapes=[pltpu.VMEM((HALO + Q, channels), f32), pltpu.VMEM((state, inner), f32)],
        compiler_params=pltpu.CompilerParams(
            dimension_semantics=("arbitrary",), vmem_limit_bytes=60 * 1024 * 1024
        ),
        cost_estimate=pl.CostEstimate(flops=2 * t * d * proj, bytes_accessed=50_000_000, transcendentals=0),
    )(tokens, tokens, gain_row, w_in, conv_w, conv_b, dt_bias, rate_row, aux, x2)


def middle_kernel(
    sizes,
    tok_ref, act_ref, gate_ref, dt_ref, cum_ref, aux_ref, segrow_ref, cot_ref, sb_ref, w_ref,
    rate_ref, skip_ref, og_ref, x2_ref, r_ref,
    out_ref, nout_ref, dgate_ref, dy_ref, dv_ref, dbc_ref, drate_ref, dq_ref, sf_ref, dog_ref, dsk_ref,
    decay_ref, mix_ref, state_ref, adj_ref, ssm_ref, gated_ref, dno_ref, yf_ref, yb_ref, wide_ref,
    p_ref, q_ref, scal_ref,
):
    inner, channels, heads, state = sizes
    quad = 256
    step = pl.program_id(0)

    @pl.when(step == 0)
    def _():
        state_ref[...] = jnp.zeros_like(state_ref)
        adj_ref[...] = jnp.zeros_like(adj_ref)
        dog_ref[...] = jnp.zeros_like(dog_ref)
        dsk_ref[...] = jnp.zeros_like(dsk_ref)
        q_ref[...] = jnp.zeros_like(q_ref)

    sf_ref[0] = state_ref[...].astype(bf16)
    aux = aux_ref[...]
    row, col = iotas((Q, Q))
    lower = col < row
    same = aux[:, 3:4] == segrow_ref[0]
    b_f = act_ref[:, inner : inner + state].astype(bf16)
    c_f = act_ref[:, inner + state : inner + 2 * state].astype(bf16)
    b_b = act_ref[:, inner + 2 * state : inner + 3 * state].astype(bf16)
    c_b = act_ref[:, inner + 3 * state :].astype(bf16)
    g = jnp.where(same & (col != row), jnp.where(lower, nt(c_f, b_f), nt(c_b, b_b)), 0.0)
    dt = dt_ref[...]
    cum = cum_ref[...]
    rate = -dt * rate_ref[...]
    cf, cb = cum[:, :heads], cum[:, heads:] - rate[:, heads:]
    dtf, dtb = dt[:, :heads], dt[:, heads:]
    total_f, total_b = cum[Q - 1 :, :heads], cum[Q - 1 :, heads:]
    ldt = jnp.log(jnp.maximum(dt, 1e-37))
    rows = jnp.transpose(
        jnp.concatenate(
            [cf - ldt[:, :heads], cb + ldt[:, heads:], jnp.zeros((Q, Q - 2 * heads), f32)], axis=1
        )
    )
    scales = split2(
        jnp.concatenate(
            [
                jnp.exp(cf) * aux[:, 6:7],
                jnp.exp(total_b - cb) * aux[:, 7:8],
                dtf * jnp.exp(total_f - cf) * aux[:, 4:5],
                dtb * jnp.exp(cb) * aux[:, 5:6],
                jnp.broadcast_to(jnp.exp(total_f) * aux[Q - 1 :, 6:7], (8, heads)),
                jnp.broadcast_to(jnp.exp(total_b) * aux[0:1, 7:8], (8, heads)),
            ],
            axis=0,
        )
    )
    lane = lax.broadcasted_iota(jnp.int32, (1, Q), 1)
    first = (lane < Q // 2).astype(bf16)
    second = (lane >= Q // 2).astype(bf16)

    def apart(x):
        return jnp.concatenate([x * first, x * second], axis=0)

    squares = jnp.zeros((Q, quad), f32)
    dots = jnp.zeros((Q, quad), f32)
    cot = cot_ref[...]
    for at in range(0, inner, quad):
        sl = slice(at, at + quad)
        wide_ref[:, sl] = nn(scales, x2_ref[:, sl])
        v = act_ref[:, sl]
        low = v.astype(bf16)
        yf = nn(c_f, state_ref[:, sl].astype(bf16)) * wide_ref[:Q, sl]
        yb = nn(c_b, sb_ref[0, :, sl]) * wide_ref[Q : 2 * Q, sl]
        yf_ref[:, sl] = yf
        yb_ref[:, sl] = yb
        parts = []
        for half in range(2):
            mixes = []
            for h in (at // 64 + 2 * half, at // 64 + 2 * half + 1):
                gap = jnp.where(
                    lower,
                    cf[:, h : h + 1] - rows[h : h + 1, :],
                    rows[heads + h : heads + h + 1, :] - cb[:, h : h + 1],
                )
                decay = jnp.exp(gap)
                decay_ref[h] = decay
                mix = (g * decay).astype(bf16)
                mix_ref[h * Q : (h + 1) * Q, :] = mix
                mixes.append(mix)
            parts.append(
                nn(jnp.concatenate(mixes, axis=1), apart(low[:, half * Q : (half + 1) * Q]))
            )
        ssm = jnp.concatenate(parts, axis=1) + yf + yb + skip_ref[:, sl] * v
        ssm_ref[:, sl] = ssm
        gate = gate_ref[:, sl]
        gated = ssm * (gate / (1.0 + jnp.exp(-gate)))
        gated_ref[:, sl] = gated
        dno = nn(cot, w_ref[:, sl])
        dno_ref[:, sl] = dno
        squares += gated * gated
        dots += dno * og_ref[:, sl] * gated

    inv = lax.rsqrt(jnp.sum(squares, axis=1, keepdims=True) / inner + eps)
    drag = inv * (inv * jnp.sum(dots, axis=1, keepdims=True) / inner)
    dg = jnp.zeros((Q, Q), f32)
    d_cf = jnp.zeros((Q, state), f32)
    d_cb = jnp.zeros((Q, state), f32)
    d_bb = jnp.zeros((Q, state), f32)
    heads_of = jnp.zeros((3 * Q, Q), f32)
    for at in range(0, inner, quad):
        sl = slice(at, at + quad)
        v = act_ref[:, sl]
        low = v.astype(bf16)
        low_f = low.astype(f32)
        ssm, gate, gated, dno = ssm_ref[:, sl], gate_ref[:, sl], gated_ref[:, sl], dno_ref[:, sl]
        og = og_ref[:, sl]
        unit = gated * inv
        nout_ref[:, sl] = (unit * og).astype(bf16)
        dog_ref[:, sl] += jnp.sum(dno * unit, axis=0, keepdims=True)
        d_gated = inv * (dno * og) - gated * (inv * drag)
        sig = 1.0 / (1.0 + jnp.exp(-gate))
        d_ssm = d_gated * (gate * sig)
        dgate_ref[:, sl] = (d_gated * ssm * (sig * (1.0 + gate * (1.0 - sig)))).astype(bf16)
        dsk_ref[:, sl] += jnp.sum(d_ssm * v, axis=0, keepdims=True)
        dy = d_ssm.astype(bf16)
        dy_ref[:, sl] = dy
        dy_f = dy.astype(f32)
        parts = []
        for half in range(2):
            h0 = at // 64 + 2 * half
            cut = slice(half * Q, (half + 1) * Q)
            d_mix = nt(dy[:, cut], apart(low[:, cut]))
            for i in range(2):
                h = h0 + i
                x = d_mix[:, i * Q : (i + 1) * Q] * decay_ref[h]
                dg += x
                full = x * g
                under = jnp.where(lower, full, 0.0)
                over = full - under
                q_ref[h : h + 1, :] = jnp.sum(under, axis=0, keepdims=True)
                q_ref[heads + h : heads + h + 1, :] = jnp.sum(over, axis=0, keepdims=True)
                p_ref[:, h : h + 1] = jnp.sum(under, axis=1, keepdims=True)
                p_ref[:, heads + h : heads + h + 1] = jnp.sum(over, axis=1, keepdims=True)
            parts.append(tn(mix_ref[h0 * Q : (h0 + 2) * Q, :], apart(dy[:, cut])))
        adj = adj_ref[:, sl]
        adj_low = adj.astype(bf16)
        sf_low = state_ref[:, sl].astype(bf16)
        sb_low = sb_ref[0, :, sl]
        wide_wb = wide_ref[3 * Q : 4 * Q, sl]
        dvb = wide_wb * nn(b_b, adj_low)
        dv_ref[:, sl] = d_ssm * skip_ref[:, sl] + jnp.concatenate(parts, axis=1) + dvb
        prods = jnp.concatenate(
            [
                (dy_f * yf_ref[:, sl]).astype(bf16),
                (dy_f * yb_ref[:, sl]).astype(bf16),
                (low_f * dvb).astype(bf16),
            ],
            axis=0,
        )
        heads_of += nn(prods, r_ref[sl, :])
        dye_f = (dy_f * wide_ref[:Q, sl]).astype(bf16)
        dye_b = (dy_f * wide_ref[Q : 2 * Q, sl]).astype(bf16)
        vs_f = (low_f * wide_ref[2 * Q : 3 * Q, sl]).astype(bf16)
        vs_b = (low_f * wide_wb).astype(bf16)
        d_cf += nt(dye_f, sf_low)
        d_cb += nt(dye_b, sb_low)
        d_bb += nt(vs_b, adj_low)
        across_b = wide_ref[4 * Q + 8 : 4 * Q + 9, sl]
        scal_ref[:, sl] = jnp.sum(adj * sb_low.astype(f32), axis=0, keepdims=True) * across_b
        adj_ref[:, sl] = adj * across_b + tn(c_b, dye_b)
        state_ref[:, sl] = state_ref[:, sl] * wide_ref[4 * Q : 4 * Q + 1, sl] + tn(b_f, vs_f)

    out_ref[...] = (tok_ref[...].astype(f32) + nt(nout_ref[...], w_ref[...])).astype(bf16)
    dg = jnp.where(same & (col != row), dg, 0.0)
    dg_f = jnp.where(lower, dg, 0.0)
    dg_b = (dg - dg_f).astype(bf16)
    dg_f = dg_f.astype(bf16)
    dbc_ref[...] = jnp.concatenate(
        [tn(dg_f, c_f), d_cf + nn(dg_f, b_f), d_bb + tn(dg_b, c_b), d_cb + nn(dg_b, b_b)], axis=1
    )
    q_cols = jnp.transpose(q_ref[...])[:, : 2 * heads]
    dots_f, dots_b, dots_v = heads_of[:Q, :heads], heads_of[Q : 2 * Q, :heads], heads_of[2 * Q :, :heads]
    through = nn(split_rows(jnp.broadcast_to(scal_ref[...], (8, inner))), r_ref[...])
    through = (through[0:1] + through[8:9])[:, :heads]
    diff = p_ref[:, : 2 * heads] - q_cols
    d_rate_f = nn_exact((col >= row).astype(bf16), diff[:, :heads] + dots_f)
    d_rate_b = (
        nn_exact((col <= row).astype(bf16), diff[:, heads:] + dots_b)
        + nn_exact((col > row).astype(bf16), dots_v)
        + through
    )
    drate_ref[...] = jnp.concatenate([d_rate_f, d_rate_b], axis=1)
    dq_ref[...] = jnp.concatenate([q_cols[:, :heads], q_cols[:, heads:] + dots_v], axis=1)


def middle(tokens, act, gate, dt, cum, aux, segrow, cot, sb, w_out_t, rate_row, skip_row, og_row, x2, r, sizes):
    inner, channels, heads, state = sizes
    t, d = tokens.shape
    n = t // Q
    fwd = lambda i: (i, 0)
    fixed = lambda i: (0, 0)
    cube = lambda i: (i, 0, 0)
    blk = lambda width: pl.BlockSpec((Q, width), fwd)
    whole = lambda a: pl.BlockSpec(a.shape, fixed)
    out = lambda width, dtype: jax.ShapeDtypeStruct((t, width), dtype)
    line = jax.ShapeDtypeStruct((1, inner), f32)
    return pl.pallas_call(
        functools.partial(middle_kernel, sizes),
        grid=(n,),
        in_specs=[
            blk(d), blk(channels), blk(inner), blk(2 * heads), blk(2 * heads), blk(aux.shape[1]),
            pl.BlockSpec((1, 1, Q), cube), blk(d), pl.BlockSpec((1, state, inner), cube),
            whole(w_out_t), whole(rate_row), whole(skip_row), whole(og_row), whole(x2), whole(r),
        ],
        out_specs=[
            blk(d), blk(inner), blk(inner), blk(inner), blk(inner), blk(4 * state),
            blk(2 * heads), blk(2 * heads), pl.BlockSpec((1, state, inner), cube),
            pl.BlockSpec((1, inner), fixed), pl.BlockSpec((1, inner), fixed),
        ],
        out_shape=[
            out(d, bf16), out(inner, bf16), out(inner, bf16), out(inner, bf16), out(inner, f32),
            out(4 * state, f32), out(2 * heads, f32), out(2 * heads, f32),
            jax.ShapeDtypeStruct((n, state, inner), bf16), line, line,
        ],
        scratch_shapes=[
            pltpu.VMEM((heads, Q, Q), f32),
            pltpu.VMEM((heads * Q, Q), bf16),
            pltpu.VMEM((state, inner), f32),
            pltpu.VMEM((state, inner), f32),
            pltpu.VMEM((Q, inner), f32),
            pltpu.VMEM((Q, inner), f32),
            pltpu.VMEM((Q, inner), f32),
            pltpu.VMEM((Q, inner), f32),
            pltpu.VMEM((Q, inner), f32),
            pltpu.VMEM((4 * Q + 16, inner), f32),
            pltpu.VMEM((Q, Q), f32),
            pltpu.VMEM((Q, Q), f32),
            pltpu.VMEM((1, inner), f32),
        ],
        compiler_params=pltpu.CompilerParams(
            dimension_semantics=("arbitrary",), vmem_limit_bytes=60 * 1024 * 1024
        ),
        cost_estimate=pl.CostEstimate(flops=30_000_000_000, bytes_accessed=60_000_000, transcendentals=0),
    )(tokens, act, gate, dt, cum, aux, segrow, cot, sb, w_out_t, rate_row, skip_row, og_row, x2, r)


def back_kernel(
    sizes,
    tok_ref, cot_ref, gain_ref, w_ref, cw_ref, dtb_ref, rate_ref, aux_ref, x2_ref, r_ref,
    low_ref, dsil_ref, conv_ref, dt_ref, cum_ref, dtraw_ref,
    dgate_ref, dy_ref, dv_ref, dbc_ref, drate_ref, dq_ref, sf_ref,
    dproj_ref, dtok_ref, dgain_ref, dcw_ref, dcb_ref, ddtb_ref, dalog_ref,
    adj_ref, dpre_ref, scal_ref,
):
    inner, channels, heads, state = sizes
    quad = 256
    step = pl.program_id(0)

    @pl.when(step == 0)
    def _():
        adj_ref[...] = jnp.zeros_like(adj_ref)
        dpre_ref[...] = jnp.zeros_like(dpre_ref)
        dgain_ref[...] = jnp.zeros_like(dgain_ref)
        dcw_ref[...] = jnp.zeros_like(dcw_ref)
        dcb_ref[...] = jnp.zeros_like(dcb_ref)
        ddtb_ref[...] = jnp.zeros_like(ddtb_ref)
        dalog_ref[...] = jnp.zeros_like(dalog_ref)

    dpre_ref[Q:, :] = dpre_ref[0:8, :]
    aux = aux_ref[...]
    dt = dt_ref[...]
    cum = cum_ref[...]
    cf, dtf = cum[:, :heads], dt[:, :heads]
    total_f = cf[Q - 1 :, :]
    scales = split2(
        jnp.concatenate(
            [
                jnp.exp(cf) * aux[:, 6:7],
                dtf * jnp.exp(total_f - cf) * aux[:, 4:5],
                jnp.broadcast_to(jnp.exp(total_f) * aux[Q - 1 :, 6:7], (8, heads)),
            ],
            axis=0,
        )
    )
    b_f = low_ref[:, inner : inner + state]
    c_f = low_ref[:, inner + state : inner + 2 * state]
    dots = jnp.zeros((Q, Q), f32)
    d_bf = jnp.zeros((Q, state), f32)
    for at in range(0, inner, quad):
        sl = slice(at, at + quad)
        wide = nn(scales, x2_ref[:, sl])
        low_f = low_ref[:, sl].astype(f32)
        adj = adj_ref[:, sl]
        adj_low = adj.astype(bf16)
        wide_wf = wide[Q : 2 * Q]
        dvf = wide_wf * nn(b_f, adj_low)
        dots += nn((low_f * dvf).astype(bf16), r_ref[sl, :])
        d_bf += nt((low_f * wide_wf).astype(bf16), adj_low)
        across = wide[2 * Q : 2 * Q + 1]
        scal_ref[:, sl] = jnp.sum(adj * sf_ref[0, :, sl].astype(f32), axis=0, keepdims=True) * across
        dye = (dy_ref[:, sl].astype(f32) * wide[:Q]).astype(bf16)
        adj_ref[:, sl] = adj * across + tn(c_f, dye)
        dpre_ref[:Q, sl] = (dv_ref[:, sl] + dvf) * dsil_ref[:, sl]
    d_bc = dbc_ref[...] + jnp.concatenate([d_bf, jnp.zeros((Q, 3 * state), f32)], axis=1)
    dpre_ref[:Q, inner:] = d_bc * dsil_ref[:, inner:]

    n1, n2, n3 = aux[:, 8:9], aux[:, 9:10], aux[:, 10:11]
    for at in range(0, channels, quad):
        sl = slice(at, at + quad)
        conv = conv_ref[:, sl]
        z = dpre_ref[:Q, sl]
        dcb_ref[:, sl] += jnp.sum(z, axis=0, keepdims=True)
        dcw_ref[0:1, sl] += jnp.sum(z * conv, axis=0, keepdims=True)
        total = cw_ref[0:1, sl] * z
        for k, mask in ((1, n1), (2, n2), (3, n3)):
            z = dpre_ref[k : Q + k, sl] * mask
            dcw_ref[k : k + 1, sl] += jnp.sum(z * conv, axis=0, keepdims=True)
            total += cw_ref[k : k + 1, sl] * z
        dproj_ref[:, inner + at : inner + at + quad] = total.astype(bf16)
    dproj_ref[:, :inner] = dgate_ref[...]

    row, col = iotas((Q, Q))
    through = nn(split_rows(jnp.broadcast_to(scal_ref[...], (8, inner))), r_ref[...])
    through = (through[0:1] + through[8:9])[:, :heads]
    dots = dots[:, :heads]
    extra = nn_exact((col < row).astype(bf16), dots) + through
    none = jnp.zeros((Q, heads), f32)
    d_rate = drate_ref[...] + jnp.concatenate([extra, none], axis=1)
    d_dt = dq_ref[...] + jnp.concatenate([dots, none], axis=1)
    d_dt = jnp.where(dt > 0.0, d_dt / jnp.maximum(dt, 1e-37), 0.0)
    a = rate_ref[...]
    v = dtraw_ref[...] + dtb_ref[...]
    d_v = (d_dt - d_rate * a) / (1.0 + jnp.exp(-v))
    ddtb_ref[...] += jnp.sum(d_v, axis=0, keepdims=True)
    dalog_ref[...] += jnp.sum(d_rate * (-dt * a), axis=0, keepdims=True)
    dproj_ref[:, inner + channels :] = d_v.astype(bf16)

    d_normed = (
        nt(dproj_ref[:, :inner], w_ref[:, :inner])
        + nt(dproj_ref[:, inner : inner + channels], w_ref[:, inner : inner + channels])
        + nt(dproj_ref[:, inner + channels :], w_ref[:, inner + channels :])
    )
    x = tok_ref[...].astype(f32)
    inv = lax.rsqrt(jnp.mean(x * x, axis=1, keepdims=True) + eps)
    unit = x * inv
    dgain_ref[...] += jnp.sum(d_normed * unit, axis=0, keepdims=True)
    a = d_normed * gain_ref[...]
    dtok_ref[...] = cot_ref[...].astype(f32) + inv * (a - unit * jnp.mean(a * unit, axis=1, keepdims=True))


def back(
    tokens, cot, gain_row, w_in, conv_w, dt_bias, rate_row, aux, x2, r, low, dsil, conv, dt, cum, dtraw,
    dgate, dy, dv, dbc, drate, dq, sf, sizes,
):
    inner, channels, heads, state = sizes
    t, d = tokens.shape
    n = t // Q
    proj = w_in.shape[1]
    rev = lambda i: (n - 1 - i, 0)
    fixed = lambda i: (0, 0)
    blk = lambda a: pl.BlockSpec((Q, a.shape[1]), rev)
    whole = lambda a: pl.BlockSpec(a.shape, fixed)
    lines = [(1, d), (conv_w.shape[0], channels), (1, channels), (1, 2 * heads), (1, 2 * heads)]
    return pl.pallas_call(
        functools.partial(back_kernel, sizes),
        grid=(n,),
        in_specs=[
            blk(tokens), blk(cot), whole(gain_row), whole(w_in), whole(conv_w), whole(dt_bias), whole(rate_row),
            blk(aux), whole(x2), whole(r), blk(low), blk(dsil), blk(conv), blk(dt), blk(cum), blk(dtraw),
            blk(dgate), blk(dy), blk(dv), blk(dbc), blk(drate), blk(dq),
            pl.BlockSpec((1, state, inner), lambda i: (n - 1 - i, 0, 0)),
        ],
        out_specs=[pl.BlockSpec((Q, proj), rev), pl.BlockSpec((Q, d), rev)]
        + [pl.BlockSpec(s, fixed) for s in lines],
        out_shape=[jax.ShapeDtypeStruct((t, proj), bf16), jax.ShapeDtypeStruct((t, d), f32)]
        + [jax.ShapeDtypeStruct(s, f32) for s in lines],
        scratch_shapes=[
            pltpu.VMEM((state, inner), f32),
            pltpu.VMEM((Q + 8, channels), f32),
            pltpu.VMEM((1, inner), f32),
        ],
        compiler_params=pltpu.CompilerParams(
            dimension_semantics=("arbitrary",), vmem_limit_bytes=60 * 1024 * 1024
        ),
        cost_estimate=pl.CostEstimate(flops=20_000_000_000, bytes_accessed=60_000_000, transcendentals=0),
    )(
        tokens, cot, gain_row, w_in, conv_w, dt_bias, rate_row, aux, x2, r, low, dsil, conv, dt, cum, dtraw,
        dgate, dy, dv, dbc, drate, dq, sf,
    )


def features(segment_ids):
    t = segment_ids.shape[0]
    n = t // Q
    seg = segment_ids.astype(f32)
    earlier = [jnp.concatenate([jnp.full((k,), -1.0, f32), seg[: t - k]]) == seg for k in (1, 2, 3)]
    later = [jnp.concatenate([seg[k:], jnp.full((k,), -1.0, f32)]) == seg for k in (1, 2, 3)]
    chunks = seg.reshape(n, Q)
    ends, starts = chunks[:, -1:], chunks[:, :1]
    none = jnp.full((1, 1), -1.0, f32)
    like = lambda edge: (chunks == edge).reshape(t)
    columns = earlier + [
        seg,
        like(ends),
        like(starts),
        like(jnp.concatenate([none, ends[:-1]])),
        like(jnp.concatenate([starts[1:], none])),
    ] + later
    aux = jnp.stack([c.astype(f32) for c in columns], axis=1)
    return aux, chunks.reshape(n, 1, Q)


def local(tokens, segment_ids, w_in, w_out_t, gain, conv_w, conv_b, dt_bias, a_log, d_skip, out_gain, cotangent):
    heads = d_skip.shape[0]
    inner = out_gain.shape[0]
    channels = conv_w.shape[1]
    state = (channels - inner) // 4
    width = inner // heads
    sizes = (inner, channels, heads, state)
    aux, segrow = features(segment_ids)
    spread = np.arange(inner)[None, :] // width == np.arange(heads)[:, None]
    x2 = jnp.asarray(np.concatenate([spread, spread], axis=0), bf16)
    r = jnp.asarray(np.pad(spread.T, ((0, 0), (0, Q - heads))), bf16)
    gain_row = gain.astype(f32)[None, :]
    rate_row = jnp.exp(a_log)[None, :]
    dtb_row = dt_bias[None, :]
    skip_row = jnp.repeat(d_skip, width)[None, :]
    normed, gate, conv, act, low, dsil, dt, cum, dtraw, sb = front(
        tokens, gain_row, w_in, conv_w, conv_b[None, :], dtb_row, rate_row, aux, x2, sizes
    )
    output, nout, dgate, dy, dv, dbc, drate, dq, sf, d_og, d_sk = middle(
        tokens, act, gate, dt, cum, aux, segrow, cotangent, sb, w_out_t, rate_row, skip_row,
        out_gain[None, :], x2, r, sizes,
    )
    d_w_out_t = tn(cotangent, nout)
    dproj, d_tokens, d_gain, d_cw, d_cb, d_dtb, d_alog = back(
        tokens, cotangent, gain_row, w_in, conv_w, dtb_row, rate_row, aux, x2, r, low, dsil, conv, dt, cum, dtraw,
        dgate, dy, dv, dbc, drate, dq, sf, sizes,
    )
    d_w_in = tn(normed, dproj)
    d_sk = jnp.sum(d_sk.reshape(heads, width), axis=1)
    return output, d_tokens, d_w_in, d_w_out_t, d_gain[0], (d_cw, d_cb[0], d_dtb[0], d_alog[0], d_sk, d_og[0])


def body(tokens, segment_ids, w_in, w_out, norm_gain, conv_w, conv_b, dt_bias, a_log, d_skip, out_gain, cotangent):
    full_in = lax.all_gather(w_in, AXES, axis=0, tiled=True)
    full_out_t = lax.all_gather(w_out.T, AXES, axis=0, tiled=True)
    full_gain = lax.all_gather(norm_gain, AXES, axis=0, tiled=True)
    output, d_tokens, g_in, g_out_t, g_gain, small = local(
        tokens, segment_ids, full_in, full_out_t, full_gain, conv_w, conv_b, dt_bias, a_log, d_skip, out_gain,
        cotangent,
    )
    d_w_in = lax.psum_scatter(g_in, AXES, scatter_dimension=0, tiled=True)
    d_w_out = lax.psum_scatter(g_out_t, AXES, scatter_dimension=0, tiled=True).T
    d_gain = lax.psum_scatter(g_gain, AXES, scatter_dimension=0, tiled=True)
    small = lax.psum(small, AXES)
    return (output, d_tokens, d_w_in, d_w_out, d_gain) + tuple(small)


def solution(mesh):
    rows, cols, line, none = P(AXES, None), P(None, AXES), P(AXES), P()
    return jax.shard_map(
        body,
        mesh=mesh,
        in_specs=(rows, line, rows, cols, line, none, none, none, none, none, none, rows),
        out_specs=(rows, rows, rows, cols, line, none, none, none, none, none, none),
        check_vma=False,
    )
```

time: 943 us -> 460 us (0.49)
  matrix products: 417 us -> 18.2 us
  other arithmetic: 274 us -> 1.74 us
  waiting for transfers between devices: 96.5 us -> 217 us
  Pallas kernels: 0 us -> 111 us
  local copies, waits for them, and re-layouts: 46 us -> 15.7 us
    dot_general x30 -> x2, matrix products: 417 us -> 18.2 us  [tn(): lax.dot_general(a, b, (((0,), (0,)), ((), ())), preferred_element_type=f32)]
    pallas_call x0 -> x3, Pallas kernels: none -> 111 us  [the longest x1 46.5 us: middle(): pl.pallas_call(functools.partial(middle_kernel, sizes), grid=(n,), in_spe...]
    another operation x17 -> x1, other arithmetic: 91 us -> 0.77 us  [features(): aux = jnp.stack([c.astype(f32) for c in columns], axis=1)]
    unnamed x5 -> x6, waiting for transfers between devices: 76.1 us -> 163 us
    reduce_sum x8 -> x1, other arithmetic: 60.7 us -> 0.12 us  [local(): d_sk = jnp.sum(d_sk.reshape(heads, width), axis=1)]
    add x7 -> x0, other arithmetic: 60.3 us -> none  [the longest x6 55.8 us: group_backward(): grad_bwd + jnp.sum(d_mixer * decay_bwd * dt_bwd_g[:, None, :], axis=0)]
    all_gather x2, waiting for transfers between devices: 20.3 us -> 53.4 us  [the longest x1 34.9 us: body(): full_out_t = lax.all_gather(w_out.T, AXES, axis=0, tiled=True)]
    and x12 -> x0, other arithmetic: 31 us -> none  [body(): lower_mask = same_seg & (positions[None, :] < positions[:, None])]
  transfers between devices with their start and end apart: 4 -> 4, of which waited for: 2 -> 4; matrix products, arithmetic and copies ran while one was open for 76% -> 5% of each run, Pallas kernels for 0% -> 14%
where the time goes in v1:
time: 460 us; the launch traced here: 459 us
  waiting for transfers between devices  217 us (47%)
  Pallas kernels  111 us (24%)
  blocking collectives  82.2 us (18%)
  matrix products  18.2 us (4%)
  local copies, waits for them, and re-layouts  15.7 us (3%)
  between operations  13.9 us (3%)
    unnamed x6, waiting for transfers between devices  163 us
    unnamed x2, blocking collectives  82.2 us
    pallas_call x1, Pallas kernels, middle(): pl.pallas_call(functools.partial(middle_kernel, sizes), grid=(n,), in_spe...  46.5 us
    pallas_call x1, Pallas kernels, back(): pl.pallas_call(functools.partial(back_kernel, sizes), grid=(n,), in_specs...  39.9 us
    all_gather x1, waiting for transfers between devices, body(): full_out_t = lax.all_gather(w_out.T, AXES, axis=0, tiled=True)  34.9 us
    pallas_call x1, Pallas kernels, front(): pl.pallas_call(functools.partial(front_kernel, sizes), grid=(n,), in_spec...  24.1 us
    all_gather x1, waiting for transfers between devices, body(): full_in = lax.all_gather(w_in, AXES, axis=0, tiled=True)  18.5 us
    dot_general x2, matrix products, tn(): lax.dot_general(a, b, (((0,), (0,)), ((), ())), preferred_element_type=f32)  18.2 us
  transfers between devices with their start and end apart: 4, of which 4 were waited for; matrix products, arithmetic and copies ran while one was open for 5% of the time, Pallas kernels for 14%

profile of v1, /device:TPU:0, one launch (start us, length us, event | category | flops | bytes accessed | tf_op | source)
XLA Modules:
  0.0 459.2 jit_solution(186761371165241718)
XLA Ops:
  7.2 0.7 all-gather.3.cloned.1.call-update
  8.0 0.7 all-gather.5.cloned.1.call-update
  8.7 0.7 convert_bitcast_fusion
  10.1 0.8 fusion.3
  11.0 1.0 copy.52.aux_ref
  12.0 0.8 dynamic-update-slice
  12.9 42.1 %all-reduce.4 = bf16[768]{0:T(1024)(128)(2,1)S(1)} all-reduce(bf16[768]{0:T(1024)(128)(2,1)S(1)} %dynamic-update-slice), channel_id=1, replica_groups=mesh['fsdp'=8,'rep'=4] {'fsdp','rep'}, use_global_device_ids=true, to_apply=%add.4 | all-reduce | flops 768 | bytes 3072
  55.6 1.3 broadcast_in_dim.22.cb_ref
  56.8 0.7 broadcast_in_dim.25
  57.6 0.7 broadcast_in_dim_reshape.3.skip_ref
  58.2 1.3 broadcast_in_dim.26.og_ref
  59.5 1.2 exponential_bitcast_fusion.rate_ref
  60.7 18.5 %all-gather.3.cloned.1.call-done.w_ref = bf16[768,3376]{1,0:T(8,128)(2,1)} async-done(((bf16[24,3376]{1,0:T(8,128)(2,1)}), bf16[768,3376]{1,0:T(8,128)(2,1)}) %all-gather.3.cloned.1.call-update) | async-done | bytes 5185552 | tf_op jit(solution)/shard_map/all_gather | solution.py:601
  79.2 24.1 %shard_map.221 = (bf16[1024,768]{1,0:T(8,128)(2,1)}, f32[1024,1536]{1,0:T(8,128)}, f32[1024,1792]{1,0:T(8,128)}, f32[1024,1792]{1,0:T(8,128)}, bf16[1024,1792]{1...) custom-call(bf16[1024,768]{1,0:T(8,128)(2,1)} %tok_ref.5, ...), custom_call_target="tpu_custom_call" | custom-call | flops 5309988864 | bytes 50000000 | tf_op jit(solution)/shard_map/pallas_call | solution.py:130
  103.4 34.9 %all-gather.5.cloned.1.call-done.w_ref = bf16[768,1536]{1,0:T(8,128)(2,1)} async-done(((bf16[24,1536]{1,0:T(8,128)(2,1)}), bf16[768,1536]{1,0:T(8,128)(2,1)}) %all-gather.5.cloned.1.call-update) | async-done | bytes 2359312 | tf_op jit(solution)/shard_map/all_gather | solution.py:602
  138.3 46.5 %shard_map.222 = (bf16[1024,768]{1,0:T(8,128)(2,1)}, bf16[1024,1536]{1,0:T(8,128)(2,1)}, bf16[1024,1536]{1,0:T(8,128)(2,1)}, bf16[1024,1536]{1,0:T(8,128)(2,1)},...) custom-call(bf16[1024,768]{1,0:T(8,128)(2,1)} %tok_ref.5, ...), custom_call_target="tpu_custom_call" | custom-call | flops 30000001024 | bytes 60000000 | tf_op jit(solution)/shard_map/pallas_call | solution.py:362
  184.8 6.7 %convolution_bitcast_fusion = f32[768,1536]{0,1:T(8,128)} fusion(bf16[1024,1536]{1,0:T(8,128)(2,1)} %get-tuple-element.59, bf16[1024,768]{1,0:T(8,128)(2,1)S(1)} %copy-done.8), kind=kOutput, calls=%fused_computation | convolution fusion | flops 2415919104 | bytes 9437184 | tf_op jit(solution)/shard_map/dot_general | solution.py:28
  191.5 6.1 %copy.56 = f32[768,1536]{1,0:T(8,128)} copy(f32[768,1536]{0,1:T(8,128)} %convolution_bitcast_fusion) | data formatting | bytes 9437184
  197.8 39.9 %shard_map.223 = (bf16[1024,3376]{1,0:T(8,128)(2,1)}, f32[1024,768]{1,0:T(8,128)}, f32[1,768]{1,0:T(1,128)}, f32[4,1792]{1,0:T(4,128)}, f32[1,1792]{1,0:T(1,128)}, /*index=5*/f32[1,48]{1,0:T(1,128)}, f32[1,48]{1,0:T(1,128)}) custom-call(bf16[1024,768]{1,0:T(8,128)(2,1)} %tok_ref.5, bf16[1024,768]{1,0:T(8,128)(2,1)} %cot_ref.3, f32[1,768]{1,0:T(1,128)} %reshape.38.gain_ref, ...), custom_call_target="tpu_custom_call" | custom-call | flops 20000000000 | bytes 60000000 | tf_op jit(solution)/shard_map/pallas_call | solution.py:519
  237.8 11.5 %fusion.14 = f32[768,3376]{1,0:T(8,128)} fusion(bf16[1024,768]{1,0:T(8,128)(2,1)S(1)} %copy-done.9, bf16[1024,3376]{1,0:T(8,128)(2,1)} %get-tuple-element.58), kind=kOutput, calls=%fused_computation.31 | convolution fusion | flops 5309988864 | bytes 18857984 | tf_op jit(solution)/shard_map/dot_general | solution.py:28
  249.3 0.6 copy-done.2
  250.3 40.1 %all-reduce.7 = (f32[768]{0:T(1024)S(1)}, f32[4,1792]{1,0:T(4,128)}, f32[1792]{0:T(1024)}, f32[48]{0:T(128)}, f32[48]{0:T(128)}, /*index=5*/f32[24]{0:T(128)}, f32[1536]{0:T(1024)}) all-reduce(f32[768]{0:T(1024)S(1)} %reduce.2, f32[4,1792]{1,0:T(4,128)S(1)} %copy-done.1, ...), channel_id=4, replica_groups=mesh['fsdp'=8,'rep'=4] {'fsdp','rep'}, use_global_device_ids=true, to_apply=%region_2.0.clone | all-reduce | flops 11384 | bytes 91072
  291.0 13.2 %reduce-scatter.7.cloned.1.call-done = f32[24,1536]{1,0:T(8,128)} async-done(((f32[768,1536]{1,0:T(8,128)}), f32[24,1536]{1,0:T(8,128)}) %reduce-scatter.7.cloned.1.call-update) | async-done | bytes 147472
  304.2 148.5 %reduce-scatter.9.cloned.1.call-done = f32[24,3376]{1,0:T(8,128)} async-done(((f32[768,3376]{1,0:T(8,128)}), f32[24,3376]{1,0:T(8,128)}) %reduce-scatter.9.cloned.1.call-update) | async-done | bytes 324112
  (43 shorter events, 2.7 us)
Async XLA Ops:
  7.2 72.1 %all-gather.3.cloned.1.call-start = ((), (), s32[]{:S(2)}) async-start(), calls=%async_computation.2 | async-start | bytes 5474304 | tf_op jit(solution)/shard_map/all_gather | solution.py:601
  7.9 130.4 %all-gather.5.cloned.1.call-start = ((), (), s32[]{:S(2)}) async-start(), calls=%async_computation.3 | async-start | bytes 2433024 | tf_op jit(solution)/shard_map/all_gather | solution.py:602
  8.7 295.5 %reduce-scatter.7.cloned.1.call-start = ((), (), s32[]{:S(2)}) async-start(), calls=%async_computation.4 | async-start | bytes 4866048
  9.4 94.0 %copy-start = (f32[1024]{0:T(1024)}, f32[1024]{0:T(1024)S(1)}, u32[]{:S(2)}) copy-start(f32[1024]{0:T(1024)S(1)} %get-tuple-element.139) | copy-start | bytes 12292
  138.3 46.5 %copy-start.8 = (bf16[1024,768]{1,0:T(8,128)(2,1)S(1)}, bf16[1024,768]{1,0:T(8,128)(2,1)}, u32[]{:S(2)}) copy-start(bf16[1024,768]{1,0:T(8,128)(2,1)} %cot_ref.3) | copy-start | bytes 4718596
  197.6 255.1 %reduce-scatter.9.cloned.1.call-start = ((), (), s32[]{:S(2)}) async-start(), calls=%async_computation.5 | async-start | bytes 10948608
  197.8 40.0 %copy-start.9 = (bf16[1024,768]{1,0:T(8,128)(2,1)S(1)}, bf16[1024,768]{1,0:T(8,128)(2,1)}, u32[]{:S(2)}) copy-start(bf16[1024,768]{1,0:T(8,128)(2,1)} %get-tuple-element.57) | copy-start | bytes 4718596
  249.3 0.7 copy-start.2
  249.3 0.7 copy-start.5
  249.3 0.8 copy-start.4
  249.3 0.9 copy-start.3
  249.3 1.0 copy-start.1
  249.3 1.0 copy-start.6
  249.3 1.0 copy-start.7
Sparse Core Ops, SparseCore 0:
  10.9 68.3 all-gather.2
  82.0 56.1 all-gather.4
  197.7 106.4 reduce-scatter.6
  311.7 140.9 reduce-scatter.8

commit v2 on v1

--- a/solution.py
+++ b/solution.py
@@ -14,6 +14,7 @@
 f32 = jnp.float32
 bf16 = jnp.bfloat16
 AXES = ("fsdp", "rep")
+BIAS_AT, LOG_AT, SKIP_AT = 768, 896, 1024
 
 
 def nn(a, b):
@@ -78,7 +79,7 @@
     normed_ref[...] = normed
     both = jnp.concatenate([norm(halo_ref[...]), normed], axis=0)
     gate_ref[...] = nn(normed, w_ref[:, :inner])
-    dt_raw = nn(normed, w_ref[:, inner + channels :])
+    dt_raw = nn(normed, w_ref[:, inner + channels : inner + channels + 2 * heads])
     dtraw_ref[...] = dt_raw
     aux = aux_ref[...]
     m1, m2, m3 = aux[:, 0:1], aux[:, 1:2], aux[:, 2:3]
@@ -403,8 +404,8 @@
     sizes,
     tok_ref, cot_ref, gain_ref, w_ref, cw_ref, dtb_ref, rate_ref, aux_ref, x2_ref, r_ref,
     low_ref, dsil_ref, conv_ref, dt_ref, cum_ref, dtraw_ref,
-    dgate_ref, dy_ref, dv_ref, dbc_ref, drate_ref, dq_ref, sf_ref,
-    dproj_ref, dtok_ref, dgain_ref, dcw_ref, dcb_ref, ddtb_ref, dalog_ref,
+    dgate_ref, dy_ref, dv_ref, dbc_ref, drate_ref, dq_ref, sf_ref, dog_ref, dsk_ref,
+    dproj_ref, dtok_ref, small_ref,
     adj_ref, dpre_ref, scal_ref,
 ):
     inner, channels, heads, state = sizes
@@ -415,11 +416,12 @@
     def _():
         adj_ref[...] = jnp.zeros_like(adj_ref)
         dpre_ref[...] = jnp.zeros_like(dpre_ref)
-        dgain_ref[...] = jnp.zeros_like(dgain_ref)
-        dcw_ref[...] = jnp.zeros_like(dcw_ref)
-        dcb_ref[...] = jnp.zeros_like(dcb_ref)
-        ddtb_ref[...] = jnp.zeros_like(ddtb_ref)
-        dalog_ref[...] = jnp.zeros_like(dalog_ref)
+        small_ref[...] = jnp.zeros_like(small_ref)
+        small_ref[5:6, :inner] = dog_ref[...]
+        skips = nn(split_rows(jnp.broadcast_to(dsk_ref[...], (8, inner))), r_ref[...])
+        small_ref[6:7, SKIP_AT : SKIP_AT + Q] = skips[0:1] + skips[8:9]
+
+    d = tok_ref.shape[1]
 
     dpre_ref[Q:, :] = dpre_ref[0:8, :]
     aux = aux_ref[...]
@@ -464,12 +466,12 @@
         sl = slice(at, at + quad)
         conv = conv_ref[:, sl]
         z = dpre_ref[:Q, sl]
-        dcb_ref[:, sl] += jnp.sum(z, axis=0, keepdims=True)
-        dcw_ref[0:1, sl] += jnp.sum(z * conv, axis=0, keepdims=True)
+        small_ref[4:5, sl] += jnp.sum(z, axis=0, keepdims=True)
+        small_ref[0:1, sl] += jnp.sum(z * conv, axis=0, keepdims=True)
         total = cw_ref[0:1, sl] * z
         for k, mask in ((1, n1), (2, n2), (3, n3)):
             z = dpre_ref[k : Q + k, sl] * mask
-            dcw_ref[k : k + 1, sl] += jnp.sum(z * conv, axis=0, keepdims=True)
+            small_ref[k : k + 1, sl] += jnp.sum(z * conv, axis=0, keepdims=True)
             total += cw_ref[k : k + 1, sl] * z
         dproj_ref[:, inner + at : inner + at + quad] = total.astype(bf16)
     dproj_ref[:, :inner] = dgate_ref[...]
@@ -486,36 +488,35 @@
     a = rate_ref[...]
     v = dtraw_ref[...] + dtb_ref[...]
     d_v = (d_dt - d_rate * a) / (1.0 + jnp.exp(-v))
-    ddtb_ref[...] += jnp.sum(d_v, axis=0, keepdims=True)
-    dalog_ref[...] += jnp.sum(d_rate * (-dt * a), axis=0, keepdims=True)
+    small_ref[6:7, BIAS_AT : BIAS_AT + 2 * heads] += jnp.sum(d_v, axis=0, keepdims=True)
+    small_ref[6:7, LOG_AT : LOG_AT + 2 * heads] += jnp.sum(d_rate * (-dt * a), axis=0, keepdims=True)
     dproj_ref[:, inner + channels :] = d_v.astype(bf16)
 
     d_normed = (
         nt(dproj_ref[:, :inner], w_ref[:, :inner])
         + nt(dproj_ref[:, inner : inner + channels], w_ref[:, inner : inner + channels])
-        + nt(dproj_ref[:, inner + channels :], w_ref[:, inner + channels :])
+        + nt(dproj_ref[:, inner + channels :], w_ref[:, inner + channels : inner + channels + 2 * heads])
     )
     x = tok_ref[...].astype(f32)
     inv = lax.rsqrt(jnp.mean(x * x, axis=1, keepdims=True) + eps)
     unit = x * inv
-    dgain_ref[...] += jnp.sum(d_normed * unit, axis=0, keepdims=True)
+    small_ref[6:7, :d] += jnp.sum(d_normed * unit, axis=0, keepdims=True)
     a = d_normed * gain_ref[...]
     dtok_ref[...] = cot_ref[...].astype(f32) + inv * (a - unit * jnp.mean(a * unit, axis=1, keepdims=True))
 
 
 def back(
     tokens, cot, gain_row, w_in, conv_w, dt_bias, rate_row, aux, x2, r, low, dsil, conv, dt, cum, dtraw,
-    dgate, dy, dv, dbc, drate, dq, sf, sizes,
+    dgate, dy, dv, dbc, drate, dq, sf, dog, dsk, sizes,
 ):
     inner, channels, heads, state = sizes
     t, d = tokens.shape
     n = t // Q
-    proj = w_in.shape[1]
+    proj = inner + channels + 2 * heads
     rev = lambda i: (n - 1 - i, 0)
     fixed = lambda i: (0, 0)
     blk = lambda a: pl.BlockSpec((Q, a.shape[1]), rev)
     whole = lambda a: pl.BlockSpec(a.shape, fixed)
-    lines = [(1, d), (conv_w.shape[0], channels), (1, channels), (1, 2 * heads), (1, 2 * heads)]
     return pl.pallas_call(
         functools.partial(back_kernel, sizes),
         grid=(n,),
@@ -523,12 +524,14 @@
             blk(tokens), blk(cot), whole(gain_row), whole(w_in), whole(conv_w), whole(dt_bias), whole(rate_row),
             blk(aux), whole(x2), whole(r), blk(low), blk(dsil), blk(conv), blk(dt), blk(cum), blk(dtraw),
             blk(dgate), blk(dy), blk(dv), blk(dbc), blk(drate), blk(dq),
-            pl.BlockSpec((1, state, inner), lambda i: (n - 1 - i, 0, 0)),
-        ],
-        out_specs=[pl.BlockSpec((Q, proj), rev), pl.BlockSpec((Q, d), rev)]
-        + [pl.BlockSpec(s, fixed) for s in lines],
-        out_shape=[jax.ShapeDtypeStruct((t, proj), bf16), jax.ShapeDtypeStruct((t, d), f32)]
-        + [jax.ShapeDtypeStruct(s, f32) for s in lines],
+            pl.BlockSpec((1, state, inner), lambda i: (n - 1 - i, 0, 0)), whole(dog), whole(dsk),
+        ],
+        out_specs=[pl.BlockSpec((Q, proj), rev), pl.BlockSpec((Q, d), rev), pl.BlockSpec((8, channels), fixed)],
+        out_shape=[
+            jax.ShapeDtypeStruct((t, proj), bf16),
+            jax.ShapeDtypeStruct((t, d), f32),
+            jax.ShapeDtypeStruct((8, channels), f32),
+        ],
         scratch_shapes=[
             pltpu.VMEM((state, inner), f32),
             pltpu.VMEM((Q + 8, channels), f32),
@@ -540,7 +543,7 @@
         cost_estimate=pl.CostEstimate(flops=20_000_000_000, bytes_accessed=60_000_000, transcendentals=0),
     )(
         tokens, cot, gain_row, w_in, conv_w, dt_bias, rate_row, aux, x2, r, low, dsil, conv, dt, cum, dtraw,
-        dgate, dy, dv, dbc, drate, dq, sf,
+        dgate, dy, dv, dbc, drate, dq, sf, dog, dsk,
     )
 
 
@@ -587,35 +590,381 @@
         tokens, act, gate, dt, cum, aux, segrow, cotangent, sb, w_out_t, rate_row, skip_row,
         out_gain[None, :], x2, r, sizes,
     )
-    d_w_out_t = tn(cotangent, nout)
-    dproj, d_tokens, d_gain, d_cw, d_cb, d_dtb, d_alog = back(
+    d_w_out_t = tn(cotangent, nout).astype(bf16)
+    dproj, d_tokens, small = back(
         tokens, cotangent, gain_row, w_in, conv_w, dtb_row, rate_row, aux, x2, r, low, dsil, conv, dt, cum, dtraw,
-        dgate, dy, dv, dbc, drate, dq, sf, sizes,
-    )
-    d_w_in = tn(normed, dproj)
-    d_sk = jnp.sum(d_sk.reshape(heads, width), axis=1)
-    return output, d_tokens, d_w_in, d_w_out_t, d_gain[0], (d_cw, d_cb[0], d_dtb[0], d_alog[0], d_sk, d_og[0])
-
-
-def body(tokens, segment_ids, w_in, w_out, norm_gain, conv_w, conv_b, dt_bias, a_log, d_skip, out_gain, cotangent):
-    full_in = lax.all_gather(w_in, AXES, axis=0, tiled=True)
-    full_out_t = lax.all_gather(w_out.T, AXES, axis=0, tiled=True)
-    full_gain = lax.all_gather(norm_gain, AXES, axis=0, tiled=True)
-    output, d_tokens, g_in, g_out_t, g_gain, small = local(
-        tokens, segment_ids, full_in, full_out_t, full_gain, conv_w, conv_b, dt_bias, a_log, d_skip, out_gain,
-        cotangent,
-    )
-    d_w_in = lax.psum_scatter(g_in, AXES, scatter_dimension=0, tiled=True)
-    d_w_out = lax.psum_scatter(g_out_t, AXES, scatter_dimension=0, tiled=True).T
-    d_gain = lax.psum_scatter(g_gain, AXES, scatter_dimension=0, tiled=True)
-    small = lax.psum(small, AXES)
-    return (output, d_tokens, d_w_in, d_w_out, d_gain) + tuple(small)
+        dgate, dy, dv, dbc, drate, dq, sf, d_og, d_sk, sizes,
+    )
+    d_w_in = tn(normed, dproj).astype(bf16)
+    return output, d_tokens, d_w_in, d_w_out_t, small
+
+
+def unpack(small, taps, inner, heads, d):
+    return small[6, :d], (
+        small[:taps],
+        small[taps],
+        small[6, BIAS_AT : BIAS_AT + 2 * heads],
+        small[6, LOG_AT : LOG_AT + 2 * heads],
+        small[6, SKIP_AT : SKIP_AT + heads],
+        small[5, :inner],
+    )
+
+
+MESH = pl.DeviceIdType.MESH
+
+
+def place():
+    f = lax.axis_index("fsdp")
+    return f // 4, (f // 2) % 2, f % 2, lax.axis_index("rep")
+
+
+def flip(at, dy, dx, dc, k):
+    y, x, c, z = at
+    z_at = {0: z, 1: z + 1 - 2 * (z % 2), 2: (z + 2) % 4, 3: 3 - z}[k]
+    return (1 - y if dy else y, 1 - x if dx else x, 1 - c if dc else c, z_at)
+
+
+def device(at):
+    y, x, c, z = at
+    return ((y * 2 + x) * 2 + c, z)
+
+
+def slot(at):
+    y, x, c, z = at
+    return ((y * 2 + x) * 2 + c) * 4 + z
+
+
+def greet(me):
+    barrier = pltpu.get_barrier_semaphore()
+    others = [(0, 0, 1, 0), (0, 1, 0, 0), (1, 0, 0, 0), (0, 0, 0, 1), (0, 0, 0, 2), (0, 0, 0, 3)]
+    for other in others:
+        pl.semaphore_signal(barrier, inc=1, device_id=device(flip(me, *other)), device_id_type=MESH)
+    pl.semaphore_wait(barrier, len(others))
+
+
+def halves(width):
+    cut = (width // 2 + 127) // 128 * 128
+    return slice(0, cut), slice(cut, width)
+
+
+class Gatherer:
+    count = 39
+
+    def __init__(self, me, own, full, send, recv):
+        self.me, self.own, self.full, self.send, self.recv = me, own, full, send, recv
+        self.left, self.right = halves(full.shape[2])
+        self.copies = {}
+
+    def copy(self, name, block, to, cols=None):
+        i = len(self.copies)
+        at = slot(flip(self.me, *block))
+        dst = self.full.at[at] if cols is None else self.full.at[at, :, cols]
+        src = dst
+        if block == (0, 0, 0, 0):
+            src = self.own if cols is None else self.own.at[:, cols]
+        made = pltpu.make_async_remote_copy(
+            src_ref=src, dst_ref=dst, send_sem=self.send.at[i], recv_sem=self.recv.at[i],
+            device_id=device(flip(self.me, *to)), device_id_type=MESH,
+        )
+        made.start()
+        self.copies[name] = made
+
+    def arrived(self, name):
+        self.copies[name].wait_recv()
+
+    def start(self):
+        for k in (1, 2, 3):
+            self.copy(("z", k), (0, 0, 0, 0), (0, 0, 0, k))
+        self.spread(0)
+
+    def spread(self, k):
+        self.copy(("x", k), (0, 0, 0, k), (0, 1, 0, 0))
+        self.copy(("y", k), (0, 0, 0, k), (1, 0, 0, 0))
+        self.copy(("c", k), (0, 0, 0, k), (0, 0, 1, 0))
+
+    def column(self):
+        for k in (1, 2, 3):
+            self.arrived(("z", k))
+            self.spread(k)
+
+    def corner(self):
+        for k in range(4):
+            self.arrived(("x", k))
+            self.copy(("left", k), (0, 1, 0, k), (1, 0, 0, 0), self.left)
+            self.copy(("cx", k), (0, 1, 0, k), (0, 0, 1, 0))
+            self.arrived(("y", k))
+            self.copy(("right", k), (1, 0, 0, k), (0, 1, 0, 0), self.right)
+            self.copy(("cy", k), (1, 0, 0, k), (0, 0, 1, 0))
+
+    def last(self):
+        for k in range(4):
+            self.arrived(("left", k))
+            self.copy(("cl", k), (1, 1, 0, k), (0, 0, 1, 0), self.left)
+            self.arrived(("right", k))
+            self.copy(("cr", k), (1, 1, 0, k), (0, 0, 1, 0), self.right)
+
+    def finish(self):
+        for name, made in self.copies.items():
+            if name[0][0] == "c":
+                made.wait_recv()
+        for made in self.copies.values():
+            made.wait_send()
+
+
+def gather_kernel(*refs):
+    n = (len(refs) - 3) // 2
+    owns, fulls = refs[:n], refs[n : 2 * n]
+    send, recv, here = refs[2 * n :]
+    me = place()
+    greet(me)
+    work = [Gatherer(me, owns[i], fulls[i], send.at[i], recv.at[i]) for i in range(n)]
+    for w in work:
+        w.start()
+    locals_ = [pltpu.make_async_copy(owns[i], fulls[i].at[slot(me)], here.at[i]) for i in range(n)]
+    for made in locals_:
+        made.start()
+    for phase in ("column", "corner", "last", "finish"):
+        for w in work:
+            getattr(w, phase)()
+    for made in locals_:
+        made.wait()
+
+
+def gather(*shards):
+    n = len(shards)
+    return pl.pallas_call(
+        gather_kernel,
+        in_specs=[pl.BlockSpec(memory_space=pl.ANY)] * n,
+        out_specs=[pl.BlockSpec(memory_space=pl.ANY)] * n,
+        out_shape=[jax.ShapeDtypeStruct((32,) + s.shape, s.dtype) for s in shards],
+        scratch_shapes=[
+            pltpu.SemaphoreType.DMA((n, Gatherer.count)),
+            pltpu.SemaphoreType.DMA((n, Gatherer.count)),
+            pltpu.SemaphoreType.DMA((n,)),
+        ],
+        compiler_params=pltpu.CompilerParams(collective_id=0, has_side_effects=True),
+    )(*shards)
+
+
+BLOCKS = ((1, 1), (0, 1), (1, 0), (0, 0))
+
+
+class Scatterer:
+    count = 43
+
+    def __init__(self, me, part, out, mine, from_core, from_pair, from_far, from_line, send, recv, here):
+        self.me, self.part, self.out = me, part, out
+        self.mine, self.from_core, self.from_pair, self.from_far, self.from_line = (
+            mine, from_core, from_pair, from_far, from_line,
+        )
+        self.send, self.recv, self.here = send, recv, here
+        self.left, self.right = halves(part.shape[2])
+        self.copies = {}
+
+    def copy(self, name, src, dst, to):
+        i = len(self.copies)
+        made = pltpu.make_async_remote_copy(
+            src_ref=src, dst_ref=dst, send_sem=self.send.at[i], recv_sem=self.recv.at[i],
+            device_id=device(flip(self.me, *to)), device_id_type=MESH,
+        )
+        made.start()
+        self.copies[name] = made
+
+    def start(self):
+        self.locals = {}
+        for b, (dy, dx) in enumerate(BLOCKS):
+            for k in range(4):
+                other = slot(flip(self.me, dy, dx, 1, k))
+                self.copy(("core", b, k), self.part.at[other], self.from_core.at[b, k], (0, 0, 1, 0))
+                own = slot(flip(self.me, dy, dx, 0, k))
+                made = pltpu.make_async_copy(self.part.at[own], self.mine.at[b, k], self.here.at[b * 4 + k])
+                made.start()
+                self.locals[b, k] = made
+
+    def add(self, b, k, cols, others):
+        total = self.mine[b, k, :, cols].astype(f32)
+        for ref in others:
+            total += ref.astype(f32)
+        return total
+
+    def pair(self):
+        for b, (dy, dx) in enumerate(BLOCKS):
+            for k in range(4):
+                self.locals[b, k].wait()
+                self.copies["core", b, k].wait_recv()
+                self.mine[b, k] = (self.mine[b, k].astype(f32) + self.from_core[b, k].astype(f32)).astype(bf16)
+                if dx:
+                    self.copy(
+                        ("x", b, k), self.mine.at[b, k, :, self.left], self.from_pair.at[b, k, :, self.left],
+                        (0, 1, 0, 0),
+                    )
+                if dy:
+                    self.copy(
+                        ("y", b, k), self.mine.at[b, k, :, self.right], self.from_pair.at[b // 2, k, :, self.right],
+                        (1, 0, 0, 0),
+                    )
+
+    def far(self):
+        for k in range(4):
+            self.copies["x", 0, k].wait_recv()
+            self.mine[2, k, :, self.left] = self.add(
+                2, k, self.left, [self.from_pair[0, k, :, self.left]]
+            ).astype(bf16)
+            self.copy(("fy", k), self.mine.at[2, k, :, self.left], self.from_far.at[k, :, self.left], (1, 0, 0, 0))
+            self.copies["y", 0, k].wait_recv()
+            self.mine[1, k, :, self.right] = self.add(
+                1, k, self.right, [self.from_pair[0, k, :, self.right]]
+            ).astype(bf16)
+            self.copy(("fx", k), self.mine.at[1, k, :, self.right], self.from_far.at[k, :, self.right], (0, 1, 0, 0))
+
+    def line(self):
+        for k in (1, 2, 3, 0):
+            for name in (("x", 1, k), ("y", 2, k), ("fy", k), ("fx", k)):
+                self.copies[name].wait_recv()
+            if k:
+                self.mine[3, k] = self.add(3, k, slice(None), [self.from_pair[1, k], self.from_far[k]]).astype(bf16)
+                self.copy(("z", k), self.mine.at[3, k], self.from_line.at[k - 1], (0, 0, 0, k))
+
+    def finish(self):
+        for k in (1, 2, 3):
+            self.copies["z", k].wait_recv()
+        self.out[...] = self.add(
+            3, 0, slice(None),
+            [self.from_pair[1, 0], self.from_far[0], self.from_line[0], self.from_line[1], self.from_line[2]],
+        )
+        for made in self.copies.values():
+            made.wait_send()
+
+
+def scatter_scratch(rows, width):
+    vmem = lambda *lead: pltpu.VMEM(lead + (rows, width), bf16)
+    return [
+        vmem(4, 4), vmem(4, 4), vmem(2, 4), vmem(4), vmem(3),
+        pltpu.SemaphoreType.DMA((Scatterer.count,)), pltpu.SemaphoreType.DMA((Scatterer.count,)),
+        pltpu.SemaphoreType.DMA((16,)),
+    ]
+
+
+class Summer:
+    def __init__(self, me, own, out, held, send, recv):
+        self.me, self.own, self.out, self.held, self.send, self.recv = me, own, out, held, send, recv
+        self.copies = []
+
+    def copy(self, src, dst, to):
+        i = len(self.copies)
+        made = pltpu.make_async_remote_copy(
+            src_ref=src, dst_ref=dst, send_sem=self.send.at[i], recv_sem=self.recv.at[i],
+            device_id=device(flip(self.me, *to)), device_id_type=MESH,
+        )
+        made.start()
+        self.copies.append(made)
+
+    def start(self):
+        self.copy(self.own, self.held.at[0], (0, 0, 1, 0))
+
+    def second(self):
+        self.copies[0].wait_recv()
+        self.out[...] = self.own[...] + self.held[0]
+        self.held[6] = self.out[...]
+        self.copy(self.held.at[6], self.held.at[1], (0, 1, 0, 0))
+
+    def third(self):
+        self.copies[1].wait_recv()
+        self.held[7] = self.held[6] + self.held[1]
+        self.copy(self.held.at[7], self.held.at[2], (1, 0, 0, 0))
+
+    def fourth(self):
+        self.copies[2].wait_recv()
+        self.held[8] = self.held[7] + self.held[2]
+        for k in (1, 2, 3):
+            self.copy(self.held.at[8], self.held.at[2 + k], (0, 0, 0, k))
+
+    def finish(self):
+        for made in self.copies[3:]:
+            made.wait_recv()
+        self.out[...] = (self.held[8] + self.held[3]) + (self.held[4] + self.held[5])
+        for made in self.copies:
+            made.wait_send()
+
+
+def scatter_kernel(n, *refs):
+    parts, small = refs[:n], refs[n]
+    outs, small_out = refs[n + 1 : 2 * n + 1], refs[2 * n + 1]
+    scratch = refs[2 * n + 2 :]
+    me = place()
+    greet(me)
+    work = [Scatterer(me, parts[i], outs[i], *scratch[8 * i : 8 * i + 8]) for i in range(n)]
+    tiny = Summer(me, small, small_out, *scratch[8 * n :])
+    tiny.start()
+    for w in work:
+        w.start()
+    tiny.second()
+    for w in work:
+        w.pair()
+    tiny.third()
+    for w in work:
+        w.far()
+    tiny.fourth()
+    for w in work:
+        w.line()
+    for w in work:
+        w.finish()
+    tiny.finish()
+
+
+def scatter(parts, small):
+    n = len(parts)
+    scratch = []
+    for p in parts:
+        scratch += scatter_scratch(p.shape[1], p.shape[2])
+    scratch += [
+        pltpu.VMEM((9,) + small.shape, f32), pltpu.SemaphoreType.DMA((6,)), pltpu.SemaphoreType.DMA((6,)),
+    ]
+    vmem = pl.BlockSpec(memory_space=pltpu.VMEM)
+    return pl.pallas_call(
+        functools.partial(scatter_kernel, n),
+        in_specs=[pl.BlockSpec(memory_space=pl.ANY)] * n + [vmem],
+        out_specs=[vmem] * (n + 1),
+        out_shape=[jax.ShapeDtypeStruct(p.shape[1:], f32) for p in parts]
+        + [jax.ShapeDtypeStruct(small.shape, f32)],
+        scratch_shapes=scratch,
+        compiler_params=pltpu.CompilerParams(
+            collective_id=1, has_side_effects=True, vmem_limit_bytes=60 * 1024 * 1024
+        ),
+    )(*parts, small)
+
+
+def body(here, tokens, segment_ids, w_in, w_out, norm_gain, conv_w, conv_b, dt_bias, a_log, d_skip, out_gain, cotangent):
+    rows, proj = w_in.shape
+    d, inner, heads = tokens.shape[1], out_gain.shape[0], d_skip.shape[0]
+    parts = d // rows
+    w_ext = jnp.concatenate([w_in, norm_gain[:, None]], axis=1)
+    if here:
+        full_in, full_out_t = gather(w_ext, w_out.T)
+    else:
+        full_in, full_out_t = lax.all_gather(w_ext, AXES), lax.all_gather(w_out.T, AXES)
+    full_in = full_in.reshape(d, proj + 1)
+    output, d_tokens, g_in, g_out_t, small = local(
+        tokens, segment_ids, full_in, full_out_t.reshape(d, inner), full_in[:, proj], conv_w, conv_b, dt_bias, a_log,
+        d_skip, out_gain, cotangent,
+    )
+    g_in, g_out_t = g_in.reshape(parts, rows, proj), g_out_t.reshape(parts, rows, inner)
+    if here:
+        d_w_in, d_w_out, small = scatter([g_in, g_out_t], small)
+    else:
+        d_w_in = lax.psum_scatter(g_in.astype(f32), AXES, scatter_dimension=0)
+        d_w_out = lax.psum_scatter(g_out_t.astype(f32), AXES, scatter_dimension=0)
+        small = lax.psum(small, AXES)
+    d_gain, small = unpack(small, conv_w.shape[0], inner, heads, d)
+    d_gain = lax.dynamic_slice_in_dim(d_gain, lax.axis_index(AXES) * rows, rows)
+    return (output, d_tokens, d_w_in, d_w_out.T, d_gain) + small
 
 
 def solution(mesh):
     rows, cols, line, none = P(AXES, None), P(None, AXES), P(AXES), P()
+    here = dict(mesh.shape) == {"fsdp": 8, "rep": 4}
     return jax.shard_map(
-        body,
+        functools.partial(body, here),
         mesh=mesh,
         in_specs=(rows, line, rows, cols, line, none, none, none, none, none, none, rows),
         out_specs=(rows, rows, rows, cols, line, none, none, none, none, none, none),

time: 460 us -> 266 us (0.58)
  waiting for transfers between devices: 217 us -> 0 us
  Pallas kernels: 111 us -> 215 us
  blocking collectives: 82.2 us -> 0 us
  between operations: 13.9 us -> 0.73 us
  local copies, waits for them, and re-layouts: 15.7 us -> 26.2 us
    unnamed x6 -> x0, waiting for transfers between devices: 163 us -> none
    pallas_call x0 -> x2, Pallas kernels: none -> 104 us  [the longest x1 59.7 us: scatter(): pl.pallas_call(functools.partial(scatter_kernel, n), in_specs=[pl.BlockSp...]
    unnamed x2 -> x0, blocking collectives: 82.2 us -> none
    all_gather x2 -> x0, waiting for transfers between devices: 53.4 us -> none  [the longest x1 34.9 us: body(): full_out_t = lax.all_gather(w_out.T, AXES, axis=0, tiled=True)]
    convert_element_type x0 -> x2, local copies, waits for them, and re-layouts: none -> 8.54 us  [the longest x1 7.95 us: local(): d_w_in = tn(normed, dproj).astype(bf16)]
    slice x0 -> x4, local copies, waits for them, and re-layouts: none -> 5.03 us  [the longest x1 1.44 us: unpack(): small[taps]]
    unnamed x24 -> x12, local copies, waits for them, and re-layouts: 8.14 us -> 3.32 us
  transfers between devices with their start and end apart: 4 -> 0, of which waited for: 4 -> 0; matrix products, arithmetic and copies ran while one was open for 5% -> 0% of each run, Pallas kernels for 14% -> 0%
where the time goes in v2:
time: 266 us; the launch traced here: 265 us
  Pallas kernels  215 us (81%)
  local copies, waits for them, and re-layouts  26.2 us (10%)
  matrix products  19.1 us (7%)
  other arithmetic  4.35 us (2%)
    pallas_call x1, Pallas kernels, scatter(): pl.pallas_call(functools.partial(scatter_kernel, n), in_specs=[pl.BlockSp...  59.7 us
    pallas_call x1, Pallas kernels, middle(): pl.pallas_call(functools.partial(middle_kernel, sizes), grid=(n,), in_spe...  46.4 us
    pallas_call x1, Pallas kernels, gather(): pl.pallas_call(gather_kernel, in_specs=[pl.BlockSpec(memory_space=pl.ANY)...  44.7 us
    pallas_call x1, Pallas kernels, back(): pl.pallas_call(functools.partial(back_kernel, sizes), grid=(n,), in_specs...  40.2 us
    pallas_call x1, Pallas kernels, front(): pl.pallas_call(functools.partial(front_kernel, sizes), grid=(n,), in_spec...  24.2 us
    dot_general x2, matrix products, tn(): lax.dot_general(a, b, (((0,), (0,)), ((), ())), preferred_element_type=f32)  19.1 us
    convert_element_type x1, local copies, waits for them, and re-layouts, local(): d_w_in = tn(normed, dproj).astype(bf16)  7.95 us

profile of v2, /device:TPU:0, one launch (start us, length us, event | category | flops | bytes accessed | tf_op | source)
XLA Modules:
  0.0 265.5 jit_solution(11859960836402982827)
XLA Ops:
  0.6 0.7 convert_bitcast_fusion
  2.1 0.8 fusion.3
  2.9 1.0 copy.56.aux_ref
  4.0 0.7 copy.53
  4.7 1.7 pad_maximum_fusion.refs_0_
  6.4 44.7 %shard_map.221 = (bf16[32,24,3377]{2,1,0:T(8,128)(2,1)}, bf16[32,24,1536]{2,1,0:T(8,128)(2,1)}) custom-call(bf16[24,3377]{1,0:T(8,128)(2,1)} %pad_maximum_fusion.refs_0_, bf16[24,1536]{1,0:T(8,128)(2,1)} %bitcast.63), custom_call_target="tpu_custom_call" | custom-call | tf_op jit(solution)/shard_map/pallas_call | solution.py:735
  51.0 1.1 convert_reduce_fusion
  52.8 1.2 exponential_bitcast_fusion.rate_ref
  54.0 1.3 broadcast_in_dim.20.cb_ref
  55.3 24.2 %shard_map.222 = (bf16[1024,768]{1,0:T(8,128)(2,1)}, f32[1024,1536]{1,0:T(8,128)}, f32[1024,1792]{1,0:T(8,128)}, f32[1024,1792]{1,0:T(8,128)}, bf16[1024,1792]{1...) custom-call(bf16[1024,768]{1,0:T(8,128)(2,1)} %tok_ref.5, ...), custom_call_target="tpu_custom_call" | custom-call | flops 5311561728 | bytes 50000000 | tf_op jit(solution)/shard_map/pallas_call | solution.py:131
  80.8 46.4 %shard_map.223 = (bf16[1024,768]{1,0:T(8,128)(2,1)}, bf16[1024,1536]{1,0:T(8,128)(2,1)}, bf16[1024,1536]{1,0:T(8,128)(2,1)}, bf16[1024,1536]{1,0:T(8,128)(2,1)},...) custom-call(bf16[1024,768]{1,0:T(8,128)(2,1)} %tok_ref.5, ...), custom_call_target="tpu_custom_call" | custom-call | flops 30000001024 | bytes 60000000 | tf_op jit(solution)/shard_map/pallas_call | solution.py:363
  127.2 40.2 %shard_map.224 = (bf16[1024,3376]{1,0:T(8,128)(2,1)}, f32[1024,768]{1,0:T(8,128)}, f32[8,1792]{1,0:T(8,128)}) custom-call(bf16[1024,768]{1,0:T(8,128)(2,1)} %tok_ref.5, bf16[1024,768]{1,0:T(8,128)(2,1)} %cot_ref.3, f32[1,768]{1,0:T(1,128)} %reshape.63.gain_ref, bf16[768,3377]{1,0:T(8,128)(2,1)} %bitcast.76, f32[4,1792]{1,0:T(4,128)} %cw_ref.3, ...), custom_call_target="tpu_custom_call" | custom-call | flops 20000000000 | bytes 60000000 | tf_op jit(solution)/shard_map/pallas_call | solution.py:520
  167.4 13.3 %convolution_convert_fusion = bf16[768,3376]{0,1:T(8,128)(2,1)} fusion(bf16[1024,768]{1,0:T(8,128)(2,1)S(1)} %copy-done.4, bf16[1024,3376]{1,0:T(8,128)(2,1)} %get-tuple-element.63), kind=kOutput, calls=%fused_computation | convolution fusion | flops 5312581632 | bytes 13672448 | tf_op jit(solution)/shard_map/dot_general | solution.py:29
  180.7 8.0 %copy.59 = bf16[768,3376]{1,0:T(8,128)(2,1)} copy(bf16[768,3376]{0,1:T(8,128)(2,1)} %convolution_convert_fusion) | data formatting | bytes 10371072 | tf_op jit(solution)/shard_map/convert_element_type | solution.py:598
  188.7 5.8 %convolution_convert_fusion.1 = bf16[1536,768]{0,1:T(8,128)(2,1)} fusion(bf16[1024,1536]{1,0:T(8,128)(2,1)} %get-tuple-element.64, bf16[1024,768]{1,0:T(8,128)(2,1)S(1)} %copy-done.3), kind=kOutput, calls=%fused_computation.1 | convolution fusion | flops 2417098752 | bytes 7077888 | tf_op jit(solution)/shard_map/dot_general | solution.py:29
  194.5 59.7 %shard_map.225 = (f32[24,3376]{1,0:T(8,128)}, f32[24,1536]{1,0:T(8,128)}, f32[8,1792]{1,0:T(8,128)}) custom-call(bf16[32,24,3376]{2,1,0:T(8,128)(2,1)} %bitcast.58, bf16[32,24,1536]{2,1,0:T(8,128)(2,1)} %bitcast.59, f32[8,1792]{1,0:T(8,128)} %get-tuple-element.65.refs_2_), custom_call_target="tpu_custom_call" | custom-call | tf_op jit(solution)/shard_map/pallas_call | solution.py:924
  254.2 1.4 slice.68
  255.6 0.7 slice.67
  257.0 1.4 slice_reduce_fusion
  258.4 1.4 slice_reduce_fusion.1
  259.8 1.2 slice_bitcast_fusion.1
  261.0 1.2 slice_bitcast_fusion
  262.2 1.7 copy.62
  263.9 1.6 copy.63
  (24 shorter events, 3.3 us)
Async XLA Ops:
  1.3 78.1 %copy-start = (f32[1024]{0:T(1024)}, f32[1024]{0:T(1024)S(1)}, u32[]{:S(2)}) copy-start(f32[1024]{0:T(1024)S(1)} %get-tuple-element.92) | copy-start | bytes 12292
  55.3 24.2 %copy-start.2 = (f32[24]{0:T(128)S(1)}, f32[24]{0:T(128)}, u32[]{:S(2)}) copy-start(f32[24]{0:T(128)} %param.23) | copy-start | bytes 292
  55.3 24.9 %copy-start.1 = (f32[1536]{0:T(1024)S(1)}, f32[1536]{0:T(1024)}, u32[]{:S(2)}) copy-start(f32[1536]{0:T(1024)} %param.24) | copy-start | bytes 18436
  127.2 40.2 %copy-start.4 = (bf16[1024,768]{1,0:T(8,128)(2,1)S(1)}, bf16[1024,768]{1,0:T(8,128)(2,1)}, u32[]{:S(2)}) copy-start(bf16[1024,768]{1,0:T(8,128)(2,1)} %get-tuple-element.62) | copy-start | bytes 4718596
  180.7 8.0 %copy-start.3 = (bf16[1024,768]{1,0:T(8,128)(2,1)S(1)}, bf16[1024,768]{1,0:T(8,128)(2,1)}, u32[]{:S(2)}) copy-start(bf16[1024,768]{1,0:T(8,128)(2,1)} %cot_ref.3) | copy-start | bytes 4718596

commit v3 on v1

--- a/solution.py
+++ b/solution.py
@@ -14,6 +14,7 @@
 f32 = jnp.float32
 bf16 = jnp.bfloat16
 AXES = ("fsdp", "rep")
+BIAS_AT, LOG_AT, SKIP_AT = 768, 896, 1024
 
 
 def nn(a, b):
@@ -54,14 +55,438 @@
     )
 
 
+MESH = pl.DeviceIdType.MESH
+LINE = 4
+STEPS = (0, -1, 1, -2, 2, -3, 3)
+LAG = 2
+
+
+def place():
+    f = lax.axis_index("fsdp")
+    return f // 4, (f // 2) % 2, f % 2, lax.axis_index("rep")
+
+
+def flip(at, dy, dx, dc, dz):
+    y, x, c, z = at
+    return (1 - y if dy else y, 1 - x if dx else x, 1 - c if dc else c, z + dz)
+
+
+def device(at):
+    y, x, c, z = at
+    return ((y * 2 + x) * 2 + c, z)
+
+
+def slot(at):
+    y, x, c, z = at
+    return ((y * 2 + x) * 2 + c) * LINE + z
+
+
+def on_line(me, dz):
+    z = me[3]
+    return z >= -dz if dz < 0 else z < LINE - dz
+
+
+def when(condition, act):
+    if condition is True:
+        act()
+    else:
+        pl.when(condition)(act)
+
+
+def greet(me):
+    barrier = pltpu.get_barrier_semaphore()
+    for other in ((0, 0, 1, 0), (0, 1, 0, 0), (1, 0, 0, 0)):
+        pl.semaphore_signal(barrier, inc=1, device_id=device(flip(me, *other)), device_id_type=MESH)
+    for dz in (-1, 1):
+
+        @pl.when(on_line(me, dz))
+        def _():
+            pl.semaphore_signal(barrier, inc=1, device_id=device(flip(me, 0, 0, 0, dz)), device_id_type=MESH)
+
+    inside = jnp.where((me[3] > 0) & (me[3] < LINE - 1), 1, 0)
+    pl.semaphore_wait(barrier, 4 + inside)
+
+
+def halves(width):
+    cut = (width // 2 + 127) // 128 * 128
+    return slice(0, cut), slice(cut, width)
+
+
+class Gatherer:
+    kinds = ("z", "x", "y", "c", "left", "right", "cx", "cy", "cl", "cr")
+    count = len(kinds) * len(STEPS)
+
+    def __init__(self, me, own, full, send, recv):
+        self.me, self.own, self.full, self.send, self.recv = me, own, full, send, recv
+        self.left, self.right = halves(full.shape[2])
+
+    def made(self, kind, dz, block, to, cols=None):
+        i = self.kinds.index(kind) * len(STEPS) + STEPS.index(dz)
+        at = slot(flip(self.me, *block))
+        dst = self.full.at[at] if cols is None else self.full.at[at, :, cols]
+        src = dst
+        if block == (0, 0, 0, 0):
+            src = self.own if cols is None else self.own.at[:, cols]
+        return pltpu.make_async_remote_copy(
+            src_ref=src, dst_ref=dst, send_sem=self.send.at[i], recv_sem=self.recv.at[i],
+            device_id=device(flip(self.me, *to)), device_id_type=MESH,
+        )
+
+    def copy(self, kind, dz):
+        return {
+            "x": lambda: self.made("x", dz, (0, 0, 0, dz), (0, 1, 0, 0)),
+            "y": lambda: self.made("y", dz, (0, 0, 0, dz), (1, 0, 0, 0)),
+            "c": lambda: self.made("c", dz, (0, 0, 0, dz), (0, 0, 1, 0)),
+            "left": lambda: self.made("left", dz, (0, 1, 0, dz), (1, 0, 0, 0), self.left),
+            "right": lambda: self.made("right", dz, (1, 0, 0, dz), (0, 1, 0, 0), self.right),
+            "cx": lambda: self.made("cx", dz, (0, 1, 0, dz), (0, 0, 1, 0)),
+            "cy": lambda: self.made("cy", dz, (1, 0, 0, dz), (0, 0, 1, 0)),
+            "cl": lambda: self.made("cl", dz, (1, 1, 0, dz), (0, 0, 1, 0), self.left),
+            "cr": lambda: self.made("cr", dz, (1, 1, 0, dz), (0, 0, 1, 0), self.right),
+        }[kind]()
+
+    def along(self, dz, way):
+        i = self.kinds.index("z") * len(STEPS) + STEPS.index(dz - way)
+        at = slot(flip(self.me, 0, 0, 0, dz))
+        return pltpu.make_async_remote_copy(
+            src_ref=self.full.at[at] if dz else self.own, dst_ref=self.full.at[at],
+            send_sem=self.send.at[i], recv_sem=self.recv.at[i],
+            device_id=device(flip(self.me, 0, 0, 0, way)), device_id_type=MESH,
+        )
+
+    def sent_along(self):
+        for dz in STEPS:
+            for way in (-1, 1):
+                if dz * way <= 0 and abs(dz - way) < LINE:
+                    yield dz, way, on_line(self.me, way) & (True if dz == 0 else on_line(self.me, dz))
+
+    def each(self, act):
+        for dz in STEPS:
+            when(True if dz == 0 else on_line(self.me, dz), functools.partial(act, dz))
+
+    def start(self):
+        for dz, way, ok in self.sent_along():
+            if dz == 0:
+                when(ok, lambda dz=dz, way=way: self.along(dz, way).start())
+        self.spread(0)
+
+    def spread(self, dz):
+        for kind in ("x", "y", "c"):
+            self.copy(kind, dz).start()
+
+    def column(self, dz):
+        if dz == 0:
+            return
+        way = -1 if dz > 0 else 1
+        self.along_arrived(dz)
+        if abs(dz) < LINE - 1:
+            when(on_line(self.me, way), lambda: self.along(dz, way).start())
+        self.spread(dz)
+
+    def along_arrived(self, dz):
+        i = self.kinds.index("z") * len(STEPS) + STEPS.index(dz)
+        ref = self.full.at[slot(flip(self.me, 0, 0, 0, dz))]
+        pltpu.make_async_remote_copy(
+            src_ref=ref, dst_ref=ref, send_sem=self.send.at[i], recv_sem=self.recv.at[i],
+            device_id=device(flip(self.me, 0, 0, 0, 1 if dz > 0 else -1)), device_id_type=MESH,
+        ).wait_recv()
+
+    def corner(self, dz):
+        self.copy("x", dz).wait_recv()
+        self.copy("left", dz).start()
+        self.copy("cx", dz).start()
+        self.copy("y", dz).wait_recv()
+        self.copy("right", dz).start()
+        self.copy("cy", dz).start()
+
+    def last(self, dz):
+        self.copy("left", dz).wait_recv()
+        self.copy("cl", dz).start()
+        self.copy("right", dz).wait_recv()
+        self.copy("cr", dz).start()
+
+    def beat(self, t):
+        for lag, act in ((0, self.column), (LAG, self.corner), (2 * LAG, self.last)):
+            if 0 <= t - lag < len(STEPS):
+                dz = STEPS[t - lag]
+                when(True if dz == 0 else on_line(self.me, dz), functools.partial(act, dz))
+
+    beats = len(STEPS) + 2 * LAG
+
+    def finish(self):
+        def act(dz):
+            for kind in ("c", "cx", "cy", "cl", "cr"):
+                self.copy(kind, dz).wait_recv()
+            for kind in self.kinds[1:]:
+                self.copy(kind, dz).wait_send()
+
+        self.each(act)
+        for dz, way, ok in self.sent_along():
+            when(ok, lambda dz=dz, way=way: self.along(dz, way).wait_send())
+
+
+def gather_kernel(*refs):
+    n = (len(refs) - 3) // 2
+    owns, fulls = refs[:n], refs[n : 2 * n]
+    send, recv, here = refs[2 * n :]
+    me = place()
+    greet(me)
+    work = [Gatherer(me, owns[i], fulls[i], send.at[i], recv.at[i]) for i in range(n)]
+    for w in work:
+        w.start()
+    locals_ = [pltpu.make_async_copy(owns[i], fulls[i].at[slot(me)], here.at[i]) for i in range(n)]
+    for made in locals_:
+        made.start()
+    for t in range(Gatherer.beats):
+        for w in work:
+            w.beat(t)
+    for w in work:
+        w.finish()
+    for made in locals_:
+        made.wait()
+
+
+def gather(*shards):
+    n = len(shards)
+    return pl.pallas_call(
+        gather_kernel,
+        in_specs=[pl.BlockSpec(memory_space=pl.ANY)] * n,
+        out_specs=[pl.BlockSpec(memory_space=pl.ANY)] * n,
+        out_shape=[jax.ShapeDtypeStruct((32,) + s.shape, s.dtype) for s in shards],
+        scratch_shapes=[
+            pltpu.SemaphoreType.DMA((n, Gatherer.count)),
+            pltpu.SemaphoreType.DMA((n, Gatherer.count)),
+            pltpu.SemaphoreType.DMA((n,)),
+        ],
+        compiler_params=pltpu.CompilerParams(collective_id=0, has_side_effects=True),
+    )(*shards)
+
+
+def partner(at, dy, dx, dc, k):
+    return flip(at, dy, dx, dc, 0)[:3] + ({0: at[3], 1: at[3] + 1 - 2 * (at[3] % 2), 2: (at[3] + 2) % 4, 3: 3 - at[3]}[k],)
+
+
+def greet_all(me):
+    barrier = pltpu.get_barrier_semaphore()
+    others = [(0, 0, 1, 0), (0, 1, 0, 0), (1, 0, 0, 0), (0, 0, 0, 1), (0, 0, 0, 2), (0, 0, 0, 3)]
+    for other in others:
+        pl.semaphore_signal(barrier, inc=1, device_id=device(partner(me, *other)), device_id_type=MESH)
+    pl.semaphore_wait(barrier, len(others))
+
+
+BLOCKS = ((1, 1), (0, 1), (1, 0), (0, 0))
+
+
+class Scatterer:
+    count = 43
+
+    def __init__(self, me, part, out, mine, from_core, from_pair, from_far, from_line, send, recv, here):
+        self.me, self.part, self.out = me, part, out
+        self.mine, self.from_core, self.from_pair, self.from_far, self.from_line = (
+            mine, from_core, from_pair, from_far, from_line,
+        )
+        self.send, self.recv, self.here = send, recv, here
+        self.left, self.right = halves(part.shape[2])
+        self.copies = {}
+
+    def copy(self, name, src, dst, to):
+        i = len(self.copies)
+        made = pltpu.make_async_remote_copy(
+            src_ref=src, dst_ref=dst, send_sem=self.send.at[i], recv_sem=self.recv.at[i],
+            device_id=device(partner(self.me, *to)), device_id_type=MESH,
+        )
+        made.start()
+        self.copies[name] = made
+
+    def start(self):
+        self.locals = {}
+        for b, (dy, dx) in enumerate(BLOCKS):
+            for k in range(4):
+                other = slot(partner(self.me, dy, dx, 1, k))
+                self.copy(("core", b, k), self.part.at[other], self.from_core.at[b, k], (0, 0, 1, 0))
+                own = slot(partner(self.me, dy, dx, 0, k))
+                made = pltpu.make_async_copy(self.part.at[own], self.mine.at[b, k], self.here.at[b * 4 + k])
+                made.start()
+                self.locals[b, k] = made
+
+    def add(self, b, k, cols, others):
+        total = self.mine[b, k, :, cols].astype(f32)
+        for ref in others:
+            total += ref.astype(f32)
+        return total
+
+    def pair(self):
+        for b, (dy, dx) in enumerate(BLOCKS):
+            for k in range(4):
+                self.locals[b, k].wait()
+                self.copies["core", b, k].wait_recv()
+                self.mine[b, k] = (self.mine[b, k].astype(f32) + self.from_core[b, k].astype(f32)).astype(bf16)
+                if dx:
+                    self.copy(
+                        ("x", b, k), self.mine.at[b, k, :, self.left], self.from_pair.at[b, k, :, self.left],
+                        (0, 1, 0, 0),
+                    )
+                if dy:
+                    self.copy(
+                        ("y", b, k), self.mine.at[b, k, :, self.right], self.from_pair.at[b // 2, k, :, self.right],
+                        (1, 0, 0, 0),
+                    )
+
+    def far(self):
+        for k in range(4):
+            self.copies["x", 0, k].wait_recv()
+            self.mine[2, k, :, self.left] = self.add(
+                2, k, self.left, [self.from_pair[0, k, :, self.left]]
+            ).astype(bf16)
+            self.copy(("fy", k), self.mine.at[2, k, :, self.left], self.from_far.at[k, :, self.left], (1, 0, 0, 0))
+            self.copies["y", 0, k].wait_recv()
+            self.mine[1, k, :, self.right] = self.add(
+                1, k, self.right, [self.from_pair[0, k, :, self.right]]
+            ).astype(bf16)
+            self.copy(("fx", k), self.mine.at[1, k, :, self.right], self.from_far.at[k, :, self.right], (0, 1, 0, 0))
+
+    def line(self):
+        for k in (1, 2, 3, 0):
+            for name in (("x", 1, k), ("y", 2, k), ("fy", k), ("fx", k)):
+                self.copies[name].wait_recv()
+            if k:
+                self.mine[3, k] = self.add(3, k, slice(None), [self.from_pair[1, k], self.from_far[k]]).astype(bf16)
+                self.copy(("z", k), self.mine.at[3, k], self.from_line.at[k - 1], (0, 0, 0, k))
+
+    def finish(self):
+        for k in (1, 2, 3):
+            self.copies["z", k].wait_recv()
+        self.out[...] = self.add(
+            3, 0, slice(None),
+            [self.from_pair[1, 0], self.from_far[0], self.from_line[0], self.from_line[1], self.from_line[2]],
+        )
+        for made in self.copies.values():
+            made.wait_send()
+
+
+def scatter_scratch(rows, width):
+    vmem = lambda *lead: pltpu.VMEM(lead + (rows, width), bf16)
+    return [
+        vmem(4, 4), vmem(4, 4), vmem(2, 4), vmem(4), vmem(3),
+        pltpu.SemaphoreType.DMA((Scatterer.count,)), pltpu.SemaphoreType.DMA((Scatterer.count,)),
+        pltpu.SemaphoreType.DMA((16,)),
+    ]
+
+
+class Summer:
+    def __init__(self, me, own, out, held, send, recv):
+        self.me, self.own, self.out, self.held, self.send, self.recv = me, own, out, held, send, recv
+        self.copies = []
+
+    def copy(self, src, dst, to):
+        i = len(self.copies)
+        made = pltpu.make_async_remote_copy(
+            src_ref=src, dst_ref=dst, send_sem=self.send.at[i], recv_sem=self.recv.at[i],
+            device_id=device(partner(self.me, *to)), device_id_type=MESH,
+        )
+        made.start()
+        self.copies.append(made)
+
+    def start(self):
+        self.copy(self.own, self.held.at[0], (0, 0, 1, 0))
+
+    def second(self):
+        self.copies[0].wait_recv()
+        self.out[...] = self.own[...] + self.held[0]
+        self.held[6] = self.out[...]
+        self.copy(self.held.at[6], self.held.at[1], (0, 1, 0, 0))
+
+    def third(self):
+        self.copies[1].wait_recv()
+        self.held[7] = self.held[6] + self.held[1]
+        self.copy(self.held.at[7], self.held.at[2], (1, 0, 0, 0))
+
+    def fourth(self):
+        self.copies[2].wait_recv()
+        self.held[8] = self.held[7] + self.held[2]
+        for k in (1, 2, 3):
+            self.copy(self.held.at[8], self.held.at[2 + k], (0, 0, 0, k))
+
+    def finish(self):
+        for made in self.copies[3:]:
+            made.wait_recv()
+        self.out[...] = (self.held[8] + self.held[3]) + (self.held[4] + self.held[5])
+        for made in self.copies:
+            made.wait_send()
+
+
+def scatter_kernel(n, *refs):
+    parts, small = refs[:n], refs[n]
+    outs, small_out = refs[n + 1 : 2 * n + 1], refs[2 * n + 1]
+    scratch = refs[2 * n + 2 :]
+    me = place()
+    greet_all(me)
+    work = [Scatterer(me, parts[i], outs[i], *scratch[8 * i : 8 * i + 8]) for i in range(n)]
+    tiny = Summer(me, small, small_out, *scratch[8 * n :])
+    tiny.start()
+    for w in work:
+        w.start()
+    tiny.second()
+    for w in work:
+        w.pair()
+    tiny.third()
+    for w in work:
+        w.far()
+    tiny.fourth()
+    for w in work:
+        w.line()
+    for w in work:
+        w.finish()
+    tiny.finish()
+
+
+def scatter(parts, small):
+    n = len(parts)
+    scratch = []
+    for p in parts:
+        scratch += scatter_scratch(p.shape[1], p.shape[2])
+    scratch += [
+        pltpu.VMEM((9,) + small.shape, f32), pltpu.SemaphoreType.DMA((6,)), pltpu.SemaphoreType.DMA((6,)),
+    ]
+    vmem = pl.BlockSpec(memory_space=pltpu.VMEM)
+    return pl.pallas_call(
+        functools.partial(scatter_kernel, n),
+        in_specs=[pl.BlockSpec(memory_space=pl.ANY)] * n + [vmem],
+        out_specs=[vmem] * (n + 1),
+        out_shape=[jax.ShapeDtypeStruct(p.shape[1:], f32) for p in parts]
+        + [jax.ShapeDtypeStruct(small.shape, f32)],
+        scratch_shapes=scratch,
+        compiler_params=pltpu.CompilerParams(
+            collective_id=2, has_side_effects=True, vmem_limit_bytes=60 * 1024 * 1024
+        ),
+    )(*parts, small)
+
+
+def reaches(here, number):
+    return dict(collective_id=number, has_side_effects=True) if here else {}
+
+
+BEATS = (0, 2, 4, 5, 7, 8, 9, 10, 11)
+
+
 def front_kernel(
-    sizes,
-    tok_ref, halo_ref, gain_ref, w_ref, cw_ref, cb_ref, dtb_ref, rate_ref, aux_ref, x2_ref,
-    normed_ref, gate_ref, conv_ref, act_ref, low_ref, dsil_ref, dt_ref, cum_ref, dtraw_ref, sb_ref,
-    ext_ref, state_ref,
+    sizes, here,
+    tok_ref, halo_ref, gain_ref, w_ref, cw_ref, cb_ref, dtb_ref, rate_ref, aux_ref, x2_ref, own_ref,
+    normed_ref, conv_ref, act_ref, low_ref, dsil_ref, dt_ref, cum_ref, dtraw_ref, sb_ref, full_ref,
+    ext_ref, state_ref, send_ref, recv_ref, copy_ref,
 ):
     inner, channels, heads, state = sizes
     step = pl.program_id(0)
+    if here:
+        me = place()
+        others = Gatherer(me, own_ref, full_ref, send_ref, recv_ref)
+        mine = pltpu.make_async_copy(own_ref, full_ref.at[slot(me)], copy_ref)
+
+        @pl.when(step == 0)
+        def _():
+            greet(me)
+            others.start()
+            mine.start()
 
     @pl.when(step == 0)
     def _():
@@ -77,15 +502,14 @@
     normed = norm(tok_ref[...])
     normed_ref[...] = normed
     both = jnp.concatenate([norm(halo_ref[...]), normed], axis=0)
-    gate_ref[...] = nn(normed, w_ref[:, :inner])
-    dt_raw = nn(normed, w_ref[:, inner + channels :])
+    dt_raw = nn(normed, w_ref[:, channels : channels + 2 * heads])
     dtraw_ref[...] = dt_raw
     aux = aux_ref[...]
     m1, m2, m3 = aux[:, 0:1], aux[:, 1:2], aux[:, 2:3]
     block = 256
     for at in range(0, channels, block):
         sl = slice(at, at + block)
-        ext_ref[:, sl] = nn(both, w_ref[:, inner + at : inner + at + block])
+        ext_ref[:, sl] = nn(both, w_ref[:, at : at + block])
         x0 = ext_ref[HALO : HALO + Q, sl]
         conv_ref[:, sl] = x0
         pre = cb_ref[:, sl] + cw_ref[0:1, sl] * x0
@@ -114,13 +538,24 @@
         wide = nn(scales, x2_ref[:, sl])
         vs = (low_ref[:, sl].astype(f32) * wide[:Q]).astype(bf16)
         state_ref[:, sl] = state_ref[:, sl] * wide[Q : Q + 1] + tn(b_bwd, vs)
-
-
-def front(tokens, gain_row, w_in, conv_w, conv_b, dt_bias, rate_row, aux, x2, sizes):
+    if here:
+        steps = len(BEATS) - 1
+        for i in range(steps):
+
+            @pl.when(step == i)
+            def _():
+                for t in range(BEATS[i], BEATS[i + 1]):
+                    others.beat(t)
+                if i == steps - 1:
+                    others.finish()
+                    mine.wait()
+
+
+def front(tokens, gain_row, w_in, conv_w, conv_b, dt_bias, rate_row, aux, x2, own, sizes, here):
     inner, channels, heads, state = sizes
     t, d = tokens.shape
     n = t // Q
-    proj = w_in.shape[1]
+    rows = own.shape[0]
     rev = lambda i: (n - 1 - i, 0)
     fixed = lambda i: (0, 0)
     blk = lambda width: pl.BlockSpec((Q, width), rev)
@@ -128,39 +563,47 @@
     per = Q // HALO
     out = lambda width, dtype: jax.ShapeDtypeStruct((t, width), dtype)
     return pl.pallas_call(
-        functools.partial(front_kernel, sizes),
+        functools.partial(front_kernel, sizes, here),
         grid=(n,),
         in_specs=[
             blk(d),
             pl.BlockSpec((HALO, d), lambda i: (jnp.maximum((n - 1 - i) * per - 1, 0), 0)),
             whole(gain_row), whole(w_in), whole(conv_w), whole(conv_b), whole(dt_bias), whole(rate_row),
-            blk(aux.shape[1]), whole(x2),
+            blk(aux.shape[1]), whole(x2), pl.BlockSpec(memory_space=pl.ANY),
         ],
         out_specs=[
-            blk(d), blk(inner), blk(channels), blk(channels), blk(channels), blk(channels),
+            blk(d), blk(channels), blk(channels), blk(channels), blk(channels),
             blk(2 * heads), blk(2 * heads), blk(2 * heads),
             pl.BlockSpec((1, state, inner), lambda i: (n - 1 - i, 0, 0)),
+            pl.BlockSpec(memory_space=pl.ANY),
         ],
         out_shape=[
-            out(d, bf16), out(inner, f32), out(channels, f32), out(channels, f32), out(channels, bf16), out(channels, f32),
+            out(d, bf16), out(channels, f32), out(channels, f32), out(channels, bf16), out(channels, f32),
             out(2 * heads, f32), out(2 * heads, f32), out(2 * heads, f32),
             jax.ShapeDtypeStruct((n, state, inner), bf16),
-        ],
-        scratch_shapes=[pltpu.VMEM((HALO + Q, channels), f32), pltpu.VMEM((state, inner), f32)],
+            jax.ShapeDtypeStruct((32 if here else 1,) + own.shape, bf16),
+        ],
+        scratch_shapes=[
+            pltpu.VMEM((HALO + Q, channels), f32),
+            pltpu.VMEM((state, inner), f32),
+            pltpu.SemaphoreType.DMA((Gatherer.count,)),
+            pltpu.SemaphoreType.DMA((Gatherer.count,)),
+            pltpu.SemaphoreType.DMA,
+        ],
         compiler_params=pltpu.CompilerParams(
-            dimension_semantics=("arbitrary",), vmem_limit_bytes=60 * 1024 * 1024
+            dimension_semantics=("arbitrary",), vmem_limit_bytes=60 * 1024 * 1024, **reaches(here, 1)
         ),
-        cost_estimate=pl.CostEstimate(flops=2 * t * d * proj, bytes_accessed=50_000_000, transcendentals=0),
-    )(tokens, tokens, gain_row, w_in, conv_w, conv_b, dt_bias, rate_row, aux, x2)
+        cost_estimate=pl.CostEstimate(flops=5_000_000_000, bytes_accessed=50_000_000, transcendentals=0),
+    )(tokens, tokens, gain_row, w_in, conv_w, conv_b, dt_bias, rate_row, aux, x2, own)
 
 
 def middle_kernel(
     sizes,
-    tok_ref, act_ref, gate_ref, dt_ref, cum_ref, aux_ref, segrow_ref, cot_ref, sb_ref, w_ref,
+    tok_ref, act_ref, normed_ref, dt_ref, cum_ref, aux_ref, segrow_ref, cot_ref, sb_ref, w_ref,
     rate_ref, skip_ref, og_ref, x2_ref, r_ref,
     out_ref, nout_ref, dgate_ref, dy_ref, dv_ref, dbc_ref, drate_ref, dq_ref, sf_ref, dog_ref, dsk_ref,
     decay_ref, mix_ref, state_ref, adj_ref, ssm_ref, gated_ref, dno_ref, yf_ref, yb_ref, wide_ref,
-    p_ref, q_ref, scal_ref,
+    p_ref, q_ref, scal_ref, gate_ref,
 ):
     inner, channels, heads, state = sizes
     quad = 256
@@ -247,10 +690,11 @@
             )
         ssm = jnp.concatenate(parts, axis=1) + yf + yb + skip_ref[:, sl] * v
         ssm_ref[:, sl] = ssm
-        gate = gate_ref[:, sl]
+        gate = nn(normed_ref[...], w_ref[:, sl])
+        gate_ref[:, sl] = gate
         gated = ssm * (gate / (1.0 + jnp.exp(-gate)))
         gated_ref[:, sl] = gated
-        dno = nn(cot, w_ref[:, sl])
+        dno = nn(cot, w_ref[:, inner + at : inner + at + quad])
         dno_ref[:, sl] = dno
         squares += gated * gated
         dots += dno * og_ref[:, sl] * gated
@@ -325,7 +769,7 @@
         adj_ref[:, sl] = adj * across_b + tn(c_b, dye_b)
         state_ref[:, sl] = state_ref[:, sl] * wide_ref[4 * Q : 4 * Q + 1, sl] + tn(b_f, vs_f)
 
-    out_ref[...] = (tok_ref[...].astype(f32) + nt(nout_ref[...], w_ref[...])).astype(bf16)
+    out_ref[...] = (tok_ref[...].astype(f32) + nt(nout_ref[...], w_ref[:, inner:])).astype(bf16)
     dg = jnp.where(same & (col != row), dg, 0.0)
     dg_f = jnp.where(lower, dg, 0.0)
     dg_b = (dg - dg_f).astype(bf16)
@@ -348,7 +792,7 @@
     dq_ref[...] = jnp.concatenate([q_cols[:, :heads], q_cols[:, heads:] + dots_v], axis=1)
 
 
-def middle(tokens, act, gate, dt, cum, aux, segrow, cot, sb, w_out_t, rate_row, skip_row, og_row, x2, r, sizes):
+def middle(tokens, act, normed, dt, cum, aux, segrow, cot, sb, w_side, rate_row, skip_row, og_row, x2, r, sizes):
     inner, channels, heads, state = sizes
     t, d = tokens.shape
     n = t // Q
@@ -363,9 +807,9 @@
         functools.partial(middle_kernel, sizes),
         grid=(n,),
         in_specs=[
-            blk(d), blk(channels), blk(inner), blk(2 * heads), blk(2 * heads), blk(aux.shape[1]),
+            blk(d), blk(channels), blk(d), blk(2 * heads), blk(2 * heads), blk(aux.shape[1]),
             pl.BlockSpec((1, 1, Q), cube), blk(d), pl.BlockSpec((1, state, inner), cube),
-            whole(w_out_t), whole(rate_row), whole(skip_row), whole(og_row), whole(x2), whole(r),
+            whole(w_side), whole(rate_row), whole(skip_row), whole(og_row), whole(x2), whole(r),
         ],
         out_specs=[
             blk(d), blk(inner), blk(inner), blk(inner), blk(inner), blk(4 * state),
@@ -391,20 +835,21 @@
             pltpu.VMEM((Q, Q), f32),
             pltpu.VMEM((Q, Q), f32),
             pltpu.VMEM((1, inner), f32),
+            pltpu.VMEM((Q, inner), f32),
         ],
         compiler_params=pltpu.CompilerParams(
             dimension_semantics=("arbitrary",), vmem_limit_bytes=60 * 1024 * 1024
         ),
         cost_estimate=pl.CostEstimate(flops=30_000_000_000, bytes_accessed=60_000_000, transcendentals=0),
-    )(tokens, act, gate, dt, cum, aux, segrow, cot, sb, w_out_t, rate_row, skip_row, og_row, x2, r)
+    )(tokens, act, normed, dt, cum, aux, segrow, cot, sb, w_side, rate_row, skip_row, og_row, x2, r)
 
 
 def back_kernel(
     sizes,
-    tok_ref, cot_ref, gain_ref, w_ref, cw_ref, dtb_ref, rate_ref, aux_ref, x2_ref, r_ref,
+    tok_ref, cot_ref, gain_ref, w_ref, side_ref, cw_ref, dtb_ref, rate_ref, aux_ref, x2_ref, r_ref,
     low_ref, dsil_ref, conv_ref, dt_ref, cum_ref, dtraw_ref,
-    dgate_ref, dy_ref, dv_ref, dbc_ref, drate_ref, dq_ref, sf_ref,
-    dproj_ref, dtok_ref, dgain_ref, dcw_ref, dcb_ref, ddtb_ref, dalog_ref,
+    dgate_ref, dy_ref, dv_ref, dbc_ref, drate_ref, dq_ref, sf_ref, dog_ref, dsk_ref,
+    dproj_ref, dtok_ref, small_ref,
     adj_ref, dpre_ref, scal_ref,
 ):
     inner, channels, heads, state = sizes
@@ -415,11 +860,12 @@
     def _():
         adj_ref[...] = jnp.zeros_like(adj_ref)
         dpre_ref[...] = jnp.zeros_like(dpre_ref)
-        dgain_ref[...] = jnp.zeros_like(dgain_ref)
-        dcw_ref[...] = jnp.zeros_like(dcw_ref)
-        dcb_ref[...] = jnp.zeros_like(dcb_ref)
-        ddtb_ref[...] = jnp.zeros_like(ddtb_ref)
-        dalog_ref[...] = jnp.zeros_like(dalog_ref)
+        small_ref[...] = jnp.zeros_like(small_ref)
+        small_ref[5:6, :inner] = dog_ref[...]
+        skips = nn(split_rows(jnp.broadcast_to(dsk_ref[...], (8, inner))), r_ref[...])
+        small_ref[6:7, SKIP_AT : SKIP_AT + Q] = skips[0:1] + skips[8:9]
+
+    d = tok_ref.shape[1]
 
     dpre_ref[Q:, :] = dpre_ref[0:8, :]
     aux = aux_ref[...]
@@ -464,12 +910,12 @@
         sl = slice(at, at + quad)
         conv = conv_ref[:, sl]
         z = dpre_ref[:Q, sl]
-        dcb_ref[:, sl] += jnp.sum(z, axis=0, keepdims=True)
-        dcw_ref[0:1, sl] += jnp.sum(z * conv, axis=0, keepdims=True)
+        small_ref[4:5, sl] += jnp.sum(z, axis=0, keepdims=True)
+        small_ref[0:1, sl] += jnp.sum(z * conv, axis=0, keepdims=True)
         total = cw_ref[0:1, sl] * z
         for k, mask in ((1, n1), (2, n2), (3, n3)):
             z = dpre_ref[k : Q + k, sl] * mask
-            dcw_ref[k : k + 1, sl] += jnp.sum(z * conv, axis=0, keepdims=True)
+            small_ref[k : k + 1, sl] += jnp.sum(z * conv, axis=0, keepdims=True)
             total += cw_ref[k : k + 1, sl] * z
         dproj_ref[:, inner + at : inner + at + quad] = total.astype(bf16)
     dproj_ref[:, :inner] = dgate_ref[...]
@@ -486,49 +932,50 @@
     a = rate_ref[...]
     v = dtraw_ref[...] + dtb_ref[...]
     d_v = (d_dt - d_rate * a) / (1.0 + jnp.exp(-v))
-    ddtb_ref[...] += jnp.sum(d_v, axis=0, keepdims=True)
-    dalog_ref[...] += jnp.sum(d_rate * (-dt * a), axis=0, keepdims=True)
+    small_ref[6:7, BIAS_AT : BIAS_AT + 2 * heads] += jnp.sum(d_v, axis=0, keepdims=True)
+    small_ref[6:7, LOG_AT : LOG_AT + 2 * heads] += jnp.sum(d_rate * (-dt * a), axis=0, keepdims=True)
     dproj_ref[:, inner + channels :] = d_v.astype(bf16)
 
     d_normed = (
-        nt(dproj_ref[:, :inner], w_ref[:, :inner])
-        + nt(dproj_ref[:, inner : inner + channels], w_ref[:, inner : inner + channels])
-        + nt(dproj_ref[:, inner + channels :], w_ref[:, inner + channels :])
+        nt(dproj_ref[:, :inner], side_ref[:, :inner])
+        + nt(dproj_ref[:, inner : inner + channels], w_ref[:, :channels])
+        + nt(dproj_ref[:, inner + channels :], w_ref[:, channels : channels + 2 * heads])
     )
     x = tok_ref[...].astype(f32)
     inv = lax.rsqrt(jnp.mean(x * x, axis=1, keepdims=True) + eps)
     unit = x * inv
-    dgain_ref[...] += jnp.sum(d_normed * unit, axis=0, keepdims=True)
+    small_ref[6:7, :d] += jnp.sum(d_normed * unit, axis=0, keepdims=True)
     a = d_normed * gain_ref[...]
     dtok_ref[...] = cot_ref[...].astype(f32) + inv * (a - unit * jnp.mean(a * unit, axis=1, keepdims=True))
 
 
 def back(
-    tokens, cot, gain_row, w_in, conv_w, dt_bias, rate_row, aux, x2, r, low, dsil, conv, dt, cum, dtraw,
-    dgate, dy, dv, dbc, drate, dq, sf, sizes,
+    tokens, cot, gain_row, w_in, w_side, conv_w, dt_bias, rate_row, aux, x2, r, low, dsil, conv, dt, cum, dtraw,
+    dgate, dy, dv, dbc, drate, dq, sf, dog, dsk, sizes,
 ):
     inner, channels, heads, state = sizes
     t, d = tokens.shape
     n = t // Q
-    proj = w_in.shape[1]
+    proj = inner + channels + 2 * heads
     rev = lambda i: (n - 1 - i, 0)
     fixed = lambda i: (0, 0)
     blk = lambda a: pl.BlockSpec((Q, a.shape[1]), rev)
     whole = lambda a: pl.BlockSpec(a.shape, fixed)
-    lines = [(1, d), (conv_w.shape[0], channels), (1, channels), (1, 2 * heads), (1, 2 * heads)]
     return pl.pallas_call(
         functools.partial(back_kernel, sizes),
         grid=(n,),
         in_specs=[
-            blk(tokens), blk(cot), whole(gain_row), whole(w_in), whole(conv_w), whole(dt_bias), whole(rate_row),
+            blk(tokens), blk(cot), whole(gain_row), whole(w_in), pl.BlockSpec((w_side.shape[0], inner), fixed), whole(conv_w), whole(dt_bias), whole(rate_row),
             blk(aux), whole(x2), whole(r), blk(low), blk(dsil), blk(conv), blk(dt), blk(cum), blk(dtraw),
             blk(dgate), blk(dy), blk(dv), blk(dbc), blk(drate), blk(dq),
-            pl.BlockSpec((1, state, inner), lambda i: (n - 1 - i, 0, 0)),
-        ],
-        out_specs=[pl.BlockSpec((Q, proj), rev), pl.BlockSpec((Q, d), rev)]
-        + [pl.BlockSpec(s, fixed) for s in lines],
-        out_shape=[jax.ShapeDtypeStruct((t, proj), bf16), jax.ShapeDtypeStruct((t, d), f32)]
-        + [jax.ShapeDtypeStruct(s, f32) for s in lines],
+            pl.BlockSpec((1, state, inner), lambda i: (n - 1 - i, 0, 0)), whole(dog), whole(dsk),
+        ],
+        out_specs=[pl.BlockSpec((Q, proj), rev), pl.BlockSpec((Q, d), rev), pl.BlockSpec((8, channels), fixed)],
+        out_shape=[
+            jax.ShapeDtypeStruct((t, proj), bf16),
+            jax.ShapeDtypeStruct((t, d), f32),
+            jax.ShapeDtypeStruct((8, channels), f32),
+        ],
         scratch_shapes=[
             pltpu.VMEM((state, inner), f32),
             pltpu.VMEM((Q + 8, channels), f32),
@@ -539,8 +986,8 @@
         ),
         cost_estimate=pl.CostEstimate(flops=20_000_000_000, bytes_accessed=60_000_000, transcendentals=0),
     )(
-        tokens, cot, gain_row, w_in, conv_w, dt_bias, rate_row, aux, x2, r, low, dsil, conv, dt, cum, dtraw,
-        dgate, dy, dv, dbc, drate, dq, sf,
+        tokens, cot, gain_row, w_in, w_side, conv_w, dt_bias, rate_row, aux, x2, r, low, dsil, conv, dt, cum, dtraw,
+        dgate, dy, dv, dbc, drate, dq, sf, dog, dsk,
     )
 
 
@@ -565,7 +1012,7 @@
     return aux, chunks.reshape(n, 1, Q)
 
 
-def local(tokens, segment_ids, w_in, w_out_t, gain, conv_w, conv_b, dt_bias, a_log, d_skip, out_gain, cotangent):
+def local(here, tokens, segment_ids, w_in, own_side, gain, conv_w, conv_b, dt_bias, a_log, d_skip, out_gain, cotangent):
     heads = d_skip.shape[0]
     inner = out_gain.shape[0]
     channels = conv_w.shape[1]
@@ -580,42 +1027,65 @@
     rate_row = jnp.exp(a_log)[None, :]
     dtb_row = dt_bias[None, :]
     skip_row = jnp.repeat(d_skip, width)[None, :]
-    normed, gate, conv, act, low, dsil, dt, cum, dtraw, sb = front(
-        tokens, gain_row, w_in, conv_w, conv_b[None, :], dtb_row, rate_row, aux, x2, sizes
-    )
+    normed, conv, act, low, dsil, dt, cum, dtraw, sb, w_side = front(
+        tokens, gain_row, w_in, conv_w, conv_b[None, :], dtb_row, rate_row, aux, x2, own_side, sizes, here
+    )
+    if not here:
+        w_side = lax.all_gather(own_side, AXES)
+    w_side = w_side.reshape(-1, 2 * inner)
     output, nout, dgate, dy, dv, dbc, drate, dq, sf, d_og, d_sk = middle(
-        tokens, act, gate, dt, cum, aux, segrow, cotangent, sb, w_out_t, rate_row, skip_row,
+        tokens, act, normed, dt, cum, aux, segrow, cotangent, sb, w_side, rate_row, skip_row,
         out_gain[None, :], x2, r, sizes,
     )
-    d_w_out_t = tn(cotangent, nout)
-    dproj, d_tokens, d_gain, d_cw, d_cb, d_dtb, d_alog = back(
-        tokens, cotangent, gain_row, w_in, conv_w, dtb_row, rate_row, aux, x2, r, low, dsil, conv, dt, cum, dtraw,
-        dgate, dy, dv, dbc, drate, dq, sf, sizes,
-    )
-    d_w_in = tn(normed, dproj)
-    d_sk = jnp.sum(d_sk.reshape(heads, width), axis=1)
-    return output, d_tokens, d_w_in, d_w_out_t, d_gain[0], (d_cw, d_cb[0], d_dtb[0], d_alog[0], d_sk, d_og[0])
-
-
-def body(tokens, segment_ids, w_in, w_out, norm_gain, conv_w, conv_b, dt_bias, a_log, d_skip, out_gain, cotangent):
-    full_in = lax.all_gather(w_in, AXES, axis=0, tiled=True)
-    full_out_t = lax.all_gather(w_out.T, AXES, axis=0, tiled=True)
-    full_gain = lax.all_gather(norm_gain, AXES, axis=0, tiled=True)
-    output, d_tokens, g_in, g_out_t, g_gain, small = local(
-        tokens, segment_ids, full_in, full_out_t, full_gain, conv_w, conv_b, dt_bias, a_log, d_skip, out_gain,
-        cotangent,
-    )
-    d_w_in = lax.psum_scatter(g_in, AXES, scatter_dimension=0, tiled=True)
-    d_w_out = lax.psum_scatter(g_out_t, AXES, scatter_dimension=0, tiled=True).T
-    d_gain = lax.psum_scatter(g_gain, AXES, scatter_dimension=0, tiled=True)
-    small = lax.psum(small, AXES)
-    return (output, d_tokens, d_w_in, d_w_out, d_gain) + tuple(small)
+    d_w_out_t = tn(cotangent, nout).astype(bf16)
+    dproj, d_tokens, small = back(
+        tokens, cotangent, gain_row, w_in, w_side, conv_w, dtb_row, rate_row, aux, x2, r, low, dsil, conv, dt, cum, dtraw,
+        dgate, dy, dv, dbc, drate, dq, sf, d_og, d_sk, sizes,
+    )
+    d_w_in = tn(normed, dproj).astype(bf16)
+    return output, d_tokens, d_w_in, d_w_out_t, small
+
+
+def unpack(small, taps, inner, heads, d):
+    return small[6, :d], (
+        small[:taps],
+        small[taps],
+        small[6, BIAS_AT : BIAS_AT + 2 * heads],
+        small[6, LOG_AT : LOG_AT + 2 * heads],
+        small[6, SKIP_AT : SKIP_AT + heads],
+        small[5, :inner],
+    )
+
+
+def body(here, tokens, segment_ids, w_in, w_out, norm_gain, conv_w, conv_b, dt_bias, a_log, d_skip, out_gain, cotangent):
+    rows, proj = w_in.shape
+    d, inner, heads = tokens.shape[1], out_gain.shape[0], d_skip.shape[0]
+    parts = d // rows
+    own_first = jnp.concatenate([w_in[:, inner:], norm_gain[:, None]], axis=1)
+    own_side = jnp.concatenate([w_in[:, :inner], w_out.T], axis=1)
+    first = gather(own_first)[0] if here else lax.all_gather(own_first, AXES)
+    first = first.reshape(d, proj - inner + 1)
+    output, d_tokens, g_in, g_out_t, small = local(
+        here, tokens, segment_ids, first, own_side, first[:, proj - inner], conv_w, conv_b, dt_bias, a_log, d_skip,
+        out_gain, cotangent,
+    )
+    g_in, g_out_t = g_in.reshape(parts, rows, proj), g_out_t.reshape(parts, rows, inner)
+    if here:
+        d_w_in, d_w_out, small = scatter([g_in, g_out_t], small)
+    else:
+        d_w_in = lax.psum_scatter(g_in.astype(f32), AXES, scatter_dimension=0)
+        d_w_out = lax.psum_scatter(g_out_t.astype(f32), AXES, scatter_dimension=0)
+        small = lax.psum(small, AXES)
+    d_gain, small = unpack(small, conv_w.shape[0], inner, heads, d)
+    d_gain = lax.dynamic_slice_in_dim(d_gain, lax.axis_index(AXES) * rows, rows)
+    return (output, d_tokens, d_w_in, d_w_out.T, d_gain) + small
 
 
 def solution(mesh):
     rows, cols, line, none = P(AXES, None), P(None, AXES), P(AXES), P()
+    here = dict(mesh.shape) == {"fsdp": 8, "rep": 4}
     return jax.shard_map(
-        body,
+        functools.partial(body, here),
         mesh=mesh,
         in_specs=(rows, line, rows, cols, line, none, none, none, none, none, none, rows),
         out_specs=(rows, rows, rows, cols, line, none, none, none, none, none, none),

time: 460 us -> 262 us (0.57)
  waiting for transfers between devices: 217 us -> 0 us
  Pallas kernels: 111 us -> 212 us
  blocking collectives: 82.2 us -> 0 us
  between operations: 13.9 us -> 0.77 us
  local copies, waits for them, and re-layouts: 15.7 us -> 25.7 us
    unnamed x6 -> x0, waiting for transfers between devices: 163 us -> none
    pallas_call x1 -> x3, Pallas kernels: 24.1 us -> 122 us  [the longest x1 59.1 us: scatter(): pl.pallas_call(functools.partial(scatter_kernel, n), in_specs=[pl.BlockSp...]
    unnamed x2 -> x0, blocking collectives: 82.2 us -> none
    all_gather x2 -> x0, waiting for transfers between devices: 53.4 us -> none  [the longest x1 34.9 us: body(): full_out_t = lax.all_gather(w_out.T, AXES, axis=0, tiled=True)]
    convert_element_type x0 -> x2, local copies, waits for them, and re-layouts: none -> 8.5 us  [the longest x1 7.91 us: local(): d_w_in = tn(normed, dproj).astype(bf16)]
    slice x0 -> x7, local copies, waits for them, and re-layouts: none -> 5.93 us  [the longest x1 1.44 us: unpack(): small[taps]]
    unnamed x24 -> x18, local copies, waits for them, and re-layouts: 8.14 us -> 3.33 us
  transfers between devices with their start and end apart: 4 -> 0, of which waited for: 4 -> 0; matrix products, arithmetic and copies ran while one was open for 5% -> 0% of each run, Pallas kernels for 14% -> 0%
where the time goes in v3:
time: 262 us; the launch traced here: 261 us
  Pallas kernels  212 us (81%)
  local copies, waits for them, and re-layouts  25.7 us (10%)
  matrix products  18.9 us (7%)
  other arithmetic  4.14 us (2%)
    pallas_call x1, Pallas kernels, scatter(): pl.pallas_call(functools.partial(scatter_kernel, n), in_specs=[pl.BlockSp...  59.1 us
    pallas_call x1, Pallas kernels, middle(): pl.pallas_call(functools.partial(middle_kernel, sizes), grid=(n,), in_spe...  49.2 us
    pallas_call x1, Pallas kernels, back(): pl.pallas_call(functools.partial(back_kernel, sizes), grid=(n,), in_specs...  40.6 us
    pallas_call x1, Pallas kernels, front(): pl.pallas_call(functools.partial(front_kernel, sizes, here), grid=(n,), i...  36.1 us
    pallas_call x1, Pallas kernels, gather(): pl.pallas_call(gather_kernel, in_specs=[pl.BlockSpec(memory_space=pl.ANY)...  26.7 us
    dot_general x2, matrix products, tn(): lax.dot_general(a, b, (((0,), (0,)), ((), ())), preferred_element_type=f32)  18.9 us
    convert_element_type x1, local copies, waits for them, and re-layouts, local(): d_w_in = tn(normed, dproj).astype(bf16)  7.91 us

profile of v3, /device:TPU:0, one launch (start us, length us, event | category | flops | bytes accessed | tf_op | source)
XLA Modules:
  0.0 261.3 jit_solution(15573483155764387141)
XLA Ops:
  0.7 0.8 convert_bitcast_fusion
  2.2 0.8 fusion.3
  3.0 1.0 copy.56.aux_ref
  4.1 0.9 slice.62
  5.0 0.7 copy.53
  5.7 0.7 pad_maximum_fusion.1.refs_0_
  6.4 26.7 %shard_map.221 = bf16[32,24,1841]{2,1,0:T(8,128)(2,1)} custom-call(bf16[24,1841]{1,0:T(8,128)(2,1)} %pad_maximum_fusion.1.refs_0_), custom_call_target="tpu_custom_call" | custom-call | tf_op jit(solution)/shard_map/pallas_call | solution.py:251
  33.2 1.1 convert_reduce_fusion
  36.7 36.1 %shard_map.222 = (bf16[1024,768]{1,0:T(8,128)(2,1)}, f32[1024,1792]{1,0:T(8,128)}, f32[1024,1792]{1,0:T(8,128)}, bf16[1024,1792]{1,0:T(8,128)(2,1)}, f32[1024,17...) custom-call(bf16[1024,768]{1,0:T(8,128)(2,1)} %tok_ref.5, ...), custom_call_target="tpu_custom_call" | custom-call | flops 5000000000 | bytes 50000000 | tf_op jit(solution)/shard_map/pallas_call | solution.py:565
  73.0 0.7 broadcast_in_dim_reshape.3.skip_ref
  74.2 49.2 %shard_map.223 = (bf16[1024,768]{1,0:T(8,128)(2,1)}, bf16[1024,1536]{1,0:T(8,128)(2,1)}, bf16[1024,1536]{1,0:T(8,128)(2,1)}, bf16[1024,1536]{1,0:T(8,128)(2,1)},...) custom-call(bf16[1024,768]{1,0:T(8,128)(2,1)} %tok_ref.5, ...), custom_call_target="tpu_custom_call" | custom-call | flops 30000001024 | bytes 60000000 | tf_op jit(solution)/shard_map/pallas_call | solution.py:806
  123.5 40.6 %shard_map.224 = (bf16[1024,3376]{1,0:T(8,128)(2,1)}, f32[1024,768]{1,0:T(8,128)}, f32[8,1792]{1,0:T(8,128)}) custom-call(bf16[1024,768]{1,0:T(8,128)(2,1)} %tok_ref.5, bf16[1024,768]{1,0:T(8,128)(2,1)} %cot_ref.3, f32[1,768]{1,0:T(1,128)} %reshape.63.gain_ref, bf16[768,1841]{1,0:T(8,128)(2,1)} %bitcast.61, bf16[768,3072]{1,0:T(8,128)(2,1)} %bitcast.81, ...), custom_call_target="tpu_custom_call" | custom-call | flops 20000000000 | bytes 60000000 | tf_op jit(solution)/shard_map/pallas_call | solution.py:964
  164.1 13.1 %convolution_convert_fusion = bf16[768,3376]{0,1:T(8,128)(2,1)} fusion(bf16[1024,768]{1,0:T(8,128)(2,1)S(1)} %copy-done.7, bf16[1024,3376]{1,0:T(8,128)(2,1)} %get-tuple-element.59), kind=kOutput, calls=%fused_computation | convolution fusion | flops 5312581632 | bytes 13672448 | tf_op jit(solution)/shard_map/dot_general | solution.py:29
  177.2 7.9 %copy.59 = bf16[768,3376]{1,0:T(8,128)(2,1)} copy(bf16[768,3376]{0,1:T(8,128)(2,1)} %convolution_convert_fusion) | data formatting | bytes 10371072 | tf_op jit(solution)/shard_map/convert_element_type | solution.py:1045
  185.1 5.8 %convolution_convert_fusion.1 = bf16[1536,768]{0,1:T(8,128)(2,1)} fusion(bf16[1024,1536]{1,0:T(8,128)(2,1)} %get-tuple-element.60, bf16[1024,768]{1,0:T(8,128)(2,1)S(1)} %copy-done.5), kind=kOutput, calls=%fused_computation.1 | convolution fusion | flops 2417098752 | bytes 7077888 | tf_op jit(solution)/shard_map/dot_general | solution.py:29
  190.9 59.1 %shard_map.225 = (f32[24,3376]{1,0:T(8,128)}, f32[24,1536]{1,0:T(8,128)}, f32[8,1792]{1,0:T(8,128)}) custom-call(bf16[32,24,3376]{2,1,0:T(8,128)(2,1)} %bitcast.58, bf16[32,24,1536]{2,1,0:T(8,128)(2,1)} %bitcast.62, f32[8,1792]{1,0:T(8,128)} %get-tuple-element.61.refs_2_), custom_call_target="tpu_custom_call" | custom-call | tf_op jit(solution)/shard_map/pallas_call | solution.py:452
  250.0 1.4 slice.76
  251.4 0.7 slice.75
  252.7 1.4 slice_reduce_fusion
  254.2 1.4 slice_reduce_fusion.1
  255.6 1.2 slice_bitcast_fusion.1
  256.8 1.2 slice_bitcast_fusion
  258.0 1.7 copy.62
  259.7 1.6 copy.63
  (34 shorter events, 4.5 us)
Async XLA Ops:
  0.6 34.8 %slice-start = ((bf16[24,3376]{1,0:T(8,128)(2,1)}), bf16[24,1536]{1,0:T(8,128)(2,1)S(1)}, s32[]{:S(2)}) async-start(bf16[24,3376]{1,0:T(8,128)(2,1)} %param.16), calls=%async_computation | async-start | bytes 147456 | tf_op jit(solution)/shard_map/slice | solution.py:1065
  0.7 34.3 %copy-start.6 = (f32[48]{0:T(128)S(1)}, f32[48]{0:T(128)}, u32[]{:S(2)}) copy-start(f32[48]{0:T(128)} %param.22) | copy-start | bytes 580
  0.7 34.8 %copy-start.1 = (bf16[1536,24]{0,1:T(8,128)(2,1)S(1)}, bf16[1536,24]{0,1:T(8,128)(2,1)}, u32[]{:S(2)}) copy-start(bf16[1536,24]{0,1:T(8,128)(2,1)} %param.17) | copy-start | bytes 221188
  0.7 35.5 %copy-start.3 = (f32[1792]{0:T(1024)S(1)}, f32[1792]{0:T(1024)}, u32[]{:S(2)}) copy-start(f32[1792]{0:T(1024)} %param.20) | copy-start | bytes 21508
  1.4 71.4 %copy-start = (f32[1024]{0:T(1024)}, f32[1024]{0:T(1024)S(1)}, u32[]{:S(2)}) copy-start(f32[1024]{0:T(1024)S(1)} %get-tuple-element.88) | copy-start | bytes 12292
  36.7 36.1 %copy-start.4 = (f32[24]{0:T(128)S(1)}, f32[24]{0:T(128)}, u32[]{:S(2)}) copy-start(f32[24]{0:T(128)} %param.23) | copy-start | bytes 292
  36.7 36.9 %copy-start.2 = (f32[1536]{0:T(1024)S(1)}, f32[1536]{0:T(1024)}, u32[]{:S(2)}) copy-start(f32[1536]{0:T(1024)} %param.24) | copy-start | bytes 18436
  123.5 40.6 %copy-start.7 = (bf16[1024,768]{1,0:T(8,128)(2,1)S(1)}, bf16[1024,768]{1,0:T(8,128)(2,1)}, u32[]{:S(2)}) copy-start(bf16[1024,768]{1,0:T(8,128)(2,1)} %get-tuple-element.39.normed_ref) | copy-start | bytes 4718596
  177.2 7.9 %copy-start.5 = (bf16[1024,768]{1,0:T(8,128)(2,1)S(1)}, bf16[1024,768]{1,0:T(8,128)(2,1)}, u32[]{:S(2)}) copy-start(bf16[1024,768]{1,0:T(8,128)(2,1)} %cot_ref.3) | copy-start | bytes 4718596

commit v4 on v3

--- a/solution.py
+++ b/solution.py
@@ -225,43 +225,6 @@
             when(ok, lambda dz=dz, way=way: self.along(dz, way).wait_send())
 
 
-def gather_kernel(*refs):
-    n = (len(refs) - 3) // 2
-    owns, fulls = refs[:n], refs[n : 2 * n]
-    send, recv, here = refs[2 * n :]
-    me = place()
-    greet(me)
-    work = [Gatherer(me, owns[i], fulls[i], send.at[i], recv.at[i]) for i in range(n)]
-    for w in work:
-        w.start()
-    locals_ = [pltpu.make_async_copy(owns[i], fulls[i].at[slot(me)], here.at[i]) for i in range(n)]
-    for made in locals_:
-        made.start()
-    for t in range(Gatherer.beats):
-        for w in work:
-            w.beat(t)
-    for w in work:
-        w.finish()
-    for made in locals_:
-        made.wait()
-
-
-def gather(*shards):
-    n = len(shards)
-    return pl.pallas_call(
-        gather_kernel,
-        in_specs=[pl.BlockSpec(memory_space=pl.ANY)] * n,
-        out_specs=[pl.BlockSpec(memory_space=pl.ANY)] * n,
-        out_shape=[jax.ShapeDtypeStruct((32,) + s.shape, s.dtype) for s in shards],
-        scratch_shapes=[
-            pltpu.SemaphoreType.DMA((n, Gatherer.count)),
-            pltpu.SemaphoreType.DMA((n, Gatherer.count)),
-            pltpu.SemaphoreType.DMA((n,)),
-        ],
-        compiler_params=pltpu.CompilerParams(collective_id=0, has_side_effects=True),
-    )(*shards)
-
-
 def partner(at, dy, dx, dc, k):
     return flip(at, dy, dx, dc, 0)[:3] + ({0: at[3], 1: at[3] + 1 - 2 * (at[3] % 2), 2: (at[3] + 2) % 4, 3: 3 - at[3]}[k],)
 
@@ -277,37 +240,58 @@
 BLOCKS = ((1, 1), (0, 1), (1, 0), (0, 0))
 
 
+ORDER = (3, 2, 1, 0)
+
+
 class Scatterer:
-    count = 43
-
-    def __init__(self, me, part, out, mine, from_core, from_pair, from_far, from_line, send, recv, here):
+    count = 59
+
+    def __init__(self, me, part, out, mine, from_core, from_pair, from_far, from_line, send, recv, here=None):
         self.me, self.part, self.out = me, part, out
         self.mine, self.from_core, self.from_pair, self.from_far, self.from_line = (
             mine, from_core, from_pair, from_far, from_line,
         )
         self.send, self.recv, self.here = send, recv, here
         self.left, self.right = halves(part.shape[2])
-        self.copies = {}
-
-    def copy(self, name, src, dst, to):
-        i = len(self.copies)
-        made = pltpu.make_async_remote_copy(
+
+    def copy(self, name, index):
+        if name == "core":
+            b, k, half = index // 8, index // 2 % 4, index % 2
+            cols = self.right if half else self.left
+            src = self.part.at[slot(partner(self.me, *BLOCKS[b], 1, k)), :, cols]
+            dst, to, i = self.from_core.at[b, k, :, cols], (0, 0, 1, 0), index
+        elif name == "x":
+            b, k = index // 4, index % 4
+            src, dst = self.mine.at[b, k, :, self.left], self.from_pair.at[b, k, :, self.left]
+            to, i = (0, 1, 0, 0), 32 + index
+        elif name == "y":
+            b, k = index // 4, index % 4
+            src, dst = self.mine.at[2 * b, k, :, self.right], self.from_pair.at[b, k, :, self.right]
+            to, i = (1, 0, 0, 0), 40 + index
+        elif name == "fy":
+            src, dst = self.mine.at[2, index, :, self.left], self.from_far.at[index, :, self.left]
+            to, i = (1, 0, 0, 0), 48 + index
+        elif name == "fx":
+            src, dst = self.mine.at[1, index, :, self.right], self.from_far.at[index, :, self.right]
+            to, i = (0, 1, 0, 0), 52 + index
+        else:
+            src, dst, to, i = self.mine.at[3, index], self.from_line.at[index - 1], (0, 0, 0, index), 55 + index
+        return pltpu.make_async_remote_copy(
             src_ref=src, dst_ref=dst, send_sem=self.send.at[i], recv_sem=self.recv.at[i],
             device_id=device(partner(self.me, *to)), device_id_type=MESH,
         )
-        made.start()
-        self.copies[name] = made
-
-    def start(self):
-        self.locals = {}
-        for b, (dy, dx) in enumerate(BLOCKS):
-            for k in range(4):
-                other = slot(partner(self.me, dy, dx, 1, k))
-                self.copy(("core", b, k), self.part.at[other], self.from_core.at[b, k], (0, 0, 1, 0))
-                own = slot(partner(self.me, dy, dx, 0, k))
-                made = pltpu.make_async_copy(self.part.at[own], self.mine.at[b, k], self.here.at[b * 4 + k])
-                made.start()
-                self.locals[b, k] = made
+
+    def local(self, b, k):
+        own = slot(partner(self.me, *BLOCKS[b], 0, k))
+        return pltpu.make_async_copy(self.part.at[own], self.mine.at[b, k], self.here.at[b * 4 + k])
+
+    def start(self, *cuts):
+        for k in ORDER:
+            for b in range(4):
+                for half in cuts or (0, 1):
+                    self.copy("core", b * 8 + k * 2 + half).start()
+                if self.here is not None:
+                    self.local(b, k).start()
 
     def add(self, b, k, cols, others):
         total = self.mine[b, k, :, cols].astype(f32)
@@ -315,53 +299,48 @@
             total += ref.astype(f32)
         return total
 
-    def pair(self):
-        for b, (dy, dx) in enumerate(BLOCKS):
-            for k in range(4):
-                self.locals[b, k].wait()
-                self.copies["core", b, k].wait_recv()
-                self.mine[b, k] = (self.mine[b, k].astype(f32) + self.from_core[b, k].astype(f32)).astype(bf16)
-                if dx:
-                    self.copy(
-                        ("x", b, k), self.mine.at[b, k, :, self.left], self.from_pair.at[b, k, :, self.left],
-                        (0, 1, 0, 0),
-                    )
-                if dy:
-                    self.copy(
-                        ("y", b, k), self.mine.at[b, k, :, self.right], self.from_pair.at[b // 2, k, :, self.right],
-                        (1, 0, 0, 0),
-                    )
-
-    def far(self):
-        for k in range(4):
-            self.copies["x", 0, k].wait_recv()
-            self.mine[2, k, :, self.left] = self.add(
-                2, k, self.left, [self.from_pair[0, k, :, self.left]]
-            ).astype(bf16)
-            self.copy(("fy", k), self.mine.at[2, k, :, self.left], self.from_far.at[k, :, self.left], (1, 0, 0, 0))
-            self.copies["y", 0, k].wait_recv()
-            self.mine[1, k, :, self.right] = self.add(
-                1, k, self.right, [self.from_pair[0, k, :, self.right]]
-            ).astype(bf16)
-            self.copy(("fx", k), self.mine.at[1, k, :, self.right], self.from_far.at[k, :, self.right], (0, 1, 0, 0))
-
-    def line(self):
-        for k in (1, 2, 3, 0):
-            for name in (("x", 1, k), ("y", 2, k), ("fy", k), ("fx", k)):
-                self.copies[name].wait_recv()
-            if k:
-                self.mine[3, k] = self.add(3, k, slice(None), [self.from_pair[1, k], self.from_far[k]]).astype(bf16)
-                self.copy(("z", k), self.mine.at[3, k], self.from_line.at[k - 1], (0, 0, 0, k))
+    def pair(self, k):
+        for b in range(4):
+            for half in (0, 1):
+                self.copy("core", b * 8 + k * 2 + half).wait_recv()
+            if self.here is not None:
+                self.local(b, k).wait()
+                own = self.mine[b, k]
+            else:
+                own = self.part[slot(partner(self.me, *BLOCKS[b], 0, k))]
+            self.mine[b, k] = (own.astype(f32) + self.from_core[b, k].astype(f32)).astype(bf16)
+            if b < 2:
+                self.copy("x", b * 4 + k).start()
+            if b % 2 == 0:
+                self.copy("y", b * 2 + k).start()
+
+    def far(self, k):
+        self.copy("x", k).wait_recv()
+        self.mine[2, k, :, self.left] = self.add(2, k, self.left, [self.from_pair[0, k, :, self.left]]).astype(bf16)
+        self.copy("fy", k).start()
+        self.copy("y", k).wait_recv()
+        self.mine[1, k, :, self.right] = self.add(1, k, self.right, [self.from_pair[0, k, :, self.right]]).astype(bf16)
+        self.copy("fx", k).start()
+
+    def line(self, k):
+        for made in (self.copy("x", 4 + k), self.copy("y", 4 + k), self.copy("fy", k), self.copy("fx", k)):
+            made.wait_recv()
+        if k:
+            self.mine[3, k] = self.add(3, k, slice(None), [self.from_pair[1, k], self.from_far[k]]).astype(bf16)
+            self.copy("z", k).start()
 
     def finish(self):
         for k in (1, 2, 3):
-            self.copies["z", k].wait_recv()
+            self.copy("z", k).wait_recv()
         self.out[...] = self.add(
             3, 0, slice(None),
             [self.from_pair[1, 0], self.from_far[0], self.from_line[0], self.from_line[1], self.from_line[2]],
         )
-        for made in self.copies.values():
-            made.wait_send()
+        for name, indices in (
+            ("core", range(32)), ("x", range(8)), ("y", range(8)), ("fy", range(4)), ("fx", range(4)), ("z", (1, 2, 3)),
+        ):
+            for i in indices:
+                self.copy(name, i).wait_send()
 
 
 def scatter_scratch(rows, width):
@@ -369,128 +348,129 @@
     return [
         vmem(4, 4), vmem(4, 4), vmem(2, 4), vmem(4), vmem(3),
         pltpu.SemaphoreType.DMA((Scatterer.count,)), pltpu.SemaphoreType.DMA((Scatterer.count,)),
-        pltpu.SemaphoreType.DMA((16,)),
     ]
 
 
 class Summer:
     def __init__(self, me, own, out, held, send, recv):
         self.me, self.own, self.out, self.held, self.send, self.recv = me, own, out, held, send, recv
-        self.copies = []
-
-    def copy(self, src, dst, to):
-        i = len(self.copies)
-        made = pltpu.make_async_remote_copy(
-            src_ref=src, dst_ref=dst, send_sem=self.send.at[i], recv_sem=self.recv.at[i],
+
+    def copy(self, i):
+        src = self.own if i == 0 else self.held.at[5 + min(i, 3)]
+        to = ((0, 0, 1, 0), (0, 1, 0, 0), (1, 0, 0, 0), (0, 0, 0, 1), (0, 0, 0, 2), (0, 0, 0, 3))[i]
+        return pltpu.make_async_remote_copy(
+            src_ref=src, dst_ref=self.held.at[i], send_sem=self.send.at[i], recv_sem=self.recv.at[i],
             device_id=device(partner(self.me, *to)), device_id_type=MESH,
         )
-        made.start()
-        self.copies.append(made)
 
     def start(self):
-        self.copy(self.own, self.held.at[0], (0, 0, 1, 0))
-
-    def second(self):
-        self.copies[0].wait_recv()
-        self.out[...] = self.own[...] + self.held[0]
-        self.held[6] = self.out[...]
-        self.copy(self.held.at[6], self.held.at[1], (0, 1, 0, 0))
-
-    def third(self):
-        self.copies[1].wait_recv()
-        self.held[7] = self.held[6] + self.held[1]
-        self.copy(self.held.at[7], self.held.at[2], (1, 0, 0, 0))
-
-    def fourth(self):
-        self.copies[2].wait_recv()
-        self.held[8] = self.held[7] + self.held[2]
-        for k in (1, 2, 3):
-            self.copy(self.held.at[8], self.held.at[2 + k], (0, 0, 0, k))
+        self.copy(0).start()
+
+    def next(self, i):
+        self.copy(i - 1).wait_recv()
+        before = self.own[...] if i == 1 else self.held[4 + i]
+        self.held[5 + i] = before + self.held[i - 1]
+        for j in (i,) if i < 3 else (3, 4, 5):
+            self.copy(j).start()
 
     def finish(self):
-        for made in self.copies[3:]:
-            made.wait_recv()
+        for j in (3, 4, 5):
+            self.copy(j).wait_recv()
         self.out[...] = (self.held[8] + self.held[3]) + (self.held[4] + self.held[5])
-        for made in self.copies:
-            made.wait_send()
-
-
-def scatter_kernel(n, *refs):
-    parts, small = refs[:n], refs[n]
-    outs, small_out = refs[n + 1 : 2 * n + 1], refs[2 * n + 1]
-    scratch = refs[2 * n + 2 :]
-    me = place()
-    greet_all(me)
-    work = [Scatterer(me, parts[i], outs[i], *scratch[8 * i : 8 * i + 8]) for i in range(n)]
-    tiny = Summer(me, small, small_out, *scratch[8 * n :])
-    tiny.start()
-    for w in work:
-        w.start()
-    tiny.second()
-    for w in work:
-        w.pair()
-    tiny.third()
-    for w in work:
-        w.far()
-    tiny.fourth()
-    for w in work:
-        w.line()
-    for w in work:
-        w.finish()
-    tiny.finish()
-
-
-def scatter(parts, small):
-    n = len(parts)
-    scratch = []
-    for p in parts:
-        scratch += scatter_scratch(p.shape[1], p.shape[2])
-    scratch += [
-        pltpu.VMEM((9,) + small.shape, f32), pltpu.SemaphoreType.DMA((6,)), pltpu.SemaphoreType.DMA((6,)),
+        for j in range(6):
+            self.copy(j).wait_send()
+
+
+AUX = 16
+
+
+def features(seg_ref, at):
+    last = seg_ref.shape[0] - 1
+    line = lambda i: jnp.broadcast_to(seg_ref[pl.ds(i, 1), :].astype(f32), (8, Q))
+    seg = line(at)
+    before = jnp.where(at > 0, line(jnp.maximum(at - 1, 0)), -1.0)
+    after = jnp.where(at < last, line(jnp.minimum(at + 1, last)), -1.0)
+    lane = lax.broadcasted_iota(jnp.int32, (8, Q), 1)
+    earlier = [jnp.where(lane < k, pltpu.roll(before, k, 1), pltpu.roll(seg, k, 1)) == seg for k in (1, 2, 3)]
+    later = [
+        jnp.where(lane < Q - k, pltpu.roll(seg, Q - k, 1), pltpu.roll(after, Q - k, 1)) == seg for k in (1, 2, 3)
     ]
-    vmem = pl.BlockSpec(memory_space=pltpu.VMEM)
-    return pl.pallas_call(
-        functools.partial(scatter_kernel, n),
-        in_specs=[pl.BlockSpec(memory_space=pl.ANY)] * n + [vmem],
-        out_specs=[vmem] * (n + 1),
-        out_shape=[jax.ShapeDtypeStruct(p.shape[1:], f32) for p in parts]
-        + [jax.ShapeDtypeStruct(small.shape, f32)],
-        scratch_shapes=scratch,
-        compiler_params=pltpu.CompilerParams(
-            collective_id=2, has_side_effects=True, vmem_limit_bytes=60 * 1024 * 1024
-        ),
-    )(*parts, small)
+    edges = [seg == x for x in (seg[:, Q - 1 :], seg[:, :1], before[:, Q - 1 :], after[:, :1])]
+    one = lambda mask: jnp.where(mask, 1.0, 0.0)
+    lines = [one(m) for m in earlier] + [seg] + [one(m) for m in edges + later]
+    row = lax.broadcasted_iota(jnp.int32, (8, Q), 0)
+    blocks = []
+    for i in range(0, AUX, 8):
+        block = jnp.zeros((8, Q), f32)
+        for j, x in enumerate(lines[i : i + 8]):
+            block = jnp.where(row == j, x, block)
+        blocks.append(block)
+    return jnp.transpose(jnp.concatenate(blocks + [jnp.zeros((Q - AUX, Q), f32)], axis=0))
 
 
 def reaches(here, number):
     return dict(collective_id=number, has_side_effects=True) if here else {}
 
 
-BEATS = (0, 2, 4, 5, 7, 8, 9, 10, 11)
+OTHERS_AT = 3
+OTHERS_LAG = 4
+BEATS = (5, 6, 7, 8, 9, 10, 11, 11, 11)
 
 
 def front_kernel(
     sizes, here,
-    tok_ref, halo_ref, gain_ref, w_ref, cw_ref, cb_ref, dtb_ref, rate_ref, aux_ref, x2_ref, own_ref,
-    normed_ref, conv_ref, act_ref, low_ref, dsil_ref, dt_ref, cum_ref, dtraw_ref, sb_ref, full_ref,
-    ext_ref, state_ref, send_ref, recv_ref, copy_ref,
+    tok_ref, halo_ref, seg_ref, cw_ref, cb_ref, dtb_ref, alog_ref, x2_ref, first_ref, own_ref, gain_in_ref,
+    normed_ref, turned_ref, conv_ref, act_ref, low_ref, dsil_ref, dt_ref, cum_ref, dtraw_ref, aux_ref, sb_ref, w_ref, gain_ref,
+    full_ref,
+    ext_ref, column_ref, state_ref, land_ref, near_ref, side_ref, send_ref, recv_ref, copy_ref,
 ):
     inner, channels, heads, state = sizes
     step = pl.program_id(0)
+    taken = channels + 2 * heads
     if here:
         me = place()
-        others = Gatherer(me, own_ref, full_ref, send_ref, recv_ref)
-        mine = pltpu.make_async_copy(own_ref, full_ref.at[slot(me)], copy_ref)
-
-        @pl.when(step == 0)
-        def _():
-            greet(me)
-            others.start()
-            mine.start()
+        urgent = Gatherer(me, near_ref, land_ref, send_ref.at[0], recv_ref.at[0])
+        others = Gatherer(me, side_ref, full_ref, send_ref.at[1], recv_ref.at[1])
+        mine = [
+            pltpu.make_async_copy(near_ref, land_ref.at[slot(me)], copy_ref.at[0]),
+            pltpu.make_async_copy(side_ref, full_ref.at[slot(me)], copy_ref.at[1]),
+        ]
 
     @pl.when(step == 0)
     def _():
         state_ref[...] = jnp.zeros_like(state_ref)
+        if here:
+            near_ref[:, :taken] = first_ref[:, inner:]
+            gain_in = gain_in_ref[...]
+            gain_in = jnp.concatenate([gain_in, jnp.zeros((1, Q - gain_in.shape[1]), f32)], axis=1)
+            gain_in = jnp.transpose(jnp.broadcast_to(gain_in, (Q, Q)))
+            near_ref[:, taken:] = gain_in[: near_ref.shape[0], 0:1].astype(bf16)
+            side_ref[:, :inner] = first_ref[:, :inner]
+            side_ref[:, inner:] = own_ref[...]
+            greet(me)
+            urgent.start()
+            mine[0].start()
+            for t in range(Gatherer.beats):
+                if t == OTHERS_AT:
+                    others.start()
+                    mine[1].start()
+                urgent.beat(t)
+                if 0 <= t - OTHERS_LAG < BEATS[0]:
+                    others.beat(t - OTHERS_LAG)
+            mine[0].wait()
+            urgent.finish()
+            source = land_ref
+        else:
+            source = first_ref
+        rows = source.shape[1]
+        group = 1 if rows % 16 == 0 else 48 // rows
+        for j in range(0, source.shape[0], group):
+            block = jnp.concatenate([source[j + i].astype(f32) for i in range(group)], axis=0)
+            at = slice(j * rows, (j + group) * rows)
+            w_ref[at, :] = block[:, :taken].astype(bf16)
+            column_ref[at, :] = jnp.broadcast_to(block[:, taken:], (block.shape[0], Q))
+        for at in range(0, gain_ref.shape[1], Q):
+            gain_ref[:, at : at + Q] = jnp.transpose(column_ref[at : at + Q, :])[0:1, :]
 
     gain = gain_ref[...]
 
@@ -501,10 +481,12 @@
 
     normed = norm(tok_ref[...])
     normed_ref[...] = normed
+    turned_ref[...] = jnp.transpose(normed)
     both = jnp.concatenate([norm(halo_ref[...]), normed], axis=0)
     dt_raw = nn(normed, w_ref[:, channels : channels + 2 * heads])
     dtraw_ref[...] = dt_raw
-    aux = aux_ref[...]
+    aux = features(seg_ref, pl.num_programs(0) - 1 - step)
+    aux_ref[...] = aux[:, : aux_ref.shape[1]]
     m1, m2, m3 = aux[:, 0:1], aux[:, 1:2], aux[:, 2:3]
     block = 256
     for at in range(0, channels, block):
@@ -512,7 +494,7 @@
         ext_ref[:, sl] = nn(both, w_ref[:, at : at + block])
         x0 = ext_ref[HALO : HALO + Q, sl]
         conv_ref[:, sl] = x0
-        pre = cb_ref[:, sl] + cw_ref[0:1, sl] * x0
+        pre = cb_ref[sl][None, :] + cw_ref[0:1, sl] * x0
         pre += cw_ref[1:2, sl] * (ext_ref[HALO - 1 : HALO - 1 + Q, sl] * m1)
         pre += cw_ref[2:3, sl] * (ext_ref[HALO - 2 : HALO - 2 + Q, sl] * m2)
         pre += cw_ref[3:4, sl] * (ext_ref[HALO - 3 : HALO - 3 + Q, sl] * m3)
@@ -524,7 +506,7 @@
     v = dt_raw + dtb_ref[...]
     dt = jnp.maximum(v, 0.0) + jnp.log1p(jnp.exp(-jnp.abs(v)))
     dt_ref[...] = dt
-    rate = -dt * rate_ref[...]
+    rate = -dt * jnp.exp(alog_ref[...])
     row, col = iotas((Q, Q))
     cum = nn_exact((col <= row).astype(bf16), rate)
     cum_ref[...] = cum
@@ -547,63 +529,72 @@
                 for t in range(BEATS[i], BEATS[i + 1]):
                     others.beat(t)
                 if i == steps - 1:
+                    mine[1].wait()
                     others.finish()
-                    mine.wait()
-
-
-def front(tokens, gain_row, w_in, conv_w, conv_b, dt_bias, rate_row, aux, x2, own, sizes, here):
+
+
+def front(tokens, seg, conv_w, conv_b, dt_bias, a_log, x2, first, own, gain, sizes, here):
     inner, channels, heads, state = sizes
     t, d = tokens.shape
     n = t // Q
-    rows = own.shape[0]
     rev = lambda i: (n - 1 - i, 0)
     fixed = lambda i: (0, 0)
     blk = lambda width: pl.BlockSpec((Q, width), rev)
-    whole = lambda a: pl.BlockSpec(a.shape, fixed)
+    whole = lambda a: pl.BlockSpec(a.shape, lambda i: (0,) * a.ndim)
+    anywhere = pl.BlockSpec(memory_space=pl.ANY)
     per = Q // HALO
     out = lambda width, dtype: jax.ShapeDtypeStruct((t, width), dtype)
+    taken = channels + 2 * heads
+    rows = own.shape[0]
     return pl.pallas_call(
         functools.partial(front_kernel, sizes, here),
         grid=(n,),
         in_specs=[
             blk(d),
             pl.BlockSpec((HALO, d), lambda i: (jnp.maximum((n - 1 - i) * per - 1, 0), 0)),
-            whole(gain_row), whole(w_in), whole(conv_w), whole(conv_b), whole(dt_bias), whole(rate_row),
-            blk(aux.shape[1]), whole(x2), pl.BlockSpec(memory_space=pl.ANY),
+            whole(seg), whole(conv_w), whole(conv_b), whole(dt_bias), whole(a_log), whole(x2), whole(first), whole(own),
+            whole(gain),
         ],
         out_specs=[
-            blk(d), blk(channels), blk(channels), blk(channels), blk(channels),
-            blk(2 * heads), blk(2 * heads), blk(2 * heads),
+            blk(d), pl.BlockSpec((d, Q), lambda i: (0, n - 1 - i)), blk(channels), blk(channels), blk(channels), blk(channels),
+            blk(2 * heads), blk(2 * heads), blk(2 * heads), blk(AUX),
             pl.BlockSpec((1, state, inner), lambda i: (n - 1 - i, 0, 0)),
-            pl.BlockSpec(memory_space=pl.ANY),
+            pl.BlockSpec((d, taken), fixed), pl.BlockSpec((1, d), fixed),
+            anywhere,
         ],
         out_shape=[
-            out(d, bf16), out(channels, f32), out(channels, f32), out(channels, bf16), out(channels, f32),
-            out(2 * heads, f32), out(2 * heads, f32), out(2 * heads, f32),
+            out(d, bf16), jax.ShapeDtypeStruct((d, t), bf16),
+            out(channels, f32), out(channels, f32), out(channels, bf16), out(channels, f32),
+            out(2 * heads, f32), out(2 * heads, f32), out(2 * heads, f32), out(AUX, f32),
             jax.ShapeDtypeStruct((n, state, inner), bf16),
-            jax.ShapeDtypeStruct((32 if here else 1,) + own.shape, bf16),
+            jax.ShapeDtypeStruct((d, taken), bf16), jax.ShapeDtypeStruct((1, d), f32),
+            jax.ShapeDtypeStruct((32, rows, 2 * inner) if here else (1, 8, Q), bf16),
         ],
         scratch_shapes=[
             pltpu.VMEM((HALO + Q, channels), f32),
+            pltpu.VMEM((d, Q), f32),
             pltpu.VMEM((state, inner), f32),
-            pltpu.SemaphoreType.DMA((Gatherer.count,)),
-            pltpu.SemaphoreType.DMA((Gatherer.count,)),
-            pltpu.SemaphoreType.DMA,
+            pltpu.VMEM((32, rows, taken + 1) if here else (1, 8, Q), bf16),
+            pltpu.VMEM((rows, taken + 1), bf16),
+            pltpu.VMEM((rows, 2 * inner), bf16),
+            pltpu.SemaphoreType.DMA((2, Gatherer.count)),
+            pltpu.SemaphoreType.DMA((2, Gatherer.count)),
+            pltpu.SemaphoreType.DMA((2,)),
         ],
         compiler_params=pltpu.CompilerParams(
-            dimension_semantics=("arbitrary",), vmem_limit_bytes=60 * 1024 * 1024, **reaches(here, 1)
+            dimension_semantics=("arbitrary",), vmem_limit_bytes=60 * 1024 * 1024, **reaches(here, 0)
         ),
         cost_estimate=pl.CostEstimate(flops=5_000_000_000, bytes_accessed=50_000_000, transcendentals=0),
-    )(tokens, tokens, gain_row, w_in, conv_w, conv_b, dt_bias, rate_row, aux, x2, own)
+    )(tokens, tokens, seg, conv_w, conv_b, dt_bias, a_log, x2, first, own, gain)
 
 
 def middle_kernel(
     sizes,
-    tok_ref, act_ref, normed_ref, dt_ref, cum_ref, aux_ref, segrow_ref, cot_ref, sb_ref, w_ref,
-    rate_ref, skip_ref, og_ref, x2_ref, r_ref,
-    out_ref, nout_ref, dgate_ref, dy_ref, dv_ref, dbc_ref, drate_ref, dq_ref, sf_ref, dog_ref, dsk_ref,
+    tok_ref, act_ref, normed_ref, dt_ref, cum_ref, aux_ref, seg_ref, cot_ref, sb_ref, w_ref,
+    alog_ref, skip_in_ref, og_ref, x2_ref, r_ref,
+    out_ref, turned_ref, nout_ref, dgate_ref, dy_ref, dv_ref, dbc_ref, drate_ref, dq_ref, sf_ref, dog_ref, dsk_ref,
     decay_ref, mix_ref, state_ref, adj_ref, ssm_ref, gated_ref, dno_ref, yf_ref, yb_ref, wide_ref,
-    p_ref, q_ref, scal_ref, gate_ref,
+    p_ref, q_ref, scal_ref, gate_ref, skip_ref,
 ):
     inner, channels, heads, state = sizes
     quad = 256
@@ -616,12 +607,13 @@
         dog_ref[...] = jnp.zeros_like(dog_ref)
         dsk_ref[...] = jnp.zeros_like(dsk_ref)
         q_ref[...] = jnp.zeros_like(q_ref)
+        skip_ref[...] = nn(split2(jnp.broadcast_to(skip_in_ref[...], (8, heads))), x2_ref[...])[0:1]
 
     sf_ref[0] = state_ref[...].astype(bf16)
     aux = aux_ref[...]
     row, col = iotas((Q, Q))
     lower = col < row
-    same = aux[:, 3:4] == segrow_ref[0]
+    same = aux[:, 3:4] == seg_ref[pl.ds(step, 1), :].astype(f32)
     b_f = act_ref[:, inner : inner + state].astype(bf16)
     c_f = act_ref[:, inner + state : inner + 2 * state].astype(bf16)
     b_b = act_ref[:, inner + 2 * state : inner + 3 * state].astype(bf16)
@@ -629,7 +621,7 @@
     g = jnp.where(same & (col != row), jnp.where(lower, nt(c_f, b_f), nt(c_b, b_b)), 0.0)
     dt = dt_ref[...]
     cum = cum_ref[...]
-    rate = -dt * rate_ref[...]
+    rate = -dt * jnp.exp(alog_ref[...])
     cf, cb = cum[:, :heads], cum[:, heads:] - rate[:, heads:]
     dtf, dtb = dt[:, :heads], dt[:, heads:]
     total_f, total_b = cum[Q - 1 :, :heads], cum[Q - 1 :, heads:]
@@ -662,6 +654,7 @@
     squares = jnp.zeros((Q, quad), f32)
     dots = jnp.zeros((Q, quad), f32)
     cot = cot_ref[...]
+    turned_ref[...] = jnp.transpose(cot)
     for at in range(0, inner, quad):
         sl = slice(at, at + quad)
         wide_ref[:, sl] = nn(scales, x2_ref[:, sl])
@@ -697,7 +690,7 @@
         dno = nn(cot, w_ref[:, inner + at : inner + at + quad])
         dno_ref[:, sl] = dno
         squares += gated * gated
-        dots += dno * og_ref[:, sl] * gated
+        dots += dno * og_ref[sl][None, :] * gated
 
     inv = lax.rsqrt(jnp.sum(squares, axis=1, keepdims=True) / inner + eps)
     drag = inv * (inv * jnp.sum(dots, axis=1, keepdims=True) / inner)
@@ -712,7 +705,7 @@
         low = v.astype(bf16)
         low_f = low.astype(f32)
         ssm, gate, gated, dno = ssm_ref[:, sl], gate_ref[:, sl], gated_ref[:, sl], dno_ref[:, sl]
-        og = og_ref[:, sl]
+        og = og_ref[sl][None, :]
         unit = gated * inv
         nout_ref[:, sl] = (unit * og).astype(bf16)
         dog_ref[:, sl] += jnp.sum(dno * unit, axis=0, keepdims=True)
@@ -792,7 +785,7 @@
     dq_ref[...] = jnp.concatenate([q_cols[:, :heads], q_cols[:, heads:] + dots_v], axis=1)
 
 
-def middle(tokens, act, normed, dt, cum, aux, segrow, cot, sb, w_side, rate_row, skip_row, og_row, x2, r, sizes):
+def middle(tokens, act, normed, dt, cum, aux, seg, cot, sb, w_side, a_log, skip, og, x2, r, sizes):
     inner, channels, heads, state = sizes
     t, d = tokens.shape
     n = t // Q
@@ -808,16 +801,17 @@
         grid=(n,),
         in_specs=[
             blk(d), blk(channels), blk(d), blk(2 * heads), blk(2 * heads), blk(aux.shape[1]),
-            pl.BlockSpec((1, 1, Q), cube), blk(d), pl.BlockSpec((1, state, inner), cube),
-            whole(w_side), whole(rate_row), whole(skip_row), whole(og_row), whole(x2), whole(r),
+            whole(seg), blk(d), pl.BlockSpec((1, state, inner), cube),
+            whole(w_side), whole(a_log), whole(skip), pl.BlockSpec(og.shape, lambda i: (0,)), whole(x2), whole(r),
         ],
         out_specs=[
-            blk(d), blk(inner), blk(inner), blk(inner), blk(inner), blk(4 * state),
+            blk(d), pl.BlockSpec((d, Q), lambda i: (0, i)), blk(inner), blk(inner), blk(inner), blk(inner), blk(4 * state),
             blk(2 * heads), blk(2 * heads), pl.BlockSpec((1, state, inner), cube),
             pl.BlockSpec((1, inner), fixed), pl.BlockSpec((1, inner), fixed),
         ],
         out_shape=[
-            out(d, bf16), out(inner, bf16), out(inner, bf16), out(inner, bf16), out(inner, f32),
+            out(d, bf16), jax.ShapeDtypeStruct((d, t), bf16),
+            out(inner, bf16), out(inner, bf16), out(inner, bf16), out(inner, f32),
             out(4 * state, f32), out(2 * heads, f32), out(2 * heads, f32),
             jax.ShapeDtypeStruct((n, state, inner), bf16), line, line,
         ],
@@ -836,21 +830,56 @@
             pltpu.VMEM((Q, Q), f32),
             pltpu.VMEM((1, inner), f32),
             pltpu.VMEM((Q, inner), f32),
+            pltpu.VMEM((1, inner), f32),
         ],
         compiler_params=pltpu.CompilerParams(
             dimension_semantics=("arbitrary",), vmem_limit_bytes=60 * 1024 * 1024
         ),
         cost_estimate=pl.CostEstimate(flops=30_000_000_000, bytes_accessed=60_000_000, transcendentals=0),
-    )(tokens, act, normed, dt, cum, aux, segrow, cot, sb, w_side, rate_row, skip_row, og_row, x2, r)
+    )(tokens, act, normed, dt, cum, aux, seg, cot, sb, w_side, a_log, skip, og, x2, r)
+
+
+def side_kernel(half, a_ref, b_ref, u_ref, v_ref, out_ref):
+    step = pl.program_id(0)
+
+    @pl.when(step < half)
+    def _():
+        out_ref[...] = nn(a_ref[...], u_ref[...]).astype(bf16)
+
+    @pl.when(step >= half)
+    def _():
+        out_ref[...] = nn(b_ref[...], v_ref[...]).astype(bf16)
+
+
+def side(a, b, u, v):
+    d, t = a.shape
+    block = 768
+    half = u.shape[1] // block
+    fixed = lambda i: (0, 0)
+    return pl.pallas_call(
+        functools.partial(side_kernel, half),
+        grid=(2 * half,),
+        in_specs=[
+            pl.BlockSpec((d, t), fixed), pl.BlockSpec((d, t), fixed),
+            pl.BlockSpec((t, block), lambda i: (0, jnp.minimum(i, half - 1))),
+            pl.BlockSpec((t, block), lambda i: (0, jnp.maximum(i - half, 0))),
+        ],
+        out_specs=pl.BlockSpec((d, block), lambda i: (0, i)),
+        out_shape=jax.ShapeDtypeStruct((d, 2 * u.shape[1]), bf16),
+        compiler_params=pltpu.CompilerParams(
+            dimension_semantics=("arbitrary",), vmem_limit_bytes=60 * 1024 * 1024
+        ),
+        cost_estimate=pl.CostEstimate(flops=4 * d * t * u.shape[1], bytes_accessed=14_000_000, transcendentals=0),
+    )(a, b, u, v)
 
 
 def back_kernel(
-    sizes,
-    tok_ref, cot_ref, gain_ref, w_ref, side_ref, cw_ref, dtb_ref, rate_ref, aux_ref, x2_ref, r_ref,
+    sizes, here,
+    side_ref, cw_ref, dtb_ref, alog_ref, aux_ref, x2_ref, r_ref,
     low_ref, dsil_ref, conv_ref, dt_ref, cum_ref, dtraw_ref,
-    dgate_ref, dy_ref, dv_ref, dbc_ref, drate_ref, dq_ref, sf_ref, dog_ref, dsk_ref,
-    dproj_ref, dtok_ref, small_ref,
-    adj_ref, dpre_ref, scal_ref,
+    dgate_ref, dy_ref, dv_ref, dbc_ref, drate_ref, dq_ref, sf_ref, dog_ref, dsk_ref, part_ref,
+    dproj_ref, dnorm_ref, small_ref, sum_ref,
+    adj_ref, dpre_ref, scal_ref, *exchange,
 ):
     inner, channels, heads, state = sizes
     quad = 256
@@ -865,8 +894,16 @@
         skips = nn(split_rows(jnp.broadcast_to(dsk_ref[...], (8, inner))), r_ref[...])
         small_ref[6:7, SKIP_AT : SKIP_AT + Q] = skips[0:1] + skips[8:9]
 
-    d = tok_ref.shape[1]
-
+    if here:
+        me = place()
+        sums = Scatterer(me, part_ref, sum_ref, *exchange)
+
+        @pl.when(step == 0)
+        def _():
+            greet_all(me)
+            sums.start()
+
+    dnorm_ref[...] = nt(dgate_ref[...], side_ref[...])
     dpre_ref[Q:, :] = dpre_ref[0:8, :]
     aux = aux_ref[...]
     dt = dt_ref[...]
@@ -917,8 +954,7 @@
             z = dpre_ref[k : Q + k, sl] * mask
             small_ref[k : k + 1, sl] += jnp.sum(z * conv, axis=0, keepdims=True)
             total += cw_ref[k : k + 1, sl] * z
-        dproj_ref[:, inner + at : inner + at + quad] = total.astype(bf16)
-    dproj_ref[:, :inner] = dgate_ref[...]
+        dproj_ref[:, at : at + quad] = total.astype(bf16)
 
     row, col = iotas((Q, Q))
     through = nn(split_rows(jnp.broadcast_to(scal_ref[...], (8, inner))), r_ref[...])
@@ -929,121 +965,173 @@
     d_rate = drate_ref[...] + jnp.concatenate([extra, none], axis=1)
     d_dt = dq_ref[...] + jnp.concatenate([dots, none], axis=1)
     d_dt = jnp.where(dt > 0.0, d_dt / jnp.maximum(dt, 1e-37), 0.0)
-    a = rate_ref[...]
+    a = jnp.exp(alog_ref[...])
     v = dtraw_ref[...] + dtb_ref[...]
     d_v = (d_dt - d_rate * a) / (1.0 + jnp.exp(-v))
     small_ref[6:7, BIAS_AT : BIAS_AT + 2 * heads] += jnp.sum(d_v, axis=0, keepdims=True)
     small_ref[6:7, LOG_AT : LOG_AT + 2 * heads] += jnp.sum(d_rate * (-dt * a), axis=0, keepdims=True)
-    dproj_ref[:, inner + channels :] = d_v.astype(bf16)
-
-    d_normed = (
-        nt(dproj_ref[:, :inner], side_ref[:, :inner])
-        + nt(dproj_ref[:, inner : inner + channels], w_ref[:, :channels])
-        + nt(dproj_ref[:, inner + channels :], w_ref[:, channels : channels + 2 * heads])
-    )
-    x = tok_ref[...].astype(f32)
-    inv = lax.rsqrt(jnp.mean(x * x, axis=1, keepdims=True) + eps)
-    unit = x * inv
-    small_ref[6:7, :d] += jnp.sum(d_normed * unit, axis=0, keepdims=True)
-    a = d_normed * gain_ref[...]
-    dtok_ref[...] = cot_ref[...].astype(f32) + inv * (a - unit * jnp.mean(a * unit, axis=1, keepdims=True))
+    dproj_ref[:, channels:] = d_v.astype(bf16)
+    if here:
+        for i, acts in enumerate(SUM_BEATS):
+
+            @pl.when(step == i)
+            def _():
+                for name, *index in acts:
+                    getattr(sums, name)(*index)
+
+
+SUM_BEATS = (
+    (("pair", 3),),
+    (("pair", 2), ("far", 3)),
+    (("pair", 1), ("far", 2), ("line", 3)),
+    (("pair", 0), ("far", 1), ("line", 2)),
+    (("far", 0), ("line", 1)),
+    (),
+    (("line", 0),),
+    (("finish",),),
+)
 
 
 def back(
-    tokens, cot, gain_row, w_in, w_side, conv_w, dt_bias, rate_row, aux, x2, r, low, dsil, conv, dt, cum, dtraw,
-    dgate, dy, dv, dbc, drate, dq, sf, dog, dsk, sizes,
+    w_side, conv_w, dt_bias, rate_row, aux, x2, r, low, dsil, conv, dt, cum, dtraw,
+    dgate, dy, dv, dbc, drate, dq, sf, dog, dsk, part, sizes, here,
 ):
     inner, channels, heads, state = sizes
-    t, d = tokens.shape
+    t, d = low.shape[0], w_side.shape[0]
     n = t // Q
-    proj = inner + channels + 2 * heads
+    taken = channels + 2 * heads
     rev = lambda i: (n - 1 - i, 0)
     fixed = lambda i: (0, 0)
     blk = lambda a: pl.BlockSpec((Q, a.shape[1]), rev)
     whole = lambda a: pl.BlockSpec(a.shape, fixed)
+    summed = part.shape[1:]
     return pl.pallas_call(
-        functools.partial(back_kernel, sizes),
+        functools.partial(back_kernel, sizes, here),
         grid=(n,),
         in_specs=[
-            blk(tokens), blk(cot), whole(gain_row), whole(w_in), pl.BlockSpec((w_side.shape[0], inner), fixed), whole(conv_w), whole(dt_bias), whole(rate_row),
+            pl.BlockSpec((d, inner), fixed), whole(conv_w), whole(dt_bias), whole(rate_row),
             blk(aux), whole(x2), whole(r), blk(low), blk(dsil), blk(conv), blk(dt), blk(cum), blk(dtraw),
             blk(dgate), blk(dy), blk(dv), blk(dbc), blk(drate), blk(dq),
             pl.BlockSpec((1, state, inner), lambda i: (n - 1 - i, 0, 0)), whole(dog), whole(dsk),
+            pl.BlockSpec(memory_space=pl.ANY),
         ],
-        out_specs=[pl.BlockSpec((Q, proj), rev), pl.BlockSpec((Q, d), rev), pl.BlockSpec((8, channels), fixed)],
+        out_specs=[
+            pl.BlockSpec((Q, taken), rev), pl.BlockSpec((Q, d), rev), pl.BlockSpec((8, channels), fixed),
+            pl.BlockSpec(summed, fixed),
+        ],
         out_shape=[
-            jax.ShapeDtypeStruct((t, proj), bf16),
+            jax.ShapeDtypeStruct((t, taken), bf16),
             jax.ShapeDtypeStruct((t, d), f32),
             jax.ShapeDtypeStruct((8, channels), f32),
+            jax.ShapeDtypeStruct(summed, f32),
         ],
         scratch_shapes=[
             pltpu.VMEM((state, inner), f32),
             pltpu.VMEM((Q + 8, channels), f32),
             pltpu.VMEM((1, inner), f32),
-        ],
+        ]
+        + (scatter_scratch(*summed) + [pltpu.SemaphoreType.DMA((16,))] if here else []),
         compiler_params=pltpu.CompilerParams(
-            dimension_semantics=("arbitrary",), vmem_limit_bytes=60 * 1024 * 1024
+            dimension_semantics=("arbitrary",), vmem_limit_bytes=60 * 1024 * 1024, **reaches(here, 1)
         ),
         cost_estimate=pl.CostEstimate(flops=20_000_000_000, bytes_accessed=60_000_000, transcendentals=0),
     )(
-        tokens, cot, gain_row, w_in, w_side, conv_w, dt_bias, rate_row, aux, x2, r, low, dsil, conv, dt, cum, dtraw,
-        dgate, dy, dv, dbc, drate, dq, sf, dog, dsk,
+        w_side, conv_w, dt_bias, rate_row, aux, x2, r, low, dsil, conv, dt, cum, dtraw,
+        dgate, dy, dv, dbc, drate, dq, sf, dog, dsk, part,
     )
 
 
-def features(segment_ids):
-    t = segment_ids.shape[0]
-    n = t // Q
-    seg = segment_ids.astype(f32)
-    earlier = [jnp.concatenate([jnp.full((k,), -1.0, f32), seg[: t - k]]) == seg for k in (1, 2, 3)]
-    later = [jnp.concatenate([seg[k:], jnp.full((k,), -1.0, f32)]) == seg for k in (1, 2, 3)]
-    chunks = seg.reshape(n, Q)
-    ends, starts = chunks[:, -1:], chunks[:, :1]
-    none = jnp.full((1, 1), -1.0, f32)
-    like = lambda edge: (chunks == edge).reshape(t)
-    columns = earlier + [
-        seg,
-        like(ends),
-        like(starts),
-        like(jnp.concatenate([none, ends[:-1]])),
-        like(jnp.concatenate([starts[1:], none])),
-    ] + later
-    aux = jnp.stack([c.astype(f32) for c in columns], axis=1)
-    return aux, chunks.reshape(n, 1, Q)
-
-
-def local(here, tokens, segment_ids, w_in, own_side, gain, conv_w, conv_b, dt_bias, a_log, d_skip, out_gain, cotangent):
-    heads = d_skip.shape[0]
-    inner = out_gain.shape[0]
-    channels = conv_w.shape[1]
-    state = (channels - inner) // 4
-    width = inner // heads
-    sizes = (inner, channels, heads, state)
-    aux, segrow = features(segment_ids)
-    spread = np.arange(inner)[None, :] // width == np.arange(heads)[:, None]
-    x2 = jnp.asarray(np.concatenate([spread, spread], axis=0), bf16)
-    r = jnp.asarray(np.pad(spread.T, ((0, 0), (0, Q - heads))), bf16)
-    gain_row = gain.astype(f32)[None, :]
-    rate_row = jnp.exp(a_log)[None, :]
-    dtb_row = dt_bias[None, :]
-    skip_row = jnp.repeat(d_skip, width)[None, :]
-    normed, conv, act, low, dsil, dt, cum, dtraw, sb, w_side = front(
-        tokens, gain_row, w_in, conv_w, conv_b[None, :], dtb_row, rate_row, aux, x2, own_side, sizes, here
-    )
-    if not here:
-        w_side = lax.all_gather(own_side, AXES)
-    w_side = w_side.reshape(-1, 2 * inner)
-    output, nout, dgate, dy, dv, dbc, drate, dq, sf, d_og, d_sk = middle(
-        tokens, act, normed, dt, cum, aux, segrow, cotangent, sb, w_side, rate_row, skip_row,
-        out_gain[None, :], x2, r, sizes,
-    )
-    d_w_out_t = tn(cotangent, nout).astype(bf16)
-    dproj, d_tokens, small = back(
-        tokens, cotangent, gain_row, w_in, w_side, conv_w, dtb_row, rate_row, aux, x2, r, low, dsil, conv, dt, cum, dtraw,
-        dgate, dy, dv, dbc, drate, dq, sf, d_og, d_sk, sizes,
-    )
-    d_w_in = tn(normed, dproj).astype(bf16)
-    return output, d_tokens, d_w_in, d_w_out_t, small
+def tail_kernel(
+    here,
+    turned_ref, dproj_ref, w_ref, dnorm_ref, tok_ref, cot_ref, gain_ref, small_ref,
+    dtok_ref, sum_ref, total_ref,
+    own_ref, *exchange,
+):
+    step = pl.program_id(0)
+    last = pl.num_programs(0) - 1
+    d = tok_ref.shape[1]
+    if here:
+        me = place()
+        part_ref, *rest = exchange
+        sums = Scatterer(me, part_ref, sum_ref, *rest[:7])
+        tiny = Summer(me, own_ref, total_ref, *rest[7:])
+
+    @pl.when(step == 0)
+    def _():
+        own_ref[...] = small_ref[...]
+        if here:
+            greet_all(me)
+            for half, cols in enumerate((sums.left, sums.right)):
+                block = nn(turned_ref[...], dproj_ref[:, cols])
+                part_ref[:, :, cols] = block.reshape(part_ref.shape[:2] + block.shape[1:]).astype(bf16)
+                sums.start(half)
+
+    rows = pl.ds(pl.multiple_of(step * TAIL, TAIL), TAIL)
+    d_normed = dnorm_ref[...] + nt(dproj_ref[rows, :], w_ref[...])
+    x = tok_ref[...].astype(f32)
+    inv = lax.rsqrt(jnp.mean(x * x, axis=1, keepdims=True) + eps)
+    unit = x * inv
+    own_ref[6:7, :d] += jnp.sum(d_normed * unit, axis=0, keepdims=True)
+    a = d_normed * gain_ref[...]
+    dtok_ref[...] = cot_ref[...].astype(f32) + inv * (a - unit * jnp.mean(a * unit, axis=1, keepdims=True))
+    if here:
+        for i, acts in enumerate(TAIL_BEATS):
+
+            @pl.when(step == i)
+            def _():
+                for name, *index in acts:
+                    getattr(tiny if name in ("first", "next") else sums, "start" if name == "first" else name)(*index)
+                if i == len(TAIL_BEATS) - 1:
+                    tiny.finish()
+    else:
+
+        @pl.when(step == last)
+        def _():
+            total_ref[...] = own_ref[...]
+
+
+TAIL = 256
+TAIL_BEATS = (
+    (("pair", 3),),
+    (("pair", 2), ("far", 3)),
+    (("pair", 1), ("far", 2), ("line", 3)),
+    (
+        ("first",), ("pair", 0), ("far", 1), ("line", 2), ("next", 1), ("far", 0), ("line", 1), ("next", 2), ("line", 0),
+        ("next", 3), ("finish",),
+    ),
+)
+
+
+def tail(turned, dproj, w_first, dnorm, tokens, cot, gain_row, small, rows, here):
+    d, t = turned.shape
+    n = t // TAIL
+    taken = dproj.shape[1]
+    fwd = lambda i: (i, 0)
+    fixed = lambda i: (0, 0)
+    blk = pl.BlockSpec((TAIL, d), fwd)
+    whole = lambda a: pl.BlockSpec(a.shape, fixed)
+    exchange = []
+    if here:
+        exchange = [pltpu.VMEM((d // rows, rows, taken), bf16)] + scatter_scratch(rows, taken)
+        exchange += [
+            pltpu.VMEM((9,) + small.shape, f32), pltpu.SemaphoreType.DMA((6,)), pltpu.SemaphoreType.DMA((6,)),
+        ]
+    return pl.pallas_call(
+        functools.partial(tail_kernel, here),
+        grid=(n,),
+        in_specs=[whole(turned), whole(dproj), whole(w_first), blk, blk, blk, whole(gain_row), whole(small)],
+        out_specs=[blk, pl.BlockSpec((rows, taken), fixed), whole(small)],
+        out_shape=[
+            jax.ShapeDtypeStruct((t, d), f32),
+            jax.ShapeDtypeStruct((rows, taken), f32),
+            jax.ShapeDtypeStruct(small.shape, f32),
+        ],
+        scratch_shapes=[pltpu.VMEM(small.shape, f32)] + exchange,
+        compiler_params=pltpu.CompilerParams(
+            dimension_semantics=("arbitrary",), vmem_limit_bytes=60 * 1024 * 1024, **reaches(here, 2)
+        ),
+        cost_estimate=pl.CostEstimate(flops=10_000_000_000, bytes_accessed=30_000_000, transcendentals=0),
+    )(turned, dproj, w_first, dnorm, tokens, cot, gain_row, small)
 
 
 def unpack(small, taps, inner, heads, d):
@@ -1057,27 +1145,90 @@
     )
 
 
+def finish_kernel(
+    sizes, side_ref, first_ref, small_ref,
+    din_ref, dout_ref, dgain_ref, dcw_ref, dcb_ref, ddtb_ref, dalog_ref, dsk_ref, dog_ref,
+):
+    inner, channels, heads, rows = sizes
+    din_ref[:, :inner] = side_ref[:, :inner]
+    din_ref[:, inner:] = first_ref[...]
+    dout_ref[...] = side_ref[:, inner:]
+    taps = dcw_ref.shape[0]
+    dcw_ref[...] = small_ref[:taps, :]
+    dcb_ref[...] = small_ref[taps, :]
+    dog_ref[...] = small_ref[5, :inner]
+    ddtb_ref[...] = small_ref[6:7, BIAS_AT : BIAS_AT + 2 * heads]
+    dalog_ref[...] = small_ref[6:7, LOG_AT : LOG_AT + 2 * heads]
+    dsk_ref[...] = small_ref[6:7, SKIP_AT : SKIP_AT + heads]
+    d = BIAS_AT
+    row, col = iotas((d, Q))
+    own = (row == col + slot(place()) * rows) & (col < rows)
+    parts = jnp.broadcast_to(small_ref[6:7, :d], (8, d))
+    hi = parts.astype(bf16)
+    mid = (parts - hi.astype(f32)).astype(bf16)
+    lo = (parts - hi.astype(f32) - mid.astype(f32)).astype(bf16)
+    pick = jnp.where(own, 1.0, 0.0).astype(bf16)
+    dgain_ref[...] = (nn(hi, pick) + nn(mid, pick) + nn(lo, pick))[0:1, :rows]
+
+
+def finish(sides, firsts, small, taps, sizes):
+    inner, channels, heads, rows = sizes
+    shapes = [
+        (rows, inner + firsts.shape[1]), (rows, inner), (1, rows), (taps, channels), (channels,), (1, 2 * heads),
+        (1, 2 * heads), (1, heads), (inner,),
+    ]
+    return pl.pallas_call(
+        functools.partial(finish_kernel, sizes),
+        out_shape=[jax.ShapeDtypeStruct(shape, f32) for shape in shapes],
+    )(sides, firsts, small)
+
+
 def body(here, tokens, segment_ids, w_in, w_out, norm_gain, conv_w, conv_b, dt_bias, a_log, d_skip, out_gain, cotangent):
-    rows, proj = w_in.shape
+    rows = w_in.shape[0]
     d, inner, heads = tokens.shape[1], out_gain.shape[0], d_skip.shape[0]
     parts = d // rows
-    own_first = jnp.concatenate([w_in[:, inner:], norm_gain[:, None]], axis=1)
-    own_side = jnp.concatenate([w_in[:, :inner], w_out.T], axis=1)
-    first = gather(own_first)[0] if here else lax.all_gather(own_first, AXES)
-    first = first.reshape(d, proj - inner + 1)
-    output, d_tokens, g_in, g_out_t, small = local(
-        here, tokens, segment_ids, first, own_side, first[:, proj - inner], conv_w, conv_b, dt_bias, a_log, d_skip,
-        out_gain, cotangent,
+    channels = conv_w.shape[1]
+    state = (channels - inner) // 4
+    width = inner // heads
+    sizes = (inner, channels, heads, state)
+    seg = segment_ids.reshape(-1, Q)
+    spread = np.arange(inner)[None, :] // width == np.arange(heads)[:, None]
+    x2 = jnp.asarray(np.concatenate([spread, spread], axis=0), bf16)
+    r = jnp.asarray(np.pad(spread.T, ((0, 0), (0, Q - heads))), bf16)
+    first, own = w_in, w_out.T
+    if not here:
+        first = lax.all_gather(jnp.concatenate([w_in[:, inner:], norm_gain[:, None]], axis=1), AXES)
+    alog_row, dtb_row = a_log[None, :], dt_bias[None, :]
+    normed, turned, conv, act, low, dsil, dt, cum, dtraw, aux, sb, w_first, gain_row, w_side = front(
+        tokens, seg, conv_w, conv_b, dtb_row, alog_row, x2, first, own, norm_gain.astype(f32)[None, :], sizes, here
     )
-    g_in, g_out_t = g_in.reshape(parts, rows, proj), g_out_t.reshape(parts, rows, inner)
+    if not here:
+        w_side = lax.all_gather(jnp.concatenate([w_in[:, :inner], own], axis=1), AXES)
+    w_side = w_side.reshape(d, 2 * inner)
+    output, cot_turned, nout, dgate, dy, dv, dbc, drate, dq, sf, d_og, d_sk = middle(
+        tokens, act, normed, dt, cum, aux, seg, cotangent, sb, w_side, alog_row, d_skip[None, :], out_gain, x2, r, sizes,
+    )
     if here:
-        d_w_in, d_w_out, small = scatter([g_in, g_out_t], small)
+        g_side = side(turned, cot_turned, dgate, nout)
     else:
-        d_w_in = lax.psum_scatter(g_in.astype(f32), AXES, scatter_dimension=0)
-        d_w_out = lax.psum_scatter(g_out_t.astype(f32), AXES, scatter_dimension=0)
-        small = lax.psum(small, AXES)
-    d_gain, small = unpack(small, conv_w.shape[0], inner, heads, d)
-    d_gain = lax.dynamic_slice_in_dim(d_gain, lax.axis_index(AXES) * rows, rows)
+        g_side = jnp.concatenate([nn(turned, dgate), nn(cot_turned, nout)], axis=1)
+    g_side = g_side.reshape(parts, rows, 2 * inner)
+    dproj, dnorm, small, sides = back(
+        w_side, conv_w, dtb_row, alog_row, aux, x2, r, low, dsil, conv, dt, cum, dtraw,
+        dgate, dy, dv, dbc, drate, dq, sf, d_og, d_sk, g_side, sizes, here,
+    )
+    d_tokens, firsts, small = tail(turned, dproj, w_first, dnorm, tokens, cotangent, gain_row, small, rows, here)
+    if here:
+        d_w_in, d_w_out, d_gain, *small = finish(sides, firsts, small, conv_w.shape[0], (inner, channels, heads, rows))
+        d_gain = d_gain[0]
+        small = tuple(a[0] if a.ndim == 2 and a.shape[0] == 1 else a for a in small)
+    else:
+        g_first = nn(turned, dproj).reshape(parts, rows, dproj.shape[1])
+        firsts = lax.psum_scatter(g_first, AXES, scatter_dimension=0)
+        sides = lax.psum_scatter(g_side, AXES, scatter_dimension=0)
+        d_w_in, d_w_out = jnp.concatenate([sides[:, :inner], firsts], axis=1), sides[:, inner:]
+        d_gain, small = unpack(lax.psum(small, AXES), conv_w.shape[0], inner, heads, d)
+        d_gain = lax.dynamic_slice_in_dim(d_gain, lax.axis_index(AXES) * rows, rows)
     return (output, d_tokens, d_w_in, d_w_out.T, d_gain) + small
 
 

time: 262 us -> 204 us (0.78)
  local copies, waits for them, and re-layouts: 25.7 us -> 3.76 us
  matrix products: 18.9 us -> 0 us
  Pallas kernels: 212 us -> 198 us
  other arithmetic: 4.14 us -> 1.17 us
    pallas_call x3 -> x4, Pallas kernels: 126 us -> 91.2 us  [the longest x1 42.6 us: back(): pl.pallas_call(functools.partial(back_kernel, sizes, here), grid=(n,), in...]
    pallas_call x1, Pallas kernels: 36.1 us -> 58.5 us  [front(): pl.pallas_call(functools.partial(front_kernel, sizes, here), grid=(n,), i...]
    dot_general x2 -> x0, matrix products: 18.9 us -> none  [tn(): lax.dot_general(a, b, (((0,), (0,)), ((), ())), preferred_element_type=f32)]
    convert_element_type x2 -> x0, local copies, waits for them, and re-layouts: 8.5 us -> none  [the longest x1 7.91 us: local(): d_w_in = tn(normed, dproj).astype(bf16)]
    slice x14 -> x0, local copies, waits for them, and re-layouts: 6.58 us -> none  [the longest x1 1.44 us: unpack(): small[taps]]
where the time goes in v4:
time: 204 us
  Pallas kernels  198 us (97%)
  local copies, waits for them, and re-layouts  3.76 us (2%)
    pallas_call x1, Pallas kernels, front(): pl.pallas_call(functools.partial(front_kernel, sizes, here), grid=(n,), i...  58.5 us
    pallas_call x1, Pallas kernels, middle(): pl.pallas_call(functools.partial(middle_kernel, sizes), grid=(n,), in_spe...  48.6 us
    pallas_call x1, Pallas kernels, back(): pl.pallas_call(functools.partial(back_kernel, sizes, here), grid=(n,), in...  42.6 us
    pallas_call x1, Pallas kernels, tail(): pl.pallas_call(functools.partial(tail_kernel, here), grid=(n,), in_specs=...  36.5 us
    pallas_call x1, Pallas kernels, side(): pl.pallas_call(functools.partial(side_kernel, half), grid=(2 * half,), in...  10 us

profile of v4, /device:TPU:0, one launch (start us, length us, event | category | flops | bytes accessed | tf_op | source)
XLA Modules:
  0.0 203.9 jit_solution(17898286244900144411)
XLA Ops:
  0.6 1.2 bitcast_convert_fusion.gain_in_ref
  1.8 58.5 %shard_map.221 = (bf16[1024,768]{1,0:T(8,128)(2,1)}, bf16[768,1024]{1,0:T(8,128)(2,1)}, f32[1024,1792]{1,0:T(8,128)}, f32[1024,1792]{1,0:T(8,128)}, bf16[1024,17...) custom-call(bf16[1024,768]{1,0:T(8,128)(2,1)} %tok_ref.5, ...), custom_call_target="tpu_custom_call" | custom-call | flops 5000000000 | bytes 50000000 | tf_op jit(solution)/shard_map/pallas_call | solution.py:549
  60.3 48.6 %shard_map.222 = (bf16[1024,768]{1,0:T(8,128)(2,1)}, bf16[768,1024]{1,0:T(8,128)(2,1)}, bf16[1024,1536]{1,0:T(8,128)(2,1)}, bf16[1024,1536]{1,0:T(8,128)(2,1)}, ...) custom-call(bf16[1024,768]{1,0:T(8,128)(2,1)} %tok_ref.5, ...), custom_call_target="tpu_custom_call" | custom-call | flops 30000001024 | bytes 60000000 | tf_op jit(solution)/shard_map/pallas_call | solution.py:799
  108.9 10.0 %shard_map.223 = bf16[768,3072]{1,0:T(8,128)(2,1)} custom-call(bf16[768,1024]{1,0:T(8,128)(2,1)} %get-tuple-element.61.a_ref.turned_ref, bf16[768,1024]{1,0:T(8,128)(2,1)} %get-tuple-element.75.b_ref, bf16[1024,1536]{1,0:T(8,128)(2,1)} %get-tuple-element.66.u_ref.dgate_ref, bf16[1024,1536]{1,0:T(8,128)(2,1)} %get-tuple-element.76.v_ref), custom_call_target="tpu_custom_call" | custom-call | flops 4831838208 | bytes 14000000 | tf_op jit(solution)/shard_map/pallas_call | solution.py:859
  119.0 42.6 %shard_map.224 = (bf16[1024,1840]{1,0:T(8,128)(2,1)}, f32[1024,768]{1,0:T(8,128)}, f32[8,1792]{1,0:T(8,128)}, f32[24,3072]{1,0:T(8,128)}) custom-call(bf16[768,3072]{1,0:T(8,128)(2,1)} %bitcast.30, f32[4,1792]{1,0:T(4,128)} %cw_ref.3, f32[1,48]{1,0:T(1,128)} %bitcast.21, f32[1,48]{1,0:T(1,128)} %bitcast.24, f32[1024,16]{1,0:T(8,128)} %get-tuple-element.57.aux_ref, ...), custom_call_target="tpu_custom_call" | custom-call | flops 20000000000 | bytes 60000000 | tf_op jit(solution)/shard_map/pallas_call | solution.py:1008
  161.6 36.5 %shard_map.225 = (f32[1024,768]{1,0:T(8,128)}, f32[24,1840]{1,0:T(8,128)}, f32[8,1792]{1,0:T(8,128)}) custom-call(bf16[768,1024]{1,0:T(8,128)(2,1)} %get-tuple-element.61.a_ref.turned_ref, bf16[1024,1840]{1,0:T(8,128)(2,1)} %get-tuple-element.77.dproj_ref, bf16[768,1840]{1,0:T(8,128)(2,1)} %get-tuple-element.78.w_ref, ...), custom_call_target="tpu_custom_call" | custom-call | flops 10000000000 | bytes 30000000 | tf_op jit(solution)/shard_map/pallas_call | solution.py:1119
  198.2 2.0 shard_map.226
  200.1 3.8 %copy.26 = f32[1024,768]{1,0:T(8,128)} copy(f32[1024,768]{1,0:T(8,128)} %get-tuple-element.107) | data formatting | bytes 6291456

commit v5 on v4

--- a/solution.py
+++ b/solution.py
@@ -229,9 +229,12 @@
     return flip(at, dy, dx, dc, 0)[:3] + ({0: at[3], 1: at[3] + 1 - 2 * (at[3] % 2), 2: (at[3] + 2) % 4, 3: 3 - at[3]}[k],)
 
 
+CUBE = [(0, 0, 1, 0), (0, 1, 0, 0), (1, 0, 0, 0), (0, 1, 1, 0), (1, 0, 1, 0), (1, 1, 0, 0), (1, 1, 1, 0)]
+
+
 def greet_all(me):
     barrier = pltpu.get_barrier_semaphore()
-    others = [(0, 0, 1, 0), (0, 1, 0, 0), (1, 0, 0, 0), (0, 0, 0, 1), (0, 0, 0, 2), (0, 0, 0, 3)]
+    others = CUBE + [(0, 0, 0, 1), (0, 0, 0, 2), (0, 0, 0, 3)]
     for other in others:
         pl.semaphore_signal(barrier, inc=1, device_id=device(partner(me, *other)), device_id_type=MESH)
     pl.semaphore_wait(barrier, len(others))
@@ -308,7 +311,7 @@
                 own = self.mine[b, k]
             else:
                 own = self.part[slot(partner(self.me, *BLOCKS[b], 0, k))]
-            self.mine[b, k] = (own.astype(f32) + self.from_core[b, k].astype(f32)).astype(bf16)
+            self.mine[b, k] = own + self.from_core[b, k]
             if b < 2:
                 self.copy("x", b * 4 + k).start()
             if b % 2 == 0:
@@ -316,10 +319,10 @@
 
     def far(self, k):
         self.copy("x", k).wait_recv()
-        self.mine[2, k, :, self.left] = self.add(2, k, self.left, [self.from_pair[0, k, :, self.left]]).astype(bf16)
+        self.mine[2, k, :, self.left] = self.mine[2, k, :, self.left] + self.from_pair[0, k, :, self.left]
         self.copy("fy", k).start()
         self.copy("y", k).wait_recv()
-        self.mine[1, k, :, self.right] = self.add(1, k, self.right, [self.from_pair[0, k, :, self.right]]).astype(bf16)
+        self.mine[1, k, :, self.right] = self.mine[1, k, :, self.right] + self.from_pair[0, k, :, self.right]
         self.copy("fx", k).start()
 
     def line(self, k):
@@ -379,6 +382,36 @@
         self.out[...] = (self.held[8] + self.held[3]) + (self.held[4] + self.held[5])
         for j in range(6):
             self.copy(j).wait_send()
+
+
+class Quick:
+    def __init__(self, me, own, out, held, send, recv):
+        self.me, self.own, self.out, self.held, self.send, self.recv = me, own, out, held, send, recv
+
+    def copy(self, i):
+        near = i < len(CUBE)
+        to = CUBE[i] if near else (0, 0, 0, i - len(CUBE) + 1)
+        return pltpu.make_async_remote_copy(
+            src_ref=self.own if near else self.held.at[10], dst_ref=self.held.at[i],
+            send_sem=self.send.at[i], recv_sem=self.recv.at[i],
+            device_id=device(partner(self.me, *to)), device_id_type=MESH,
+        )
+
+    def start(self):
+        for i in range(7):
+            self.copy(i).start()
+
+    def finish(self):
+        for i in range(7):
+            self.copy(i).wait_recv()
+        self.held[10] = self.own[...] + functools.reduce(jnp.add, [self.held[i] for i in range(7)])
+        for i in (7, 8, 9):
+            self.copy(i).start()
+        for i in (7, 8, 9):
+            self.copy(i).wait_recv()
+        self.out[...] = (self.held[10] + self.held[7]) + (self.held[8] + self.held[9])
+        for i in range(10):
+            self.copy(i).wait_send()
 
 
 AUX = 16
@@ -873,269 +906,253 @@
     )(a, b, u, v)
 
 
-def back_kernel(
+BLOCK = 256
+ROWS = 256
+PIECES = (3, 3)
+
+
+def rear_kernel(
     sizes, here,
-    side_ref, cw_ref, dtb_ref, alog_ref, aux_ref, x2_ref, r_ref,
-    low_ref, dsil_ref, conv_ref, dt_ref, cum_ref, dtraw_ref,
-    dgate_ref, dy_ref, dv_ref, dbc_ref, drate_ref, dq_ref, sf_ref, dog_ref, dsk_ref, part_ref,
-    dproj_ref, dnorm_ref, small_ref, sum_ref,
-    adj_ref, dpre_ref, scal_ref, *exchange,
+    low_ref, dsil_ref, conv_ref, dy_ref, dv_ref, sf_ref, cw_ref, x2_ref, r_ref, dog_ref, dsk_ref,
+    bc_ref, dt_ref, cum_ref, dtraw_ref, aux_ref, dbc_ref, drate_ref, dq_ref, dtb_ref, alog_ref,
+    turned_ref, w_ref, side_ref, gain_ref,
+    dgate_ref, tok_ref, cot_ref, given_ref,
+    *rest,
 ):
     inner, channels, heads, state = sizes
-    quad = 256
+    blocks = inner // BLOCK
     step = pl.program_id(0)
+    t, d = low_ref.shape[0], turned_ref.shape[0]
+    n = t // Q
+    taken = channels + 2 * heads
+    if here:
+        dtok_ref, total_ref, gains_ref, *sum_refs = rest[:7]
+        (
+            dproj_ref, own_ref, dgain_ref, scales_ref, ct_ref, dpre_ref, dots_ref, dbf_ref, scal_ref, through_ref, *exchange,
+        ) = rest[7:]
+        me = place()
+        sums = [Scatterer(me, given_ref, sum_refs[0], *exchange[:8])]
+        for i in range(3):
+            part_ref, *held = exchange[8 + 8 * i : 16 + 8 * i]
+            sums.append(Scatterer(me, part_ref, sum_refs[1 + i], *held))
+        sums.append(Summer(me, own_ref, total_ref, *exchange[32:35]))
+        sums.append(Quick(me, dgain_ref, gains_ref, *exchange[35:]))
+    else:
+        dtok_ref, own_ref, dgain_ref, dproj_ref = rest[:4]
+        scales_ref, ct_ref, dpre_ref, dots_ref, dbf_ref, scal_ref, through_ref = rest[4:]
+
+    chunk = lambda c: slice(c * Q, (c + 1) * Q)
 
     @pl.when(step == 0)
     def _():
-        adj_ref[...] = jnp.zeros_like(adj_ref)
-        dpre_ref[...] = jnp.zeros_like(dpre_ref)
-        small_ref[...] = jnp.zeros_like(small_ref)
-        small_ref[5:6, :inner] = dog_ref[...]
-        skips = nn(split_rows(jnp.broadcast_to(dsk_ref[...], (8, inner))), r_ref[...])
-        small_ref[6:7, SKIP_AT : SKIP_AT + Q] = skips[0:1] + skips[8:9]
+        if here:
+            greet_all(me)
+            sums[0].start()
+        own_ref[...] = jnp.zeros_like(own_ref)
+        dgain_ref[...] = jnp.zeros_like(dgain_ref)
+        dots_ref[...] = jnp.zeros_like(dots_ref)
+        dbf_ref[...] = jnp.zeros_like(dbf_ref)
+        through_ref[...] = jnp.zeros_like(through_ref)
+        dpre_ref[t:, :] = jnp.zeros((8, BLOCK), f32)
+        for c in range(n):
+            cf, dtf = cum_ref[chunk(c), :heads], dt_ref[chunk(c), :heads]
+            total_f = cf[Q - 1 :, :]
+            aux = aux_ref[chunk(c), :]
+            scales_ref[c] = split2(
+                jnp.concatenate(
+                    [
+                        jnp.exp(cf) * aux[:, 6:7],
+                        dtf * jnp.exp(total_f - cf) * aux[:, 4:5],
+                        jnp.broadcast_to(jnp.exp(total_f) * aux[Q - 1 :, 6:7], (16, heads)),
+                    ],
+                    axis=0,
+                )
+            )
+            ct_ref[c] = jnp.transpose(bc_ref[chunk(c), : 2 * state])[state:, :]
+
+    def through_conv(at):
+        sl = pl.ds(at if isinstance(at, int) else pl.multiple_of(at, BLOCK), BLOCK)
+        fold = lambda x: jnp.sum(x.reshape(Q // 8, 8, BLOCK), axis=0)
+        totals = [jnp.zeros((8, BLOCK), f32) for _ in range(5)]
+        for c in range(n):
+            conv = conv_ref[chunk(c), :]
+            z = dpre_ref[chunk(c), :]
+            totals[4] += fold(z)
+            totals[0] += fold(z * conv)
+            grad = cw_ref[0:1, :] * z
+            for k in (1, 2, 3):
+                z = dpre_ref[c * Q + k : (c + 1) * Q + k, :] * aux_ref[chunk(c), 7 + k : 8 + k]
+                totals[k] += fold(z * conv)
+                grad += cw_ref[k : k + 1, :] * z
+            dproj_ref[chunk(c), sl] = grad.astype(bf16)
+        for k in range(5):
+            own_ref[k : k + 1, sl] = jnp.sum(totals[k], axis=0, keepdims=True)
+
+    @pl.when(step < blocks)
+    def _():
+        adj = jnp.zeros((state, BLOCK), f32)
+        for c in reversed(range(n)):
+            wide = nn(scales_ref[c], x2_ref[...])
+            wide_wf, across = wide[Q : 2 * Q], wide[2 * Q : 2 * Q + 1]
+            low_f = low_ref[chunk(c), :].astype(f32)
+            adj_low = adj.astype(bf16)
+            dvf = wide_wf * nn(bc_ref[chunk(c), :state], adj_low)
+            dots_ref[chunk(c), :] += nn((low_f * dvf).astype(bf16), r_ref[...])
+            dbf_ref[chunk(c), :] += nt((low_f * wide_wf).astype(bf16), adj_low)
+            scal_ref[c : c + 1, :] = jnp.sum(adj * sf_ref[c].astype(f32), axis=0, keepdims=True) * across
+            dye = (dy_ref[chunk(c), :].astype(f32) * wide[:Q]).astype(bf16)
+            adj = adj * across + nn(ct_ref[c], dye)
+            dpre_ref[chunk(c), :] = (dv_ref[chunk(c), :] + dvf) * dsil_ref[chunk(c), :]
+        both = nn(split_rows(scal_ref[...]), r_ref[...])
+        through_ref[...] += both[:n] + both[n:]
+        through_conv(step * BLOCK)
+        at = pl.ds(pl.multiple_of(step * BLOCK, BLOCK), BLOCK)
+        own_ref[5:6, at] = dog_ref[...]
+        skips = nn(split_rows(jnp.broadcast_to(dsk_ref[...], (8, BLOCK))), r_ref[...])
+        own_ref[6:7, SKIP_AT : SKIP_AT + Q] += skips[0:1] + skips[8:9]
+
+    @pl.when(step == blocks)
+    def _():
+        a = jnp.exp(alog_ref[...])
+        row, col = iotas((Q, Q))
+        before = (col < row).astype(bf16)
+        none = jnp.zeros((Q, heads), f32)
+        sum_v, sum_a = jnp.zeros((8, 2 * heads), f32), jnp.zeros((8, 2 * heads), f32)
+        fold = lambda x: jnp.sum(x.reshape(Q // 8, 8, 2 * heads), axis=0)
+        for c in range(n):
+            d_bf = jnp.concatenate([dbf_ref[chunk(c), :], jnp.zeros((Q, 3 * state), f32)], axis=1)
+            dpre_ref[chunk(c), :] = (dbc_ref[chunk(c), :] + d_bf) * dsil_ref[chunk(c), :]
+            dots, dt = dots_ref[chunk(c), :heads], dt_ref[chunk(c), :]
+            extra = nn_exact(before, dots) + through_ref[c : c + 1, :heads]
+            d_rate = drate_ref[chunk(c), :] + jnp.concatenate([extra, none], axis=1)
+            d_dt = dq_ref[chunk(c), :] + jnp.concatenate([dots, none], axis=1)
+            d_dt = jnp.where(dt > 0.0, d_dt / jnp.maximum(dt, 1e-37), 0.0)
+            d_v = (d_dt - d_rate * a) / (1.0 + jnp.exp(-(dtraw_ref[chunk(c), :] + dtb_ref[...])))
+            sum_v += fold(d_v)
+            sum_a += fold(d_rate * (-dt * a))
+            dproj_ref[chunk(c), channels:] = d_v.astype(bf16)
+        own_ref[6:7, BIAS_AT : BIAS_AT + 2 * heads] = jnp.sum(sum_v, axis=0, keepdims=True)
+        own_ref[6:7, LOG_AT : LOG_AT + 2 * heads] = jnp.sum(sum_a, axis=0, keepdims=True)
+        through_conv(inner)
+
+    @pl.when(step > blocks)
+    def _():
+        rows = pl.ds(pl.multiple_of((step - blocks - 1) * ROWS, ROWS), ROWS)
+        d_normed = nt(dgate_ref[...], side_ref[...]) + nt(dproj_ref[rows, :], w_ref[...])
+        x = tok_ref[...].astype(f32)
+        inv = lax.rsqrt(jnp.mean(x * x, axis=1, keepdims=True) + eps)
+        unit = x * inv
+        gains = jnp.sum(d_normed * unit, axis=0, keepdims=True)
+        for i in range(d // Q):
+            dgain_ref[i : i + 1, :] += gains[:, i * Q : (i + 1) * Q]
+        a = d_normed * gain_ref[...]
+        dtok_ref[...] = cot_ref[...].astype(f32) + inv * (a - unit * jnp.mean(a * unit, axis=1, keepdims=True))
 
     if here:
-        me = place()
-        sums = Scatterer(me, part_ref, sum_ref, *exchange)
-
-        @pl.when(step == 0)
-        def _():
-            greet_all(me)
-            sums.start()
-
-    dnorm_ref[...] = nt(dgate_ref[...], side_ref[...])
-    dpre_ref[Q:, :] = dpre_ref[0:8, :]
-    aux = aux_ref[...]
-    dt = dt_ref[...]
-    cum = cum_ref[...]
-    cf, dtf = cum[:, :heads], dt[:, :heads]
-    total_f = cf[Q - 1 :, :]
-    scales = split2(
-        jnp.concatenate(
-            [
-                jnp.exp(cf) * aux[:, 6:7],
-                dtf * jnp.exp(total_f - cf) * aux[:, 4:5],
-                jnp.broadcast_to(jnp.exp(total_f) * aux[Q - 1 :, 6:7], (8, heads)),
-            ],
-            axis=0,
-        )
-    )
-    b_f = low_ref[:, inner : inner + state]
-    c_f = low_ref[:, inner + state : inner + 2 * state]
-    dots = jnp.zeros((Q, Q), f32)
-    d_bf = jnp.zeros((Q, state), f32)
-    for at in range(0, inner, quad):
-        sl = slice(at, at + quad)
-        wide = nn(scales, x2_ref[:, sl])
-        low_f = low_ref[:, sl].astype(f32)
-        adj = adj_ref[:, sl]
-        adj_low = adj.astype(bf16)
-        wide_wf = wide[Q : 2 * Q]
-        dvf = wide_wf * nn(b_f, adj_low)
-        dots += nn((low_f * dvf).astype(bf16), r_ref[sl, :])
-        d_bf += nt((low_f * wide_wf).astype(bf16), adj_low)
-        across = wide[2 * Q : 2 * Q + 1]
-        scal_ref[:, sl] = jnp.sum(adj * sf_ref[0, :, sl].astype(f32), axis=0, keepdims=True) * across
-        dye = (dy_ref[:, sl].astype(f32) * wide[:Q]).astype(bf16)
-        adj_ref[:, sl] = adj * across + tn(c_f, dye)
-        dpre_ref[:Q, sl] = (dv_ref[:, sl] + dvf) * dsil_ref[:, sl]
-    d_bc = dbc_ref[...] + jnp.concatenate([d_bf, jnp.zeros((Q, 3 * state), f32)], axis=1)
-    dpre_ref[:Q, inner:] = d_bc * dsil_ref[:, inner:]
-
-    n1, n2, n3 = aux[:, 8:9], aux[:, 9:10], aux[:, 10:11]
-    for at in range(0, channels, quad):
-        sl = slice(at, at + quad)
-        conv = conv_ref[:, sl]
-        z = dpre_ref[:Q, sl]
-        small_ref[4:5, sl] += jnp.sum(z, axis=0, keepdims=True)
-        small_ref[0:1, sl] += jnp.sum(z * conv, axis=0, keepdims=True)
-        total = cw_ref[0:1, sl] * z
-        for k, mask in ((1, n1), (2, n2), (3, n3)):
-            z = dpre_ref[k : Q + k, sl] * mask
-            small_ref[k : k + 1, sl] += jnp.sum(z * conv, axis=0, keepdims=True)
-            total += cw_ref[k : k + 1, sl] * z
-        dproj_ref[:, at : at + quad] = total.astype(bf16)
-
-    row, col = iotas((Q, Q))
-    through = nn(split_rows(jnp.broadcast_to(scal_ref[...], (8, inner))), r_ref[...])
-    through = (through[0:1] + through[8:9])[:, :heads]
-    dots = dots[:, :heads]
-    extra = nn_exact((col < row).astype(bf16), dots) + through
-    none = jnp.zeros((Q, heads), f32)
-    d_rate = drate_ref[...] + jnp.concatenate([extra, none], axis=1)
-    d_dt = dq_ref[...] + jnp.concatenate([dots, none], axis=1)
-    d_dt = jnp.where(dt > 0.0, d_dt / jnp.maximum(dt, 1e-37), 0.0)
-    a = jnp.exp(alog_ref[...])
-    v = dtraw_ref[...] + dtb_ref[...]
-    d_v = (d_dt - d_rate * a) / (1.0 + jnp.exp(-v))
-    small_ref[6:7, BIAS_AT : BIAS_AT + 2 * heads] += jnp.sum(d_v, axis=0, keepdims=True)
-    small_ref[6:7, LOG_AT : LOG_AT + 2 * heads] += jnp.sum(d_rate * (-dt * a), axis=0, keepdims=True)
-    dproj_ref[:, channels:] = d_v.astype(bf16)
-    if here:
+        edges = (0, PIECES[0] * BLOCK, inner, taken)
         for i, acts in enumerate(SUM_BEATS):
 
             @pl.when(step == i)
             def _():
-                for name, *index in acts:
-                    getattr(sums, name)(*index)
+                for name, which, *index in acts:
+                    if name == "make":
+                        part = sums[which].part
+                        lo = edges[which - 1]
+                        for cols in (sums[which].left, sums[which].right):
+                            grad = nn(turned_ref[...], dproj_ref[:, lo + cols.start : lo + cols.stop])
+                            part[:, :, cols] = grad.reshape(part.shape[:2] + grad.shape[1:]).astype(bf16)
+                        sums[which].start()
+                    else:
+                        getattr(sums[which], name)(*index)
+
+
+def acts(name, which, *indices):
+    return tuple((name, which, i) for i in indices)
 
 
 SUM_BEATS = (
-    (("pair", 3),),
-    (("pair", 2), ("far", 3)),
-    (("pair", 1), ("far", 2), ("line", 3)),
-    (("pair", 0), ("far", 1), ("line", 2)),
-    (("far", 0), ("line", 1)),
-    (),
-    (("line", 0),),
-    (("finish",),),
+    acts("pair", 0, 3),
+    acts("pair", 0, 2) + acts("far", 0, 3),
+    (("make", 1),) + acts("pair", 0, 1) + acts("far", 0, 2) + acts("line", 0, 3),
+    acts("pair", 0, 0) + acts("far", 0, 1) + acts("line", 0, 2) + acts("pair", 1, 3, 2, 1, 0),
+    acts("far", 0, 0) + acts("line", 0, 1) + acts("far", 1, 3, 2, 1),
+    (("make", 2),) + acts("line", 0, 0) + acts("far", 1, 0) + acts("line", 1, 3, 2, 1),
+    (("make", 3), ("start", 4), ("finish", 0)) + acts("line", 1, 0) + acts("pair", 2, 3, 2, 1, 0),
+    (("finish", 1), ("next", 4, 1)) + acts("pair", 3, 3, 2, 1, 0) + acts("far", 2, 3, 2),
+    (("next", 4, 2),) + acts("far", 2, 1, 0) + acts("far", 3, 3, 2) + acts("line", 2, 3, 2),
+    (("next", 4, 3),) + acts("far", 3, 1, 0) + acts("line", 2, 1, 0) + acts("line", 3, 3),
+    (("start", 5),) + acts("line", 3, 2, 1, 0) + (("finish", 2), ("finish", 4), ("finish", 5), ("finish", 3)),
 )
 
 
-def back(
-    w_side, conv_w, dt_bias, rate_row, aux, x2, r, low, dsil, conv, dt, cum, dtraw,
-    dgate, dy, dv, dbc, drate, dq, sf, dog, dsk, part, sizes, here,
+def rear(
+    low, dsil, conv, dy, dv, sf, conv_w, x2, r, dog, dsk, dt, cum, dtraw, aux, dbc, drate, dq, dt_bias, a_log,
+    turned, w_first, w_side, gain_row, dgate, tokens, cot, given, rows, sizes, here,
 ):
     inner, channels, heads, state = sizes
-    t, d = low.shape[0], w_side.shape[0]
-    n = t // Q
+    t, d = tokens.shape
+    n, blocks = t // Q, inner // BLOCK
     taken = channels + 2 * heads
-    rev = lambda i: (n - 1 - i, 0)
-    fixed = lambda i: (0, 0)
-    blk = lambda a: pl.BlockSpec((Q, a.shape[1]), rev)
-    whole = lambda a: pl.BlockSpec(a.shape, fixed)
-    summed = part.shape[1:]
-    return pl.pallas_call(
-        functools.partial(back_kernel, sizes, here),
-        grid=(n,),
-        in_specs=[
-            pl.BlockSpec((d, inner), fixed), whole(conv_w), whole(dt_bias), whole(rate_row),
-            blk(aux), whole(x2), whole(r), blk(low), blk(dsil), blk(conv), blk(dt), blk(cum), blk(dtraw),
-            blk(dgate), blk(dy), blk(dv), blk(dbc), blk(drate), blk(dq),
-            pl.BlockSpec((1, state, inner), lambda i: (n - 1 - i, 0, 0)), whole(dog), whole(dsk),
-            pl.BlockSpec(memory_space=pl.ANY),
-        ],
-        out_specs=[
-            pl.BlockSpec((Q, taken), rev), pl.BlockSpec((Q, d), rev), pl.BlockSpec((8, channels), fixed),
-            pl.BlockSpec(summed, fixed),
-        ],
-        out_shape=[
-            jax.ShapeDtypeStruct((t, taken), bf16),
-            jax.ShapeDtypeStruct((t, d), f32),
-            jax.ShapeDtypeStruct((8, channels), f32),
-            jax.ShapeDtypeStruct(summed, f32),
-        ],
-        scratch_shapes=[
-            pltpu.VMEM((state, inner), f32),
-            pltpu.VMEM((Q + 8, channels), f32),
-            pltpu.VMEM((1, inner), f32),
-        ]
-        + (scatter_scratch(*summed) + [pltpu.SemaphoreType.DMA((16,))] if here else []),
-        compiler_params=pltpu.CompilerParams(
-            dimension_semantics=("arbitrary",), vmem_limit_bytes=60 * 1024 * 1024, **reaches(here, 1)
-        ),
-        cost_estimate=pl.CostEstimate(flops=20_000_000_000, bytes_accessed=60_000_000, transcendentals=0),
-    )(
-        w_side, conv_w, dt_bias, rate_row, aux, x2, r, low, dsil, conv, dt, cum, dtraw,
-        dgate, dy, dv, dbc, drate, dq, sf, dog, dsk, part,
-    )
-
-
-def tail_kernel(
-    here,
-    turned_ref, dproj_ref, w_ref, dnorm_ref, tok_ref, cot_ref, gain_ref, small_ref,
-    dtok_ref, sum_ref, total_ref,
-    own_ref, *exchange,
-):
-    step = pl.program_id(0)
-    last = pl.num_programs(0) - 1
-    d = tok_ref.shape[1]
+    steps = blocks + 1 + t // ROWS
+    one = pl.Buffered(1)
+    wide = lambda limit: pl.BlockSpec((t, BLOCK), lambda i: (0, jnp.minimum(i, limit)))
+    short = lambda lead, limit: pl.BlockSpec((lead, BLOCK), lambda i: (0, jnp.minimum(i, limit)))
+    whole = lambda a: pl.BlockSpec(a.shape, lambda i: (0, 0), pipeline_mode=one)
+    later = lambda width: pl.BlockSpec((ROWS, width), lambda i: (jnp.maximum(i - blocks - 1, 0), 0))
+    small = (8, channels)
+    scratch = [
+        pltpu.VMEM((n, 2 * Q + 16, 2 * heads), bf16),
+        pltpu.VMEM((n, state, Q), bf16),
+        pltpu.VMEM((t + 8, BLOCK), f32),
+        pltpu.VMEM((t, Q), f32),
+        pltpu.VMEM((t, state), f32),
+        pltpu.VMEM((n, BLOCK), f32),
+        pltpu.VMEM((n, Q), f32),
+    ]
     if here:
-        me = place()
-        part_ref, *rest = exchange
-        sums = Scatterer(me, part_ref, sum_ref, *rest[:7])
-        tiny = Summer(me, own_ref, total_ref, *rest[7:])
-
-    @pl.when(step == 0)
-    def _():
-        own_ref[...] = small_ref[...]
-        if here:
-            greet_all(me)
-            for half, cols in enumerate((sums.left, sums.right)):
-                block = nn(turned_ref[...], dproj_ref[:, cols])
-                part_ref[:, :, cols] = block.reshape(part_ref.shape[:2] + block.shape[1:]).astype(bf16)
-                sums.start(half)
-
-    rows = pl.ds(pl.multiple_of(step * TAIL, TAIL), TAIL)
-    d_normed = dnorm_ref[...] + nt(dproj_ref[rows, :], w_ref[...])
-    x = tok_ref[...].astype(f32)
-    inv = lax.rsqrt(jnp.mean(x * x, axis=1, keepdims=True) + eps)
-    unit = x * inv
-    own_ref[6:7, :d] += jnp.sum(d_normed * unit, axis=0, keepdims=True)
-    a = d_normed * gain_ref[...]
-    dtok_ref[...] = cot_ref[...].astype(f32) + inv * (a - unit * jnp.mean(a * unit, axis=1, keepdims=True))
-    if here:
-        for i, acts in enumerate(TAIL_BEATS):
-
-            @pl.when(step == i)
-            def _():
-                for name, *index in acts:
-                    getattr(tiny if name in ("first", "next") else sums, "start" if name == "first" else name)(*index)
-                if i == len(TAIL_BEATS) - 1:
-                    tiny.finish()
+        widths = (PIECES[0] * BLOCK, PIECES[1] * BLOCK, taken - inner)
+        out_shape = [small, (8, Q), (rows, 2 * inner)] + [(rows, w) for w in widths]
+        own = [pltpu.VMEM((t, taken), bf16), pltpu.VMEM(small, f32), pltpu.VMEM((8, Q), f32)]
+        exchange = scatter_scratch(rows, 2 * inner) + [pltpu.SemaphoreType.DMA((16,))]
+        for w in widths:
+            exchange += [pltpu.VMEM((d // rows, rows, w), bf16)] + scatter_scratch(rows, w)
+        exchange += [pltpu.VMEM((9,) + small, f32), pltpu.SemaphoreType.DMA((6,)), pltpu.SemaphoreType.DMA((6,))]
+        exchange += [pltpu.VMEM((11, 8, Q), f32), pltpu.SemaphoreType.DMA((10,)), pltpu.SemaphoreType.DMA((10,))]
+        scratch = own + scratch + exchange
+        outs = [jax.ShapeDtypeStruct(shape, f32) for shape in out_shape]
     else:
-
-        @pl.when(step == last)
-        def _():
-            total_ref[...] = own_ref[...]
-
-
-TAIL = 256
-TAIL_BEATS = (
-    (("pair", 3),),
-    (("pair", 2), ("far", 3)),
-    (("pair", 1), ("far", 2), ("line", 3)),
-    (
-        ("first",), ("pair", 0), ("far", 1), ("line", 2), ("next", 1), ("far", 0), ("line", 1), ("next", 2), ("line", 0),
-        ("next", 3), ("finish",),
-    ),
-)
-
-
-def tail(turned, dproj, w_first, dnorm, tokens, cot, gain_row, small, rows, here):
-    d, t = turned.shape
-    n = t // TAIL
-    taken = dproj.shape[1]
-    fwd = lambda i: (i, 0)
-    fixed = lambda i: (0, 0)
-    blk = pl.BlockSpec((TAIL, d), fwd)
-    whole = lambda a: pl.BlockSpec(a.shape, fixed)
-    exchange = []
-    if here:
-        exchange = [pltpu.VMEM((d // rows, rows, taken), bf16)] + scatter_scratch(rows, taken)
-        exchange += [
-            pltpu.VMEM((9,) + small.shape, f32), pltpu.SemaphoreType.DMA((6,)), pltpu.SemaphoreType.DMA((6,)),
+        outs = [
+            jax.ShapeDtypeStruct(small, f32), jax.ShapeDtypeStruct((8, Q), f32), jax.ShapeDtypeStruct((t, taken), bf16),
         ]
     return pl.pallas_call(
-        functools.partial(tail_kernel, here),
-        grid=(n,),
-        in_specs=[whole(turned), whole(dproj), whole(w_first), blk, blk, blk, whole(gain_row), whole(small)],
-        out_specs=[blk, pl.BlockSpec((rows, taken), fixed), whole(small)],
-        out_shape=[
-            jax.ShapeDtypeStruct((t, d), f32),
-            jax.ShapeDtypeStruct((rows, taken), f32),
-            jax.ShapeDtypeStruct(small.shape, f32),
+        functools.partial(rear_kernel, sizes, here),
+        grid=(steps,),
+        in_specs=[
+            wide(blocks), wide(blocks), wide(blocks), wide(blocks - 1), wide(blocks - 1),
+            pl.BlockSpec((n, state, BLOCK), lambda i: (0, 0, jnp.minimum(i, blocks - 1))),
+            short(conv_w.shape[0], blocks), short(2 * heads, blocks - 1),
+            pl.BlockSpec((BLOCK, Q), lambda i: (jnp.minimum(i, blocks - 1), 0)),
+            short(1, blocks - 1), short(1, blocks - 1),
+            pl.BlockSpec((t, BLOCK), lambda i: (0, blocks), pipeline_mode=one),
+            whole(dt), whole(cum), whole(dtraw), whole(aux), whole(dbc), whole(drate), whole(dq), whole(dt_bias), whole(a_log),
+            whole(turned), whole(w_first), pl.BlockSpec((d, inner), lambda i: (0, 0), pipeline_mode=one), whole(gain_row),
+            later(inner), later(d), later(d), pl.BlockSpec(memory_space=pl.ANY),
         ],
-        scratch_shapes=[pltpu.VMEM(small.shape, f32)] + exchange,
+        out_specs=[later(d)] + [pl.BlockSpec(o.shape, lambda i: (0, 0)) for o in outs],
+        out_shape=[jax.ShapeDtypeStruct((t, d), f32)] + outs,
+        scratch_shapes=scratch,
         compiler_params=pltpu.CompilerParams(
-            dimension_semantics=("arbitrary",), vmem_limit_bytes=60 * 1024 * 1024, **reaches(here, 2)
+            dimension_semantics=("arbitrary",), vmem_limit_bytes=62 * 1024 * 1024, **reaches(here, 1)
         ),
-        cost_estimate=pl.CostEstimate(flops=10_000_000_000, bytes_accessed=30_000_000, transcendentals=0),
-    )(turned, dproj, w_first, dnorm, tokens, cot, gain_row, small)
-
-
-def unpack(small, taps, inner, heads, d):
-    return small[6, :d], (
+        cost_estimate=pl.CostEstimate(flops=30_000_000_000, bytes_accessed=60_000_000, transcendentals=0),
+    )(
+        low, dsil, conv, dy, dv, sf, conv_w, x2, r, dog, dsk, low, dt, cum, dtraw, aux, dbc, drate, dq, dt_bias, a_log,
+        turned, w_first, w_side, gain_row, dgate, tokens, cot, given,
+    )
+
+
+def unpack(small, taps, inner, heads):
+    return (
         small[:taps],
         small[taps],
         small[6, BIAS_AT : BIAS_AT + 2 * heads],
@@ -1146,12 +1163,15 @@
 
 
 def finish_kernel(
-    sizes, side_ref, first_ref, small_ref,
+    sizes, side_ref, one_ref, two_ref, last_ref, small_ref, gains_ref,
     din_ref, dout_ref, dgain_ref, dcw_ref, dcb_ref, ddtb_ref, dalog_ref, dsk_ref, dog_ref,
 ):
     inner, channels, heads, rows = sizes
     din_ref[:, :inner] = side_ref[:, :inner]
-    din_ref[:, inner:] = first_ref[...]
+    at = inner
+    for ref in (one_ref, two_ref, last_ref):
+        din_ref[:, at : at + ref.shape[1]] = ref[...]
+        at += ref.shape[1]
     dout_ref[...] = side_ref[:, inner:]
     taps = dcw_ref.shape[0]
     dcw_ref[...] = small_ref[:taps, :]
@@ -1160,27 +1180,28 @@
     ddtb_ref[...] = small_ref[6:7, BIAS_AT : BIAS_AT + 2 * heads]
     dalog_ref[...] = small_ref[6:7, LOG_AT : LOG_AT + 2 * heads]
     dsk_ref[...] = small_ref[6:7, SKIP_AT : SKIP_AT + heads]
-    d = BIAS_AT
-    row, col = iotas((d, Q))
-    own = (row == col + slot(place()) * rows) & (col < rows)
-    parts = jnp.broadcast_to(small_ref[6:7, :d], (8, d))
-    hi = parts.astype(bf16)
-    mid = (parts - hi.astype(f32)).astype(bf16)
-    lo = (parts - hi.astype(f32) - mid.astype(f32)).astype(bf16)
-    pick = jnp.where(own, 1.0, 0.0).astype(bf16)
-    dgain_ref[...] = (nn(hi, pick) + nn(mid, pick) + nn(lo, pick))[0:1, :rows]
-
-
-def finish(sides, firsts, small, taps, sizes):
+    row, col = iotas((Q, Q))
+    picked = jnp.zeros((8, Q), f32)
+    for i in range(BIAS_AT // Q):
+        pick = ((row + i * Q == col + slot(place()) * rows) & (col < rows)).astype(f32).astype(bf16)
+        part = jnp.broadcast_to(gains_ref[i : i + 1, :], (8, Q))
+        hi = part.astype(bf16)
+        mid = (part - hi.astype(f32)).astype(bf16)
+        lo = (part - hi.astype(f32) - mid.astype(f32)).astype(bf16)
+        picked += nn(hi, pick) + nn(mid, pick) + nn(lo, pick)
+    dgain_ref[...] = picked[0:1, :rows]
+
+
+def finish(sums, small, gains, taps, sizes):
     inner, channels, heads, rows = sizes
     shapes = [
-        (rows, inner + firsts.shape[1]), (rows, inner), (1, rows), (taps, channels), (channels,), (1, 2 * heads),
+        (rows, inner + channels + 2 * heads), (rows, inner), (1, rows), (taps, channels), (channels,), (1, 2 * heads),
         (1, 2 * heads), (1, heads), (inner,),
     ]
     return pl.pallas_call(
         functools.partial(finish_kernel, sizes),
         out_shape=[jax.ShapeDtypeStruct(shape, f32) for shape in shapes],
-    )(sides, firsts, small)
+    )(*sums, small, gains)
 
 
 def body(here, tokens, segment_ids, w_in, w_out, norm_gain, conv_w, conv_b, dt_bias, a_log, d_skip, out_gain, cotangent):
@@ -1213,21 +1234,22 @@
     else:
         g_side = jnp.concatenate([nn(turned, dgate), nn(cot_turned, nout)], axis=1)
     g_side = g_side.reshape(parts, rows, 2 * inner)
-    dproj, dnorm, small, sides = back(
-        w_side, conv_w, dtb_row, alog_row, aux, x2, r, low, dsil, conv, dt, cum, dtraw,
-        dgate, dy, dv, dbc, drate, dq, sf, d_og, d_sk, g_side, sizes, here,
+    d_tokens, small, gains, *sums = rear(
+        low, dsil, conv, dy, dv, sf, conv_w, x2, r, d_og, d_sk, dt, cum, dtraw, aux, dbc, drate, dq, dtb_row, alog_row,
+        turned, w_first, w_side, gain_row, dgate, tokens, cotangent, g_side, rows, sizes, here,
     )
-    d_tokens, firsts, small = tail(turned, dproj, w_first, dnorm, tokens, cotangent, gain_row, small, rows, here)
     if here:
-        d_w_in, d_w_out, d_gain, *small = finish(sides, firsts, small, conv_w.shape[0], (inner, channels, heads, rows))
+        d_w_in, d_w_out, d_gain, *small = finish(sums, small, gains, conv_w.shape[0], (inner, channels, heads, rows))
         d_gain = d_gain[0]
         small = tuple(a[0] if a.ndim == 2 and a.shape[0] == 1 else a for a in small)
     else:
+        dproj = sums[0]
         g_first = nn(turned, dproj).reshape(parts, rows, dproj.shape[1])
         firsts = lax.psum_scatter(g_first, AXES, scatter_dimension=0)
         sides = lax.psum_scatter(g_side, AXES, scatter_dimension=0)
         d_w_in, d_w_out = jnp.concatenate([sides[:, :inner], firsts], axis=1), sides[:, inner:]
-        d_gain, small = unpack(lax.psum(small, AXES), conv_w.shape[0], inner, heads, d)
+        small, gains = lax.psum((small, gains), AXES)
+        small, d_gain = unpack(small, conv_w.shape[0], inner, heads), gains.reshape(-1)[:d]
         d_gain = lax.dynamic_slice_in_dim(d_gain, lax.axis_index(AXES) * rows, rows)
     return (output, d_tokens, d_w_in, d_w_out.T, d_gain) + small
 

time: 204 us -> 202 us (level)
    pallas_call x2 -> x1, Pallas kernels: 79.2 us -> 76.6 us  [rear(): pl.pallas_call(functools.partial(rear_kernel, sizes, here), grid=(steps,)...]
where the time goes in v5:
time: 202 us; the launch traced here: 201 us
  Pallas kernels  196 us (97%)
  local copies, waits for them, and re-layouts  3.76 us (2%)
    pallas_call x1, Pallas kernels, rear(): pl.pallas_call(functools.partial(rear_kernel, sizes, here), grid=(steps,)...  76.6 us
    pallas_call x1, Pallas kernels, front(): pl.pallas_call(functools.partial(front_kernel, sizes, here), grid=(n,), i...  58.4 us
    pallas_call x1, Pallas kernels, middle(): pl.pallas_call(functools.partial(middle_kernel, sizes), grid=(n,), in_spe...  48.6 us
    pallas_call x1, Pallas kernels, side(): pl.pallas_call(functools.partial(side_kernel, half), grid=(2 * half,), in...  10.1 us

profile of v5, /device:TPU:0, one launch (start us, length us, event | category | flops | bytes accessed | tf_op | source)
XLA Modules:
  0.0 201.3 jit_solution(11188641050127650541)
XLA Ops:
  0.6 1.2 bitcast_convert_fusion.gain_in_ref
  1.8 58.4 %shard_map.221 = (bf16[1024,768]{1,0:T(8,128)(2,1)}, bf16[768,1024]{1,0:T(8,128)(2,1)}, f32[1024,1792]{1,0:T(8,128)}, f32[1024,1792]{1,0:T(8,128)}, bf16[1024,17...) custom-call(bf16[1024,768]{1,0:T(8,128)(2,1)} %tok_ref.5, ...), custom_call_target="tpu_custom_call" | custom-call | flops 5000000000 | bytes 50000000 | tf_op jit(solution)/shard_map/pallas_call | solution.py:582
  60.2 48.6 %shard_map.222 = (bf16[1024,768]{1,0:T(8,128)(2,1)}, bf16[768,1024]{1,0:T(8,128)(2,1)}, bf16[1024,1536]{1,0:T(8,128)(2,1)}, bf16[1024,1536]{1,0:T(8,128)(2,1)}, ...) custom-call(bf16[1024,768]{1,0:T(8,128)(2,1)} %tok_ref.5, ...), custom_call_target="tpu_custom_call" | custom-call | flops 30000001024 | bytes 60000000 | tf_op jit(solution)/shard_map/pallas_call | solution.py:832
  108.8 10.1 %shard_map.223 = bf16[768,3072]{1,0:T(8,128)(2,1)} custom-call(bf16[768,1024]{1,0:T(8,128)(2,1)} %get-tuple-element.73.a_ref.turned_ref, bf16[768,1024]{1,0:T(8,128)(2,1)} %get-tuple-element.77.b_ref, bf16[1024,1536]{1,0:T(8,128)(2,1)} %get-tuple-element.76.u_ref.dgate_ref, bf16[1024,1536]{1,0:T(8,128)(2,1)} %get-tuple-element.78.v_ref), custom_call_target="tpu_custom_call" | custom-call | flops 4831838208 | bytes 14000000 | tf_op jit(solution)/shard_map/pallas_call | solution.py:892
  118.9 76.6 %shard_map.224 = (f32[1024,768]{1,0:T(8,128)}, f32[8,1792]{1,0:T(8,128)}, f32[8,128]{1,0:T(8,128)}, f32[24,3072]{1,0:T(8,128)}, f32[24,768]{1,0:T(8,128)}, /*index=5*/f32[24,768]{1,0:T(8,128)}, f32[24,304]{1,0:T(8,128)}) custom-call(bf16[1024,1792]{1,0:T(8,128)(2,1)} %get-tuple-element.61.low_ref.bc_ref, f32[1024,1792]{1,0:T(8,128)} %get-tuple-element.62.dsil_ref, ...), custom_call_target="tpu_custom_call" | custom-call | flops 30000001024 | bytes 60000000 | tf_op jit(solution)/shard_map/pallas_call | solution.py:1127
  195.5 2.0 shard_map.225
  197.5 3.8 %copy.26 = f32[1024,768]{1,0:T(8,128)} copy(f32[1024,768]{1,0:T(8,128)} %get-tuple-element.107) | data formatting | bytes 6291456

commit v6 on v5

--- a/solution.py
+++ b/solution.py
@@ -10,6 +10,7 @@
 
 eps = 1e-05
 Q = 128
+SUB = 2
 HALO = 16
 f32 = jnp.float32
 bf16 = jnp.bfloat16
@@ -547,12 +548,12 @@
     weight = dt[:, heads:] * jnp.exp(cum[:, heads:] - rate[:, heads:]) * aux[:, 5:6]
     whole = jnp.exp(cum[Q - 1 :, heads:]) * aux[0:1, 7:8]
     scales = split2(jnp.concatenate([weight, jnp.broadcast_to(whole, (8, heads))], axis=0))
-    b_bwd = low_ref[:, inner + 2 * state : inner + 3 * state]
+    b_bwd = jnp.transpose(act_ref[:, inner + 2 * state :])[:state].astype(bf16)
     for at in range(0, inner, block):
         sl = slice(at, at + block)
         wide = nn(scales, x2_ref[:, sl])
         vs = (low_ref[:, sl].astype(f32) * wide[:Q]).astype(bf16)
-        state_ref[:, sl] = state_ref[:, sl] * wide[Q : Q + 1] + tn(b_bwd, vs)
+        state_ref[:, sl] = state_ref[:, sl] * wide[Q : Q + 1] + nn(b_bwd, vs)
     if here:
         steps = len(BEATS) - 1
         for i in range(steps):
@@ -621,26 +622,16 @@
     )(tokens, tokens, seg, conv_w, conv_b, dt_bias, a_log, x2, first, own, gain)
 
 
-def middle_kernel(
-    sizes,
-    tok_ref, act_ref, normed_ref, dt_ref, cum_ref, aux_ref, seg_ref, cot_ref, sb_ref, w_ref,
-    alog_ref, skip_in_ref, og_ref, x2_ref, r_ref,
-    out_ref, turned_ref, nout_ref, dgate_ref, dy_ref, dv_ref, dbc_ref, drate_ref, dq_ref, sf_ref, dog_ref, dsk_ref,
+def middle_chunk(
+    sizes, step,
+    act_ref, dt_ref, cum_ref, aux_ref, seg_ref, cot_ref, sb_ref,
+    alog_ref, og_ref, x2_ref, r_ref,
+    turned_ref, nout_ref, dgate_ref, dy_ref, dv_ref, dbc_ref, drate_ref, dq_ref, sf_ref, dog_ref, dsk_ref,
     decay_ref, mix_ref, state_ref, adj_ref, ssm_ref, gated_ref, dno_ref, yf_ref, yb_ref, wide_ref,
     p_ref, q_ref, scal_ref, gate_ref, skip_ref,
 ):
     inner, channels, heads, state = sizes
     quad = 256
-    step = pl.program_id(0)
-
-    @pl.when(step == 0)
-    def _():
-        state_ref[...] = jnp.zeros_like(state_ref)
-        adj_ref[...] = jnp.zeros_like(adj_ref)
-        dog_ref[...] = jnp.zeros_like(dog_ref)
-        dsk_ref[...] = jnp.zeros_like(dsk_ref)
-        q_ref[...] = jnp.zeros_like(q_ref)
-        skip_ref[...] = nn(split2(jnp.broadcast_to(skip_in_ref[...], (8, heads))), x2_ref[...])[0:1]
 
     sf_ref[0] = state_ref[...].astype(bf16)
     aux = aux_ref[...]
@@ -648,9 +639,11 @@
     lower = col < row
     same = aux[:, 3:4] == seg_ref[pl.ds(step, 1), :].astype(f32)
     b_f = act_ref[:, inner : inner + state].astype(bf16)
+    b_f_turned = jnp.transpose(act_ref[:, inner : inner + 2 * state])[:state].astype(bf16)
     c_f = act_ref[:, inner + state : inner + 2 * state].astype(bf16)
     b_b = act_ref[:, inner + 2 * state : inner + 3 * state].astype(bf16)
     c_b = act_ref[:, inner + 3 * state :].astype(bf16)
+    c_b_turned = jnp.transpose(act_ref[:, inner + 2 * state :])[state:].astype(bf16)
     g = jnp.where(same & (col != row), jnp.where(lower, nt(c_f, b_f), nt(c_b, b_b)), 0.0)
     dt = dt_ref[...]
     cum = cum_ref[...]
@@ -686,8 +679,7 @@
 
     squares = jnp.zeros((Q, quad), f32)
     dots = jnp.zeros((Q, quad), f32)
-    cot = cot_ref[...]
-    turned_ref[...] = jnp.transpose(cot)
+    turned_ref[...] = jnp.transpose(cot_ref[...])
     for at in range(0, inner, quad):
         sl = slice(at, at + quad)
         wide_ref[:, sl] = nn(scales, x2_ref[:, sl])
@@ -716,12 +708,10 @@
             )
         ssm = jnp.concatenate(parts, axis=1) + yf + yb + skip_ref[:, sl] * v
         ssm_ref[:, sl] = ssm
-        gate = nn(normed_ref[...], w_ref[:, sl])
-        gate_ref[:, sl] = gate
+        gate = gate_ref[:, sl]
         gated = ssm * (gate / (1.0 + jnp.exp(-gate)))
         gated_ref[:, sl] = gated
-        dno = nn(cot, w_ref[:, inner + at : inner + at + quad])
-        dno_ref[:, sl] = dno
+        dno = dno_ref[:, sl]
         squares += gated * gated
         dots += dno * og_ref[sl][None, :] * gated
 
@@ -792,10 +782,9 @@
         d_bb += nt(vs_b, adj_low)
         across_b = wide_ref[4 * Q + 8 : 4 * Q + 9, sl]
         scal_ref[:, sl] = jnp.sum(adj * sb_low.astype(f32), axis=0, keepdims=True) * across_b
-        adj_ref[:, sl] = adj * across_b + tn(c_b, dye_b)
-        state_ref[:, sl] = state_ref[:, sl] * wide_ref[4 * Q : 4 * Q + 1, sl] + tn(b_f, vs_f)
-
-    out_ref[...] = (tok_ref[...].astype(f32) + nt(nout_ref[...], w_ref[:, inner:])).astype(bf16)
+        adj_ref[:, sl] = adj * across_b + nn(c_b_turned, dye_b)
+        state_ref[:, sl] = state_ref[:, sl] * wide_ref[4 * Q : 4 * Q + 1, sl] + nn(b_f_turned, vs_f)
+
     dg = jnp.where(same & (col != row), dg, 0.0)
     dg_f = jnp.where(lower, dg, 0.0)
     dg_b = (dg - dg_f).astype(bf16)
@@ -818,14 +807,53 @@
     dq_ref[...] = jnp.concatenate([q_cols[:, :heads], q_cols[:, heads:] + dots_v], axis=1)
 
 
+def middle_kernel(
+    sizes,
+    tok_ref, act_ref, normed_ref, dt_ref, cum_ref, aux_ref, seg_ref, cot_ref, sb_ref, w_ref,
+    alog_ref, skip_in_ref, og_ref, x2_ref, r_ref,
+    out_ref, turned_ref, nout_ref, dgate_ref, dy_ref, dv_ref, dbc_ref, drate_ref, dq_ref, sf_ref, dog_ref, dsk_ref,
+    *scratch,
+):
+    inner, _, heads, _ = sizes
+    state_ref, adj_ref, dno_ref, q_ref, gate_ref, skip_ref = (scratch[i] for i in (2, 3, 6, 11, 13, 14))
+    step = pl.program_id(0)
+
+    @pl.when(step == 0)
+    def _():
+        state_ref[...] = jnp.zeros_like(state_ref)
+        adj_ref[...] = jnp.zeros_like(adj_ref)
+        dog_ref[...] = jnp.zeros_like(dog_ref)
+        dsk_ref[...] = jnp.zeros_like(dsk_ref)
+        q_ref[...] = jnp.zeros_like(q_ref)
+        skip_ref[...] = nn(split2(jnp.broadcast_to(skip_in_ref[...], (8, heads))), x2_ref[...])[0:1]
+
+    for at in range(0, inner, 256):
+        sl = slice(at, at + 256)
+        gate_ref[:, sl] = nn(normed_ref[...], w_ref[:, sl])
+        dno_ref[:, sl] = nn(cot_ref[...], w_ref[:, inner + at : inner + at + 256])
+    for sub in range(SUB):
+        rows = slice(sub * Q, (sub + 1) * Q)
+        cut = lambda *refs: [r.at[rows] for r in refs]
+        held = [r.at[rows] if i in (6, 13) else r for i, r in enumerate(scratch)]
+        middle_chunk(
+            sizes, step * SUB + sub,
+            *cut(act_ref, dt_ref, cum_ref, aux_ref), seg_ref, cot_ref.at[rows], sb_ref.at[sub : sub + 1],
+            alog_ref, og_ref, x2_ref, r_ref,
+            turned_ref.at[:, rows],
+            *cut(nout_ref, dgate_ref, dy_ref, dv_ref, dbc_ref, drate_ref, dq_ref), sf_ref.at[sub : sub + 1], dog_ref, dsk_ref,
+            *held,
+        )
+    out_ref[...] = (tok_ref[...].astype(f32) + nt(nout_ref[...], w_ref[:, inner:])).astype(bf16)
+
+
 def middle(tokens, act, normed, dt, cum, aux, seg, cot, sb, w_side, a_log, skip, og, x2, r, sizes):
     inner, channels, heads, state = sizes
     t, d = tokens.shape
-    n = t // Q
+    n = t // Q // SUB
     fwd = lambda i: (i, 0)
     fixed = lambda i: (0, 0)
     cube = lambda i: (i, 0, 0)
-    blk = lambda width: pl.BlockSpec((Q, width), fwd)
+    blk = lambda width: pl.BlockSpec((SUB * Q, width), fwd)
     whole = lambda a: pl.BlockSpec(a.shape, fixed)
     out = lambda width, dtype: jax.ShapeDtypeStruct((t, width), dtype)
     line = jax.ShapeDtypeStruct((1, inner), f32)
@@ -834,19 +862,19 @@
         grid=(n,),
         in_specs=[
             blk(d), blk(channels), blk(d), blk(2 * heads), blk(2 * heads), blk(aux.shape[1]),
-            whole(seg), blk(d), pl.BlockSpec((1, state, inner), cube),
+            whole(seg), blk(d), pl.BlockSpec((SUB, state, inner), cube),
             whole(w_side), whole(a_log), whole(skip), pl.BlockSpec(og.shape, lambda i: (0,)), whole(x2), whole(r),
         ],
         out_specs=[
-            blk(d), pl.BlockSpec((d, Q), lambda i: (0, i)), blk(inner), blk(inner), blk(inner), blk(inner), blk(4 * state),
-            blk(2 * heads), blk(2 * heads), pl.BlockSpec((1, state, inner), cube),
+            blk(d), pl.BlockSpec((d, SUB * Q), lambda i: (0, i)), blk(inner), blk(inner), blk(inner), blk(inner), blk(4 * state),
+            blk(2 * heads), blk(2 * heads), pl.BlockSpec((SUB, state, inner), cube),
             pl.BlockSpec((1, inner), fixed), pl.BlockSpec((1, inner), fixed),
         ],
         out_shape=[
             out(d, bf16), jax.ShapeDtypeStruct((d, t), bf16),
             out(inner, bf16), out(inner, bf16), out(inner, bf16), out(inner, f32),
             out(4 * state, f32), out(2 * heads, f32), out(2 * heads, f32),
-            jax.ShapeDtypeStruct((n, state, inner), bf16), line, line,
+            jax.ShapeDtypeStruct((n * SUB, state, inner), bf16), line, line,
         ],
         scratch_shapes=[
             pltpu.VMEM((heads, Q, Q), f32),
@@ -855,14 +883,14 @@
             pltpu.VMEM((state, inner), f32),
             pltpu.VMEM((Q, inner), f32),
             pltpu.VMEM((Q, inner), f32),
-            pltpu.VMEM((Q, inner), f32),
+            pltpu.VMEM((SUB * Q, inner), f32),
             pltpu.VMEM((Q, inner), f32),
             pltpu.VMEM((Q, inner), f32),
             pltpu.VMEM((4 * Q + 16, inner), f32),
             pltpu.VMEM((Q, Q), f32),
             pltpu.VMEM((Q, Q), f32),
             pltpu.VMEM((1, inner), f32),
-            pltpu.VMEM((Q, inner), f32),
+            pltpu.VMEM((SUB * Q, inner), f32),
             pltpu.VMEM((1, inner), f32),
         ],
         compiler_params=pltpu.CompilerParams(

time: 202 us -> 200 us (0.990)
  no operation moved by 1% of the time
where the time goes in v6:
time: 200 us
  Pallas kernels  195 us (98%)
  local copies, waits for them, and re-layouts  3.76 us (2%)
    pallas_call x1, Pallas kernels, rear(): pl.pallas_call(functools.partial(rear_kernel, sizes, here), grid=(steps,)...  76.6 us
    pallas_call x1, Pallas kernels, front(): pl.pallas_call(functools.partial(front_kernel, sizes, here), grid=(n,), i...  58.2 us
    pallas_call x1, Pallas kernels, middle(): pl.pallas_call(functools.partial(middle_kernel, sizes), grid=(n,), in_spe...  47.7 us
    pallas_call x1, Pallas kernels, side(): pl.pallas_call(functools.partial(side_kernel, half), grid=(2 * half,), in...  10.1 us

profile of v6, /device:TPU:0, one launch (start us, length us, event | category | flops | bytes accessed | tf_op | source)
XLA Modules:
  0.0 200.2 jit_solution(4058381657279304212)
XLA Ops:
  0.6 1.2 bitcast_convert_fusion.gain_in_ref
  1.8 58.2 %shard_map.221 = (bf16[1024,768]{1,0:T(8,128)(2,1)}, bf16[768,1024]{1,0:T(8,128)(2,1)}, f32[1024,1792]{1,0:T(8,128)}, f32[1024,1792]{1,0:T(8,128)}, bf16[1024,17...) custom-call(bf16[1024,768]{1,0:T(8,128)(2,1)} %tok_ref.5, ...), custom_call_target="tpu_custom_call" | custom-call | flops 5000000000 | bytes 50000000 | tf_op jit(solution)/shard_map/pallas_call | solution.py:583
  60.0 47.7 %shard_map.222 = (bf16[1024,768]{1,0:T(8,128)(2,1)}, bf16[768,1024]{1,0:T(8,128)(2,1)}, bf16[1024,1536]{1,0:T(8,128)(2,1)}, bf16[1024,1536]{1,0:T(8,128)(2,1)}, ...) custom-call(bf16[1024,768]{1,0:T(8,128)(2,1)} %tok_ref.5, ...), custom_call_target="tpu_custom_call" | custom-call | flops 30000001024 | bytes 60000000 | tf_op jit(solution)/shard_map/pallas_call | solution.py:860
  107.7 10.1 %shard_map.223 = bf16[768,3072]{1,0:T(8,128)(2,1)} custom-call(bf16[768,1024]{1,0:T(8,128)(2,1)} %get-tuple-element.73.a_ref.turned_ref, bf16[768,1024]{1,0:T(8,128)(2,1)} %get-tuple-element.77.b_ref, bf16[1024,1536]{1,0:T(8,128)(2,1)} %get-tuple-element.76.u_ref.dgate_ref, bf16[1024,1536]{1,0:T(8,128)(2,1)} %get-tuple-element.78.v_ref), custom_call_target="tpu_custom_call" | custom-call | flops 4831838208 | bytes 14000000 | tf_op jit(solution)/shard_map/pallas_call | solution.py:920
  117.8 76.6 %shard_map.224 = (f32[1024,768]{1,0:T(8,128)}, f32[8,1792]{1,0:T(8,128)}, f32[8,128]{1,0:T(8,128)}, f32[24,3072]{1,0:T(8,128)}, f32[24,768]{1,0:T(8,128)}, /*index=5*/f32[24,768]{1,0:T(8,128)}, f32[24,304]{1,0:T(8,128)}) custom-call(bf16[1024,1792]{1,0:T(8,128)(2,1)} %get-tuple-element.61.low_ref.bc_ref, f32[1024,1792]{1,0:T(8,128)} %get-tuple-element.62.dsil_ref, ...), custom_call_target="tpu_custom_call" | custom-call | flops 30000001024 | bytes 60000000 | tf_op jit(solution)/shard_map/pallas_call | solution.py:1155
  194.4 2.0 %shard_map.225 = (f32[24,3376]{1,0:T(8,128)}, f32[24,1536]{1,0:T(8,128)}, f32[1,24]{1,0:T(1,128)}, f32[4,1792]{1,0:T(4,128)}, f32[1792]{0:T(1024)}, /*index=5*/f...) custom-call(f32[24,3072]{1,0:T(8,128)} %get-tuple-element.80.side_ref, ...), custom_call_target="tpu_custom_call" | custom-call | tf_op jit(solution)/shard_map/pallas_call | solution.py:1229
  196.4 3.8 %copy.26 = f32[1024,768]{1,0:T(8,128)} copy(f32[1024,768]{1,0:T(8,128)} %get-tuple-element.107) | data formatting | bytes 6291456
